TPU v7x, 32 devices: a whole 2x2x4 slice. The times are simulated.
32 devices in a mesh: energy: 16 (over z, y, x), space: 2 (over core).
Axes of the slice: x: 2, y: 2, z: 4, core: 2. Of those that a mesh axis runs over, the one named last changes fastest.
Arguments:
- green_ret: bfloat16 [16, 16, 128, 128], P('energy', 'space'), may hold values from -0.5 to 0.5
- prior_less: bfloat16 [16, 16, 128, 128], P('energy', 'space'), may hold values from -1.25 to 9.25
- prior_great: bfloat16 [16, 16, 128, 128], P('energy', 'space'), may hold values from -1.25 to 9.25
- coupling: bfloat16 [16, 128, 128], P('space'), may hold values from -0.5 to 0.5
- phonon_coupling: float32 [128, 128], P('energy'), may hold values from 0.1 to 1
- phonon_shift: int32 [2], replicated, may hold values from 1 to 8
- active_blocks: int32 [16], replicated, may hold values from 8 to 16
Outputs:
- sigma_less: bfloat16 [16, 16, 128, 128], P(None, 'space', 'energy')
- sigma_great: bfloat16 [16, 16, 128, 128], P(None, 'space', 'energy')
- current: float32 [16, 16], P('energy', 'space')
- ldos: float32 [16, 16], P('energy', 'space')
All inputs are finite; a program needn't handle non-finite values.
Results may differ from a plain program's by a relative error of at most 0.009.
Values may be sent and summed in bfloat16 or wider, within the bound.
No kernel may reach another device: no remote copies, remote signals or barrier semaphores. Data moves between devices by JAX's collectives and lax.ppermute only.
A program may use at most 64 MiB of HBM per device.

v0:
```python
import jax
import jax.numpy as jnp
from jax import lax
from jax.sharding import PartitionSpec as P

phonon_occupation = 0.5


def shifted(value, axis, steps):
    count = lax.axis_size(axis)
    initial, last = (max(0, -steps), min(count, count - steps))
    return lax.ppermute(value, axis, [(source, source + steps) for source in range(initial, last)])


def sandwich(retarded, middle_part):
    half_product = jnp.einsum(
        "enij,kenjl->kenil", retarded, middle_part, preferred_element_type=jnp.float32
    ).astype(jnp.bfloat16)
    return jnp.einsum(
        "kenil,enml->kenim", half_product, retarded, preferred_element_type=jnp.float32
    )


def displaced(blocks_in, offset):
    energies = blocks_in.shape[0]
    target = jnp.arange(energies, dtype=jnp.int32) + offset
    inside_grid = (target >= 0) & (target < energies)
    rolled = jnp.roll(blocks_in, -offset, axis=0).astype(jnp.float32)
    return jnp.where(inside_grid[:, None, None, None], rolled, jnp.float32(0.0))


def local(
    green_ret, prior_less, prior_great, coupling, phonon_coupling, phonon_shift, active_blocks
):
    energy_count, block_count, orbitals, _ = green_ret.shape
    energy_start = lax.axis_index("energy") * energy_count
    block_start = lax.axis_index("space") * block_count
    priors = jnp.stack([prior_less, prior_great])
    bare = sandwich(green_ret, priors).astype(jnp.bfloat16)
    next_first = shifted(bare[:, :, 0], "space", -1)
    following = jnp.concatenate([bare[:, :, 1:], next_first[:, :, None]], 2)
    lowered = jnp.einsum(
        "nij,kenjl->kenil", coupling, following, preferred_element_type=jnp.float32
    ).astype(jnp.bfloat16)
    downward = jnp.einsum("kenil,nml->kenim", lowered, coupling, preferred_element_type=jnp.float32)
    raised = jnp.einsum(
        "nji,kenjl->kenil", coupling, bare, preferred_element_type=jnp.float32
    ).astype(jnp.bfloat16)
    upward = jnp.einsum(
        "kenil,nlm->kenim", raised, coupling, preferred_element_type=jnp.float32
    ).astype(jnp.bfloat16)
    prev_upward = shifted(upward[:, :, -1], "space", 1)
    previous = jnp.concatenate([prev_upward[:, :, None], upward[:, :, :-1]], 2)
    source = (priors.astype(jnp.float32) + previous.astype(jnp.float32) + downward).astype(
        jnp.bfloat16
    )
    result = sandwich(green_ret, source)
    open_counts = lax.dynamic_slice_in_dim(active_blocks, energy_start, energy_count)
    block_ids = block_start + jnp.arange(block_count, dtype=jnp.int32)
    open_mask = (block_ids[None, :] < open_counts[:, None]).astype(jnp.float32)
    greens = (result * open_mask[None, :, :, None, None]).astype(jnp.bfloat16)
    lesser = greens[0]
    greater = greens[1]
    row_count = orbitals // lax.axis_size("energy")
    first_row = lax.axis_index("energy") * row_count
    columns = jnp.arange(orbitals, dtype=jnp.int32)
    row_ids = first_row + jnp.arange(row_count, dtype=jnp.int32)
    diagonal_mask = (columns[None, :] == row_ids[:, None]).astype(jnp.float32)
    occupied = jnp.float32(phonon_occupation)
    lesser_rows = lax.all_to_all(lesser, "energy", split_axis=2, concat_axis=0, tiled=True)
    greater_rows = lax.all_to_all(greater, "energy", split_axis=2, concat_axis=0, tiled=True)
    less_sum = jnp.zeros(lesser_rows.shape, jnp.float32)
    great_sum = jnp.zeros(greater_rows.shape, jnp.float32)
    for branch in range(2):
        offset = phonon_shift[branch]
        less_sum = (
            less_sum
            + (1.0 + occupied) * displaced(lesser_rows, offset)
            + occupied * displaced(lesser_rows, -offset)
        )
        great_sum = (
            great_sum
            + (1.0 + occupied) * displaced(greater_rows, -offset)
            + occupied * displaced(greater_rows, offset)
        )
    sigma_l = (phonon_coupling * less_sum).astype(jnp.bfloat16)
    sigma_g = (phonon_coupling * great_sum).astype(jnp.bfloat16)
    lesser_wide = lesser_rows.astype(jnp.float32)
    greater_wide = greater_rows.astype(jnp.float32)
    scattering = (
        jnp.sum(
            sigma_l.astype(jnp.float32) * greater_wide - sigma_g.astype(jnp.float32) * lesser_wide,
            axis=(2, 3),
        )
        / orbitals
    )
    density = jnp.sum((lesser_wide + greater_wide) * diagonal_mask, axis=(2, 3)) / orbitals
    current, ldos = (
        lax.psum_scatter(scattering, "energy", scatter_dimension=0, tiled=True),
        lax.psum_scatter(density, "energy", scatter_dimension=0, tiled=True),
    )
    return (sigma_l, sigma_g, current, ldos)


def solution(mesh):
    return jax.shard_map(
        local,
        mesh=mesh,
        in_specs=(
            P("energy", "space", None, None),
            P("energy", "space", None, None),
            P("energy", "space", None, None),
            P("space", None, None),
            P("energy", None),
            P(),
            P(),
        ),
        out_specs=(
            P(None, "space", "energy", None),
            P(None, "space", "energy", None),
            P("energy", "space"),
            P("energy", "space"),
        ),
        check_vma=False,
    )
```

profile of v0, /device:TPU:0, one launch (start us, length us, event | category | flops | bytes accessed | tf_op | source)
XLA Modules:
  0.0 125.8 jit_solution(9001748382687217051)
XLA Ops:
  0.6 0.0 copy-start
  0.7 1.2 copy.23
  1.9 0.2 copy.24
  2.0 0.8 copy-done.5
  2.8 0.5 convolution_convert_fusion.4
  3.3 1.3 %collective-permute-start.1 = (bf16[2,1,128,128]{3,2,0,1:T(8,128)(2,1)S(1)}, bf16[2,1,128,128]{3,2,0,1:T(8,128)(2,1)S(1)}, u32[]{:S(2)}, u32[]{:S(2)}) collective-permute-start(bf16[2,1,128,128]{3,2,0,1:T(8,128)(2,1)S(1)} %slice_bitcast_fusion.2), channel_id=1, source_target_pairs={{1,0},{3,2},{5,4},{7,6},{9,8},{11,10},{13,12},{15,14},{17,16},{19,... | collective-permute-start | bytes 196616 | tf_op jit(solution)/shard_map/ppermute | solution.py:12
  4.6 0.5 fusion.5
  5.2 3.0 %collective-permute-start = (bf16[2,1,128,128]{2,3,0,1:T(8,128)(2,1)S(1)}, bf16[2,1,128,128]{2,3,0,1:T(8,128)(2,1)S(1)}, u32[]{:S(2)}, u32[]{:S(2)}) collective-permute-start(bf16[2,1,128,128]{2,3,0,1:T(8,128)(2,1)S(1)} %slice_bitcast_fusion.3), channel_id=1, source_target_pairs={{0,1},{2,3},{4,5},{6,7},{8,9},{10,11},{12,13},{14,15},{16,17},{18,... | collective-permute-start | bytes 196616 | tf_op jit(solution)/shard_map/ppermute | solution.py:12
  8.3 0.6 copy-done.6
  8.9 0.6 dynamic_slice.6
  9.5 0.6 compare_convert_fusion
  10.2 0.5 convolution_bitcast_fusion
  10.7 0.5 slice-done
  11.2 1.6 %fusion.2 = bf16[2,1,8,128,128]{4,3,0,2,1:T(8,128)(2,1)S(1)} fusion(f32[2,1,8,128,128]{3,4,0,2,1:T(8,128)S(1)} %convolution_bitcast_fusion, bf16[2,1,7,128,128]{3,4,0,2,1:T(8,128)(2,1)S(1)} %slice-done, bf16[2,1,1,128,128]{3,4,0,2,1:T(8,128)(2,1)S(1)} %bitcast.146, f32[8]{0:T(128)S(1)} %compare_convert_fusion, ...), kind=kOutput, calls=%fused_computation.10 | convolution fusion | flops 136839168 | bytes 2883616 | tf_op jit(solution)/shard_map/kenil,enml->kenim/dot_general | solution.py:19
  12.8 0.9 copy.35
  13.7 8.3 %all-to-all-start.1 = ((bf16[1,8,128,128]{3,1,0,2:T(8,128)(2,1)}), bf16[1,8,128,128]{3,1,0,2:T(8,128)(2,1)S(1)}, u32[]{:S(2)}, u32[]{:S(2)}) async-start(bf16[1,8,128,128]{3,1,0,2:T(8,128)(2,1)} %copy.35), calls=%async_computation.1 | async-start | bytes 524288 | tf_op jit(solution)/shard_map/all_to_all | solution.py:71
  22.1 0.6 copy-done.4
  22.7 0.6 fusion.52
  23.3 0.9 copy.33
  24.2 7.3 %all-to-all-done.1 = bf16[1,8,128,128]{3,1,0,2:T(8,128)(2,1)S(1)} async-done(((bf16[1,8,128,128]{3,1,0,2:T(8,128)(2,1)}), bf16[1,8,128,128]{3,1,0,2:T(8,128)(2,1)S(1)}, u32[]{:S(2)}, u32[]{:S(2)}) %all-to-all-start.1) | async-done | bytes 262176 | tf_op jit(solution)/shard_map/all_to_all | solution.py:71
  31.5 3.5 %all-to-all-start = ((bf16[1,8,128,128]{3,1,0,2:T(8,128)(2,1)}), bf16[1,8,128,128]{3,1,0,2:T(8,128)(2,1)S(1)}, u32[]{:S(2)}, u32[]{:S(2)}) async-start(bf16[1,8,128,128]{3,1,0,2:T(8,128)(2,1)} %copy.33), calls=%async_computation | async-start | bytes 524288 | tf_op jit(solution)/shard_map/all_to_all | solution.py:70
  40.3 0.6 copy-done.7
  40.9 0.6 dynamic-slice
  41.5 0.7 compare_and_fusion
  42.2 0.7 compare_and_fusion.2
  42.8 0.1 fusion.45
  43.0 1.3 %all-to-all-done = bf16[1,8,128,128]{3,1,0,2:T(8,128)(2,1)S(1)} async-done(((bf16[1,8,128,128]{3,1,0,2:T(8,128)(2,1)}), bf16[1,8,128,128]{3,1,0,2:T(8,128)(2,1)S(1)}, u32[]{:S(2)}, u32[]{:S(2)}) %all-to-all-start) | async-done | bytes 262176 | tf_op jit(solution)/shard_map/all_to_all | solution.py:70
  44.3 0.7 copy-done.3
  45.0 2.8 %fusion.11 = (f32[16,8]{1,0:T(8,128)S(1)}, f32[16,8]{1,0:T(8,128)S(1)}, bf16[16,8,8,128]{3,2,1,0:T(8,128)(2,1)}, bf16[16,8,8,128]{3,2,1,0:T(8,128)(2,1)}) fusion(f32[8,128]{1,0:T(8,128)S(1)} %fusion.45, bf16[1,8,16,8,128]{4,1,3,2,0:T(8,128)(2,1)S(1)} %bitcast.136, bf16[1,8,16,8,128]{4,1,3,2,0:T(8,128)(2,1)S(1)} %bitcast.134, s32[]{:T(128)S(6)} %select_n.66, ...), kind=kLoop, calls=%fused_computation.39 | loop fusion | flops 6946560 | bytes 1582160 | tf_op jit(solution)/shard_map/reduce_sum | solution.py:97
  47.8 75.9 %all-reduce.2 = (f32[16,8]{1,0:T(8,128)S(1)}, f32[16,8]{1,0:T(8,128)S(1)}) all-reduce(f32[16,8]{1,0:T(8,128)S(1)} %broadcast_multiply_fusion.1, f32[16,8]{1,0:T(8,128)S(1)} %broadcast_multiply_fusion), channel_id=2, replica_groups=mesh['energy'=16,'space'=2] {'energy'}, use_global_device_ids=true, to_apply=%region_1.3.clone | all-reduce | flops 256 | bytes 2048
  123.6 1.1 constant_dynamic-slice_fusion
  124.7 1.1 constant_dynamic-slice_fusion.1
  (22 shorter events, 0.2 us)
Async XLA Ops:
  0.6 4.0 %copy-start = (bf16[8,128,128]{2,1,0:T(8,128)(2,1)S(1)}, bf16[8,128,128]{2,1,0:T(8,128)(2,1)}, u32[]{:S(2)}) copy-start(bf16[8,128,128]{2,1,0:T(8,128)(2,1)} %param.12) | copy-start | bytes 786436
  0.6 1.2 copy-start.2
  1.8 1.0 copy-start.5
  3.3 6.9 %collective-permute-start.1 = (bf16[2,1,128,128]{3,2,0,1:T(8,128)(2,1)S(1)}, bf16[2,1,128,128]{3,2,0,1:T(8,128)(2,1)S(1)}, u32[]{:S(2)}, u32[]{:S(2)}) collective-permute-start(bf16[2,1,128,128]{3,2,0,1:T(8,128)(2,1)S(1)} %slice_bitcast_fusion.2), channel_id=1, source_target_pairs={{1,0},{3,2},{5,4},{7,6},{9,8},{11,10},{13,12},{15,14},{17,16},{19,... | collective-permute-start | bytes 196616 | tf_op jit(solution)/shard_map/ppermute | solution.py:12
  5.2 3.1 %copy-start.1 = (bf16[2,1,8,128,128]{3,4,0,2,1:T(8,128)(2,1)}, bf16[2,1,8,128,128]{3,4,0,2,1:T(8,128)(2,1)S(1)}, u32[]{:S(2)}) copy-start(bf16[2,1,8,128,128]{3,4,0,2,1:T(8,128)(2,1)S(1)} %fusion.5) | copy-start | bytes 1572868
  5.2 5.5 %collective-permute-start = (bf16[2,1,128,128]{2,3,0,1:T(8,128)(2,1)S(1)}, bf16[2,1,128,128]{2,3,0,1:T(8,128)(2,1)S(1)}, u32[]{:S(2)}, u32[]{:S(2)}) collective-permute-start(bf16[2,1,128,128]{2,3,0,1:T(8,128)(2,1)S(1)} %slice_bitcast_fusion.3), channel_id=1, source_target_pairs={{0,1},{2,3},{4,5},{6,7},{8,9},{10,11},{12,13},{14,15},{16,17},{18,... | collective-permute-start | bytes 196616 | tf_op jit(solution)/shard_map/ppermute | solution.py:12
  8.3 0.7 copy-start.6
  10.2 1.0 slice-start
  13.7 17.8 %all-to-all-start.1 = ((bf16[1,8,128,128]{3,1,0,2:T(8,128)(2,1)}), bf16[1,8,128,128]{3,1,0,2:T(8,128)(2,1)S(1)}, u32[]{:S(2)}, u32[]{:S(2)}) async-start(bf16[1,8,128,128]{3,1,0,2:T(8,128)(2,1)} %copy.35), calls=%async_computation.1 | async-start | bytes 524288 | tf_op jit(solution)/shard_map/all_to_all | solution.py:71
  22.1 0.7 copy-start.4
  31.5 12.8 %all-to-all-start = ((bf16[1,8,128,128]{3,1,0,2:T(8,128)(2,1)}), bf16[1,8,128,128]{3,1,0,2:T(8,128)(2,1)S(1)}, u32[]{:S(2)}, u32[]{:S(2)}) async-start(bf16[1,8,128,128]{3,1,0,2:T(8,128)(2,1)} %copy.33), calls=%async_computation | async-start | bytes 524288 | tf_op jit(solution)/shard_map/all_to_all | solution.py:70
  40.3 0.7 copy-start.7
  44.3 0.7 copy-start.3
where the time goes:
time: 126 us
  blocking collectives  75.9 us (60%)
  starting transfers between devices  16.2 us (13%)
  local copies, waits for them, and re-layouts  11.1 us (9%)
  waiting for transfers between devices  8.57 us (7%)
  between operations  6.15 us (5%)
  other arithmetic  4.82 us (4%)
  matrix products  3.12 us (2%)
    unnamed x1, blocking collectives  75.9 us
    all_to_all x1, starting transfers between devices, local(): lax.all_to_all(greater, 'energy', split_axis=2, concat_axis=0, tiled=True)  8.33 us
    unnamed x21, local copies, waits for them, and re-layouts  7.5 us
    all_to_all x1, waiting for transfers between devices, local(): lax.all_to_all(greater, 'energy', split_axis=2, concat_axis=0, tiled=True)  7.3 us
    ppermute x2, starting transfers between devices, shifted(): lax.ppermute(value, axis, [(source, source + steps) for source in range(i...  4.32 us
    all_to_all x1, starting transfers between devices, local(): lax.all_to_all(lesser, 'energy', split_axis=2, concat_axis=0, tiled=True)  3.55 us
    reduce_sum x1, other arithmetic, local(): jnp.sum((lesser_wide + greater_wide) * diagonal_mask, axis=(2, 3))  2.79 us
  transfers between devices with their start and end apart: 4, of which 2 were waited for; matrix products, arithmetic and copies ran while one was open for 5% of the time, Pallas kernels for 0%

commit v1 on v0

--- a/solution.py
+++ b/solution.py
@@ -59,16 +59,17 @@
     block_ids = block_start + jnp.arange(block_count, dtype=jnp.int32)
     open_mask = (block_ids[None, :] < open_counts[:, None]).astype(jnp.float32)
     greens = (result * open_mask[None, :, :, None, None]).astype(jnp.bfloat16)
-    lesser = greens[0]
-    greater = greens[1]
-    row_count = orbitals // lax.axis_size("energy")
-    first_row = lax.axis_index("energy") * row_count
-    columns = jnp.arange(orbitals, dtype=jnp.int32)
-    row_ids = first_row + jnp.arange(row_count, dtype=jnp.int32)
-    diagonal_mask = (columns[None, :] == row_ids[:, None]).astype(jnp.float32)
+    devices = lax.axis_size("energy")
+    row_count = orbitals // devices
     occupied = jnp.float32(phonon_occupation)
-    lesser_rows = lax.all_to_all(lesser, "energy", split_axis=2, concat_axis=0, tiled=True)
-    greater_rows = lax.all_to_all(greater, "energy", split_axis=2, concat_axis=0, tiled=True)
+    identity = jnp.eye(orbitals, dtype=jnp.float32)
+    density = jnp.sum(greens.astype(jnp.float32) * identity, axis=(0, 3, 4)) / orbitals
+    outgoing = greens.reshape(2, energy_count, block_count, devices, row_count, orbitals)
+    outgoing = jnp.transpose(outgoing, (3, 1, 0, 2, 4, 5))
+    rows = lax.all_to_all(outgoing, "energy", split_axis=0, concat_axis=0, tiled=True)
+    rows = rows.reshape(devices * energy_count, 2, block_count, row_count, orbitals)
+    lesser_rows = rows[:, 0]
+    greater_rows = rows[:, 1]
     less_sum = jnp.zeros(lesser_rows.shape, jnp.float32)
     great_sum = jnp.zeros(greater_rows.shape, jnp.float32)
     for branch in range(2):
@@ -85,21 +86,15 @@
         )
     sigma_l = (phonon_coupling * less_sum).astype(jnp.bfloat16)
     sigma_g = (phonon_coupling * great_sum).astype(jnp.bfloat16)
-    lesser_wide = lesser_rows.astype(jnp.float32)
-    greater_wide = greater_rows.astype(jnp.float32)
-    scattering = (
-        jnp.sum(
-            sigma_l.astype(jnp.float32) * greater_wide - sigma_g.astype(jnp.float32) * lesser_wide,
-            axis=(2, 3),
-        )
-        / orbitals
+    scattering = jnp.sum(
+        sigma_l.astype(jnp.float32) * greater_rows.astype(jnp.float32)
+        - sigma_g.astype(jnp.float32) * lesser_rows.astype(jnp.float32),
+        axis=(2, 3),
     )
-    density = jnp.sum((lesser_wide + greater_wide) * diagonal_mask, axis=(2, 3)) / orbitals
-    current, ldos = (
-        lax.psum_scatter(scattering, "energy", scatter_dimension=0, tiled=True),
-        lax.psum_scatter(density, "energy", scatter_dimension=0, tiled=True),
-    )
-    return (sigma_l, sigma_g, current, ldos)
+    parts = scattering.reshape(devices, energy_count, block_count)
+    parts = lax.all_to_all(parts, "energy", split_axis=0, concat_axis=0, tiled=True)
+    current = jnp.sum(parts, axis=0) / orbitals
+    return (sigma_l, sigma_g, current, density)
 
 
 def solution(mesh):

time: 126 us -> 52.5 us (0.42)
  blocking collectives: 75.9 us -> 0 us
  local copies, waits for them, and re-layouts: 11.1 us -> 5.54 us
  waiting for transfers between devices: 8.57 us -> 13.7 us
  other arithmetic: 4.82 us -> 6.18 us
    unnamed x1 -> x0, blocking collectives: 75.9 us -> none
    all_to_all x2, waiting for transfers between devices: 8.57 us -> 13.7 us  [the longest x1 6.98 us: local(): lax.all_to_all(outgoing, 'energy', split_axis=0, concat_axis=0, tiled=True)]
    unnamed x21 -> x18, local copies, waits for them, and re-layouts: 7.5 us -> 2.86 us
    squeeze x3 -> x1, local copies, waits for them, and re-layouts: 1.79 us -> 0.03 us  [local(): lesser_rows = rows[:, 0]]
    reduce_sum x1 -> x2, other arithmetic: 2.79 us -> 3.19 us  [the longest x1 3.15 us: local(): jnp.sum(sigma_l.astype(jnp.float32) * greater_rows.astype(jnp.float32) -...]
  transfers between devices with their start and end apart: 4 -> 4, of which waited for: 2 -> 2; matrix products, arithmetic and copies ran while one was open for 5% -> 9% of each run, Pallas kernels for 0% -> 0%
where the time goes in v1:
time: 52.5 us; the launch traced here: 52 us
  starting transfers between devices  17.2 us (33%)
  waiting for transfers between devices  13.7 us (26%)
  other arithmetic  6.18 us (12%)
  between operations  6.1 us (12%)
  local copies, waits for them, and re-layouts  5.54 us (11%)
  matrix products  3.19 us (6%)
    all_to_all x1, starting transfers between devices, local(): lax.all_to_all(outgoing, 'energy', split_axis=0, concat_axis=0, tiled=True)  8.45 us
    all_to_all x1, waiting for transfers between devices, local(): lax.all_to_all(outgoing, 'energy', split_axis=0, concat_axis=0, tiled=True)  6.98 us
    all_to_all x1, waiting for transfers between devices, local(): lax.all_to_all(parts, 'energy', split_axis=0, concat_axis=0, tiled=True)  6.76 us
    ppermute x2, starting transfers between devices, shifted(): lax.ppermute(value, axis, [(source, source + steps) for source in range(i...  4.92 us
    all_to_all x1, starting transfers between devices, local(): lax.all_to_all(parts, 'energy', split_axis=0, concat_axis=0, tiled=True)  3.85 us
    reduce_sum x1, other arithmetic, local(): jnp.sum(sigma_l.astype(jnp.float32) * greater_rows.astype(jnp.float32) -...  3.15 us
    unnamed x18, local copies, waits for them, and re-layouts  2.86 us
    dot_general x2, matrix products, sandwich(): jnp.einsum('kenil,enml->kenim', half_product, retarded, preferred_element...  2.16 us
  transfers between devices with their start and end apart: 4, of which 2 were waited for; matrix products, arithmetic and copies ran while one was open for 9% of the time, Pallas kernels for 0%

profile of v1, /device:TPU:0, one launch (start us, length us, event | category | flops | bytes accessed | tf_op | source)
XLA Modules:
  0.0 52.0 jit_solution(9054485042536568207)
XLA Ops:
  0.6 0.0 copy-start
  0.7 1.2 %copy.23 = bf16[1,8,128,128]{2,3,1,0:T(8,128)(2,1)S(1)} copy(bf16[1,8,128,128]{3,2,1,0:T(8,128)(2,1)} %param.11) | data formatting | bytes 524288 | tf_op args[2]
  1.8 0.2 copy.22
  2.0 0.0 copy-start.4
  2.1 0.0 copy-start.1
  2.1 0.5 %convolution_convert_fusion.4 = bf16[8,2,128,128]{3,2,1,0:T(8,128)(2,1)S(1)} fusion(bf16[1,1,8,128,128]{3,4,0,2,1:T(8,128)(2,1)S(1)} %bitcast.142, bf16[1,1,8,128,128]{3,4,0,2,1:T(8,128)(2,1)S(1)} %bitcast.144, bf16[1,8,128,128]{3,2,1,0:T(8,128)(2,1)S(1)} %copy-done), kind=kOutput, calls=%fused_computation.7 | convolution fusion | flops 135004160 | bytes 1310720 | tf_op jit(solution)/shard_map/kenil,enml->kenim/dot_general | solution.py:19
  2.6 0.1 copy-done.4
  2.7 1.3 %collective-permute-start.1 = (bf16[2,1,128,128]{3,2,0,1:T(8,128)(2,1)S(1)}, bf16[2,1,128,128]{3,2,0,1:T(8,128)(2,1)S(1)}, u32[]{:S(2)}, u32[]{:S(2)}) collective-permute-start(bf16[2,1,128,128]{3,2,0,1:T(8,128)(2,1)S(1)} %slice_bitcast_fusion.2), channel_id=1, source_target_pairs={{1,0},{3,2},{5,4},{7,6},{9,8},{11,10},{13,12},{15,14},{17,16},{19,... | collective-permute-start | bytes 196616 | tf_op jit(solution)/shard_map/ppermute | solution.py:12
  4.0 0.5 %fusion.4 = bf16[2,1,8,128,128]{3,4,0,2,1:T(8,128)(2,1)S(1)} fusion(bf16[8,2,128,128]{3,2,1,0:T(8,128)(2,1)S(1)} %convolution_convert_fusion.4, bf16[8,128,128]{2,1,0:T(8,128)(2,1)S(1)} %copy-done.1), kind=kOutput, calls=%fused_computation.12 | convolution fusion | flops 134742016 | bytes 1310720 | tf_op jit(solution)/shard_map/kenil,nlm->kenim/dot_general | solution.py:49
  4.6 3.6 %collective-permute-start = (bf16[2,1,128,128]{2,3,0,1:T(8,128)(2,1)S(1)}, bf16[2,1,128,128]{2,3,0,1:T(8,128)(2,1)}, u32[]{:S(2)}, u32[]{:S(2)}) collective-permute-start(bf16[2,1,128,128]{2,3,0,1:T(8,128)(2,1)S(1)} %slice_bitcast_fusion.3), channel_id=1, source_target_pairs={{0,1},{2,3},{4,5},{6,7},{8,9},{10,11},{12,13},{14,15},{16,17},{18,... | collective-permute-start | bytes 196616 | tf_op jit(solution)/shard_map/ppermute | solution.py:12
  8.3 0.0 copy-start.7
  8.3 0.6 %copy-done.7 = s32[16]{0:T(128)S(1)} copy-done((s32[16]{0:T(128)S(1)}, s32[16]{0:T(128)}, u32[]{:S(2)}) %copy-start.7) | copy-done | bytes 88
  9.0 0.6 %dynamic_slice.6 = s32[1]{0:T(128)} dynamic-slice(s32[16]{0:T(128)S(1)} %copy-done.7, s32[]{:T(128)S(6)} %select_n.38), dynamic_slice_sizes={1} | dynamic-slice | bytes 12 | tf_op jit(solution)/shard_map/dynamic_slice | solution.py:58
  9.6 0.6 %compare_convert_fusion = f32[8]{0:T(128)S(1)} fusion(s32[]{:T(128)} %bitcast.44, s32[]{:T(128)S(6)} %mul.65), kind=kLoop, calls=%fused_computation.68 | loop fusion | flops 24 | bytes 40 | tf_op jit(solution)/shard_map/convert_element_type | solution.py:60
  10.2 0.0 collective-permute-done.1
  10.2 0.0 slice-start
  10.2 0.5 convolution_bitcast_fusion
  10.8 0.5 slice-done
  11.2 1.6 %multiply_reduce_fusion = (f32[8]{0:T(128)S(1)}, bf16[1,8,128,2,128]{2,4,3,1,0:T(8,128)(2,1)S(1)}) fusion(f32[128,128]{1,0:T(8,128)S(1)} %fusion.40, f32[8]{0:T(128)S(1)} %compare_convert_fusion, bf16[1,8,128,128]{3,2,1,0:T(8,128)(2,1)S(1)} %copy-done, f32[2,1,8,128,128]{3,4,0,2,1:T(8,128)S(1)} %convolution_bitcast_fusion, ...), kind=kOutput, calls=%fused_computation.15 | convolution fusion | flops 137625600 | bytes 2949184 | tf_op jit(solution)/shard_map/kenil,enml->kenim/dot_general | solution.py:19
  12.9 0.9 %copy_bitcast_fusion = bf16[16,1,2,8,8,128]{5,4,3,2,1,0:T(8,128)(2,1)} fusion(bf16[1,8,128,2,128]{2,4,3,1,0:T(8,128)(2,1)S(1)} %get-tuple-element.13), kind=kLoop, calls=%fused_computation.43 | loop fusion | bytes 1048576 | tf_op jit(solution)/shard_map/transpose | solution.py:68
  13.8 8.4 %all-to-all-start = ((bf16[16,1,2,8,8,128]{5,4,3,2,1,0:T(8,128)(2,1)}), bf16[16,1,2,8,8,128]{5,4,3,2,1,0:T(8,128)(2,1)S(1)}, u32[]{:S(2)}, u32[]{:S(2)}) async-start(bf16[16,1,2,8,8,128]{5,4,3,2,1,0:T(8,128)(2,1)} %copy_bitcast_fusion), calls=%async_computation | async-start | bytes 1048576 | tf_op jit(solution)/shard_map/all_to_all | solution.py:69
  22.3 0.6 %fusion.47 = (s32[1]{0:T(128)}, s32[1]{0:T(128)}) fusion(s32[2]{0:T(128)S(1)} %copy-done.6), kind=kLoop, calls=%fused_computation.75 | loop fusion | bytes 16 | tf_op jit(solution)/shard_map/slice | solution.py:76
  28.1 0.7 %compare_and_fusion = (pred[16]{0:T(512)(128)(4,1)S(1)}, pred[16]{0:T(512)(128)(4,1)S(1)}) fusion(s32[]{:T(128)S(6)} %neg.5, s32[]{:T(128)} %bitcast.50), kind=kLoop, calls=%fused_computation.65 | loop fusion | flops 128 | bytes 40 | tf_op jit(solution)/shard_map/and | solution.py:27
  28.8 0.7 %compare_and_fusion.2 = (pred[16]{0:T(512)(128)(4,1)S(1)}, pred[16]{0:T(512)(128)(4,1)S(1)}) fusion(s32[]{:T(128)S(6)} %neg.4, s32[]{:T(128)} %bitcast), kind=kLoop, calls=%fused_computation.67 | loop fusion | flops 128 | bytes 40 | tf_op jit(solution)/shard_map/and | solution.py:27
  29.4 7.0 %all-to-all-done = bf16[16,1,2,8,8,128]{5,4,3,2,1,0:T(8,128)(2,1)S(1)} async-done(((bf16[16,1,2,8,8,128]{5,4,3,2,1,0:T(8,128)(2,1)}), bf16[16,1,2,8,8,128]{5,4,3,2,1,0:T(8,128)(2,1)S(1)}, u32[]{:S(2)}, u32[]{:S(2)}) %all-to-all-start) | async-done | bytes 524320 | tf_op jit(solution)/shard_map/all_to_all | solution.py:69
  36.4 0.0 copy-start.5
  36.5 0.7 %copy-done.5 = f32[8,128]{1,0:T(8,128)S(1)} copy-done((f32[8,128]{1,0:T(8,128)S(1)}, f32[8,128]{1,0:T(8,128)}, u32[]{:S(2)}) %copy-start.5) | copy-done | bytes 4120
  37.1 3.2 %subtract_reduce_fusion = (f32[16,8]{1,0:T(8,128)}, bf16[16,8,8,128]{3,2,1,0:T(8,128)(2,1)}, bf16[16,8,8,128]{3,2,1,0:T(8,128)(2,1)}) fusion(bf16[16,2,8,8,128]{4,3,2,1,0:T(8,128)(2,1)S(1)} %bitcast.139, s32[]{:T(128)S(6)} %select_n.66, pred[16]{0:T(512)(128)(4,1)S(1)} %get-tuple-element.15, s32[]{:T(128)S(6)} %select_n.68, ...), kind=kLoop, calls=%fused_computation.44 | loop fusion | flops 6553472 | bytes 1577552 | tf_op jit(solution)/shard_map/reduce_sum | solution.py:89
  40.3 3.8 %all-to-all-start.1 = ((f32[16,1,8]{2,1,0:T(1,128)}), f32[16,1,8]{2,1,0:T(1,128)S(1)}, u32[]{:S(2)}, u32[]{:S(2)}) async-start(f32[16,1,8]{2,1,0:T(1,128)} %bitcast.69), calls=%async_computation.1 | async-start | bytes 16384 | tf_op jit(solution)/shard_map/all_to_all | solution.py:95
  44.1 0.5 multiply_bitcast_fusion
  44.7 6.8 %all-to-all-done.1 = f32[16,1,8]{2,1,0:T(1,128)S(1)} async-done(((f32[16,1,8]{2,1,0:T(1,128)}), f32[16,1,8]{2,1,0:T(1,128)S(1)}, u32[]{:S(2)}, u32[]{:S(2)}) %all-to-all-start.1) | async-done | bytes 544 | tf_op jit(solution)/shard_map/all_to_all | solution.py:95
  51.5 0.5 multiply_bitcast_fusion.1
  (15 shorter events, 0.1 us)
Async XLA Ops:
  0.6 1.4 %copy-start = (bf16[1,8,128,128]{3,2,1,0:T(8,128)(2,1)S(1)}, bf16[1,8,128,128]{3,2,1,0:T(8,128)(2,1)}, u32[]{:S(2)}) copy-start(bf16[1,8,128,128]{3,2,1,0:T(8,128)(2,1)} %param.9) | copy-start | bytes 786436
  0.6 1.2 %copy-start.3 = (bf16[1,8,128,128]{3,2,1,0:T(8,128)(2,1)S(1)}, bf16[1,8,128,128]{3,2,1,0:T(8,128)(2,1)}, u32[]{:S(2)}) copy-start(bf16[1,8,128,128]{3,2,1,0:T(8,128)(2,1)} %param.10) | copy-start | bytes 786436
  2.0 0.7 %copy-start.4 = (bf16[1,8,128,128]{2,3,1,0:T(8,128)(2,1)}, bf16[1,8,128,128]{2,3,1,0:T(8,128)(2,1)S(1)}, u32[]{:S(2)}) copy-start(bf16[1,8,128,128]{2,3,1,0:T(8,128)(2,1)S(1)} %copy.22) | copy-start | bytes 786436
  2.1 2.0 %copy-start.1 = (bf16[8,128,128]{2,1,0:T(8,128)(2,1)S(1)}, bf16[8,128,128]{2,1,0:T(8,128)(2,1)}, u32[]{:S(2)}) copy-start(bf16[8,128,128]{2,1,0:T(8,128)(2,1)} %param.12) | copy-start | bytes 786436
  2.7 7.5 %collective-permute-start.1 = (bf16[2,1,128,128]{3,2,0,1:T(8,128)(2,1)S(1)}, bf16[2,1,128,128]{3,2,0,1:T(8,128)(2,1)S(1)}, u32[]{:S(2)}, u32[]{:S(2)}) collective-permute-start(bf16[2,1,128,128]{3,2,0,1:T(8,128)(2,1)S(1)} %slice_bitcast_fusion.2), channel_id=1, source_target_pairs={{1,0},{3,2},{5,4},{7,6},{9,8},{11,10},{13,12},{15,14},{17,16},{19,... | collective-permute-start | bytes 196616 | tf_op jit(solution)/shard_map/ppermute | solution.py:12
  4.6 3.7 %copy-start.2 = (bf16[2,1,8,128,128]{3,4,0,2,1:T(8,128)(2,1)}, bf16[2,1,8,128,128]{3,4,0,2,1:T(8,128)(2,1)S(1)}, u32[]{:S(2)}) copy-start(bf16[2,1,8,128,128]{3,4,0,2,1:T(8,128)(2,1)S(1)} %fusion.4) | copy-start | bytes 1572868
  4.6 6.1 %collective-permute-start = (bf16[2,1,128,128]{2,3,0,1:T(8,128)(2,1)S(1)}, bf16[2,1,128,128]{2,3,0,1:T(8,128)(2,1)}, u32[]{:S(2)}, u32[]{:S(2)}) collective-permute-start(bf16[2,1,128,128]{2,3,0,1:T(8,128)(2,1)S(1)} %slice_bitcast_fusion.3), channel_id=1, source_target_pairs={{0,1},{2,3},{4,5},{6,7},{8,9},{10,11},{12,13},{14,15},{16,17},{18,... | collective-permute-start | bytes 196616 | tf_op jit(solution)/shard_map/ppermute | solution.py:12
  8.3 0.7 %copy-start.7 = (s32[16]{0:T(128)S(1)}, s32[16]{0:T(128)}, u32[]{:S(2)}) copy-start(s32[16]{0:T(128)} %param.15) | copy-start | bytes 196
  10.2 1.0 %slice-start = ((bf16[2,1,8,128,128]{3,4,0,2,1:T(8,128)(2,1)}), bf16[2,1,7,128,128]{3,4,0,2,1:T(8,128)(2,1)S(1)}, s32[]{:S(2)}) async-start(bf16[2,1,8,128,128]{3,4,0,2,1:T(8,128)(2,1)} %copy-done.2), calls=%async_computation.2 | async-start | bytes 917504 | tf_op jit(solution)/shard_map/slice | solution.py:53
  13.8 8.5 %copy-start.6 = (s32[2]{0:T(128)S(1)}, s32[2]{0:T(128)}, u32[]{:S(2)}) copy-start(s32[2]{0:T(128)} %param.14) | copy-start | bytes 28
  13.8 22.6 %all-to-all-start = ((bf16[16,1,2,8,8,128]{5,4,3,2,1,0:T(8,128)(2,1)}), bf16[16,1,2,8,8,128]{5,4,3,2,1,0:T(8,128)(2,1)S(1)}, u32[]{:S(2)}, u32[]{:S(2)}) async-start(bf16[16,1,2,8,8,128]{5,4,3,2,1,0:T(8,128)(2,1)} %copy_bitcast_fusion), calls=%async_computation | async-start | bytes 1048576 | tf_op jit(solution)/shard_map/all_to_all | solution.py:69
  36.4 0.7 %copy-start.5 = (f32[8,128]{1,0:T(8,128)S(1)}, f32[8,128]{1,0:T(8,128)}, u32[]{:S(2)}) copy-start(f32[8,128]{1,0:T(8,128)} %param.13) | copy-start | bytes 12292
  40.3 11.1 %all-to-all-start.1 = ((f32[16,1,8]{2,1,0:T(1,128)}), f32[16,1,8]{2,1,0:T(1,128)S(1)}, u32[]{:S(2)}, u32[]{:S(2)}) async-start(f32[16,1,8]{2,1,0:T(1,128)} %bitcast.69), calls=%async_computation.1 | async-start | bytes 16384 | tf_op jit(solution)/shard_map/all_to_all | solution.py:95

commit v2 on v1

v2 whole, which is shorter than its diff:
```python
import functools

import jax
import jax.numpy as jnp
from jax import lax
from jax.experimental import pallas as pl
from jax.experimental.pallas import tpu as pltpu
from jax.sharding import PartitionSpec as P

phonon_occupation = 0.5

VMEM = pl.BlockSpec(memory_space=pltpu.VMEM)
SMEM = pl.BlockSpec(memory_space=pltpu.SMEM)
ANY = pl.BlockSpec(memory_space=pl.ANY)


def shifted(value, axis, steps):
    count = lax.axis_size(axis)
    initial, last = (max(0, -steps), min(count, count - steps))
    return lax.ppermute(value, axis, [(source, source + steps) for source in range(initial, last)])


def params():
    return pltpu.CompilerParams(vmem_limit_bytes=24 * 1024 * 1024)


def product(left, right):
    return jnp.dot(left, right, preferred_element_type=jnp.float32)


def product_t(left, right):
    return lax.dot_general(
        left, right, (((1,), (1,)), ((), ())), preferred_element_type=jnp.float32
    )


def pack_kernel(block_of, green, less, great, coupling, packed, sems):
    block = block_of()
    copies = [
        pltpu.make_async_copy(ref, packed.at[slot], sems.at[slot])
        for slot, ref in enumerate(
            (green.at[0, block], less.at[0, block], great.at[0, block], coupling.at[block])
        )
    ]
    for copy in copies:
        copy.start()
    for copy in copies:
        copy.wait()


def pack(block_of, green, less, great, coupling):
    orbitals = green.shape[-1]
    return pl.pallas_call(
        functools.partial(pack_kernel, block_of),
        out_shape=jax.ShapeDtypeStruct((4, orbitals, orbitals), green.dtype),
        in_specs=[ANY] * 4,
        out_specs=ANY,
        scratch_shapes=[pltpu.SemaphoreType.DMA((4,))],
        compiler_params=params(),
    )(green, less, great, coupling)


def through(operator, less, great):
    rows = operator.shape[0]
    half = product(operator, jnp.concatenate([less, great], 1)).astype(jnp.bfloat16)
    stacked = jnp.concatenate([half[:, :rows], half[:, rows:]], 0)
    return product_t(stacked, operator)


def green_kernel(swap, split, active, green, less, great, coupling, *rest):
    halos, (outgoing, diagonal, source) = rest[:-3], rest[-3:]
    block_count, orbitals = green.shape[1], green.shape[2]
    energy, place = lax.axis_index("energy"), lax.axis_index("space")
    places = lax.axis_size("space")
    open_count = active[energy] - place * block_count
    for block in range(block_count):
        source[block] = jnp.concatenate([less[0, block], great[0, block]], 0).astype(jnp.float32)
    for block in range(block_count):
        retarded, low, high = green[0, block], less[0, block], great[0, block]
        rise = block + 1 < block_count
        fall = block > 0
        hops = []
        if rise:
            hops.append(coupling[block].T)
        if fall:
            hops.append(coupling[block - 1])
        hops = product(jnp.concatenate(hops, 0), retarded).astype(jnp.bfloat16)
        both = product(hops, jnp.concatenate([low, high], 1)).astype(jnp.bfloat16)
        first = 0
        for wanted, target in ((rise, block + 1), (fall, block - 1)):
            if wanted:
                piece = slice(first, first + orbitals)
                stacked = jnp.concatenate([both[piece, :orbitals], both[piece, orbitals:]], 0)
                source[target] = source[target] + product_t(stacked, hops[piece])
                first += orbitals
    last = block_count - 1
    if swap:
        (halo,) = halos
        hop = jnp.where(place == 0, coupling[last], halo[3].T)
        edge = through(product(hop, halo[0]).astype(jnp.bfloat16), halo[1], halo[2])
        source[0] = source[0] + jnp.where(place > 0, edge, 0.0)
        source[last] = source[last] + jnp.where(place == 0, edge, 0.0)
    elif halos:
        before, after = halos
        hop = product(before[3].T, before[0]).astype(jnp.bfloat16)
        source[0] = source[0] + through(hop, before[1], before[2])
        hop = product(coupling[last], after[0]).astype(jnp.bfloat16)
        source[last] = source[last] + through(hop, after[1], after[2])
    row_ids = lax.broadcasted_iota(jnp.int32, (orbitals, orbitals), 0)
    column_ids = lax.broadcasted_iota(jnp.int32, (orbitals, orbitals), 1)
    on_diagonal = row_ids == column_ids
    for block in range(block_count):
        retarded = green[0, block]
        middle = source[block].astype(jnp.bfloat16)
        half = product(retarded, jnp.concatenate([middle[:orbitals], middle[orbitals:]], 1))
        half = half.astype(jnp.bfloat16)
        stacked = jnp.concatenate([half[:, :orbitals], half[:, orbitals:]], 0)
        result = product_t(stacked, retarded)
        result = result * (block < open_count).astype(jnp.float32)
        kinds = [result[:orbitals], result[orbitals:]]
        rounded = [kind.astype(jnp.bfloat16) for kind in kinds]
        total = rounded[0].astype(jnp.float32) + rounded[1].astype(jnp.float32)
        diagonal[block : block + 1] = jnp.sum(
            jnp.where(on_diagonal, total, 0.0), axis=0, keepdims=True
        )
        for kind in range(2):
            if split:
                devices, _, _, rows, _ = outgoing.shape
                outgoing[:, kind, block] = (
                    kinds[kind].reshape(devices, rows, orbitals).astype(jnp.bfloat16)
                )
            else:
                outgoing[kind, block] = rounded[kind]


def current_kernel(shift, rows, strength, parts, total):
    energies, _, block_count, row_count, orbitals = rows.shape
    total[...] = jnp.zeros_like(total)
    scale = strength[...] * (1.0 / orbitals)

    def step(energy, carry):
        low = rows[energy, 0].astype(jnp.float32) * scale
        high = rows[energy, 1].astype(jnp.float32) * scale
        for branch in range(2):
            target = energy + shift[branch]
            inside = (target < energies).astype(jnp.float32)
            there = jnp.minimum(target, energies - 1)
            gain = (1.0 + phonon_occupation) * inside
            loss = phonon_occupation * inside
            pair = gain * (high * rows[there, 0].astype(jnp.float32)) - loss * (
                low * rows[there, 1].astype(jnp.float32)
            )
            total[energy] = total[energy] + pair
            total[there] = total[there] - pair
        return carry

    lax.fori_loop(0, energies, step, 0)
    summed = jnp.sum(total[...], axis=2).reshape(energies * block_count, orbitals)
    ones = jnp.ones((8, orbitals), jnp.float32)
    flat = lax.dot_general(
        ones,
        summed,
        (((1,), (1,)), ((), ())),
        precision=lax.Precision.HIGHEST,
        preferred_element_type=jnp.float32,
    )
    for energy in range(energies):
        parts[energy] = flat[0:1, energy * block_count : (energy + 1) * block_count]


def sigma_kernel(shift, rows, strength, less_out, great_out):
    energies = rows.shape[0]
    factor = strength[...]

    def step(energy, carry):
        less_sum, great_sum = 0.0, 0.0
        for branch in range(2):
            above, below = energy + shift[branch], energy - shift[branch]
            has_above = (above < energies).astype(jnp.float32)
            has_below = (below >= 0).astype(jnp.float32)
            above = jnp.minimum(above, energies - 1)
            below = jnp.maximum(below, 0)
            more, fewer = 1.0 + phonon_occupation, phonon_occupation
            less_sum = (
                less_sum
                + (more * has_above) * rows[above, 0].astype(jnp.float32)
                + (fewer * has_below) * rows[below, 0].astype(jnp.float32)
            )
            great_sum = (
                great_sum
                + (more * has_below) * rows[below, 1].astype(jnp.float32)
                + (fewer * has_above) * rows[above, 1].astype(jnp.float32)
            )
        less_out[energy] = (factor * less_sum).astype(less_out.dtype)
        great_out[energy] = (factor * great_sum).astype(great_out.dtype)
        return carry

    lax.fori_loop(0, energies, step, 0)


def local(
    green_ret, prior_less, prior_great, coupling, phonon_coupling, phonon_shift, active_blocks
):
    _, block_count, orbitals, _ = green_ret.shape
    devices, places = lax.axis_size("energy"), lax.axis_size("space")
    row_count = orbitals // devices
    arrays = (green_ret, prior_less, prior_great, coupling)
    last = block_count - 1
    swap = places == 2
    if swap:
        edge = pack(lambda: last * (1 - lax.axis_index("space")), *arrays)
        halos = (lax.ppermute(edge, "space", [(0, 1), (1, 0)]),)
    elif places > 1:
        halos = (
            shifted(pack(lambda: last, *arrays), "space", 1),
            shifted(pack(lambda: 0, *arrays), "space", -1),
        )
    else:
        halos = ()
    split = row_count % 8 == 0
    if split:
        out_shape = (devices, 2, block_count, row_count, orbitals)
    else:
        out_shape = (2, block_count, orbitals, orbitals)
    outgoing, diagonal = pl.pallas_call(
        functools.partial(green_kernel, swap, split),
        out_shape=(
            jax.ShapeDtypeStruct(out_shape, jnp.bfloat16),
            jax.ShapeDtypeStruct((block_count, orbitals), jnp.float32),
        ),
        in_specs=[SMEM] + [VMEM] * (4 + len(halos)),
        out_specs=(VMEM, VMEM),
        scratch_shapes=[pltpu.VMEM((block_count, 2 * orbitals, orbitals), jnp.float32)],
        compiler_params=params(),
    )(active_blocks, *arrays, *halos)
    if not split:
        outgoing = outgoing.reshape(2, block_count, devices, row_count, orbitals)
        outgoing = jnp.transpose(outgoing, (2, 0, 1, 3, 4))
    ldos = jnp.sum(diagonal, axis=1)[None, :] / orbitals
    rows = lax.all_to_all(outgoing, "energy", split_axis=0, concat_axis=0, tiled=True)
    parts = pl.pallas_call(
        current_kernel,
        out_shape=jax.ShapeDtypeStruct((devices, 1, block_count), jnp.float32),
        in_specs=[SMEM, VMEM, VMEM],
        out_specs=VMEM,
        scratch_shapes=[pltpu.VMEM((devices, block_count, row_count, orbitals), jnp.float32)],
        compiler_params=params(),
    )(phonon_shift, rows, phonon_coupling)
    parts = lax.all_to_all(parts, "energy", split_axis=0, concat_axis=0, tiled=True)
    out = jax.ShapeDtypeStruct((devices, block_count, row_count, orbitals), jnp.bfloat16)
    sigma_l, sigma_g = pl.pallas_call(
        sigma_kernel,
        out_shape=(out, out),
        in_specs=[SMEM, VMEM, VMEM],
        out_specs=(VMEM, VMEM),
        compiler_params=params(),
        cost_estimate=pl.CostEstimate(
            flops=20 * rows.size, bytes_accessed=4 * rows.size, transcendentals=0
        ),
    )(phonon_shift, rows, phonon_coupling)
    current = jnp.sum(parts, axis=0)
    return (sigma_l, sigma_g, current, ldos)


def solution(mesh):
    return jax.shard_map(
        local,
        mesh=mesh,
        in_specs=(
            P("energy", "space", None, None),
            P("energy", "space", None, None),
            P("energy", "space", None, None),
            P("space", None, None),
            P("energy", None),
            P(),
            P(),
        ),
        out_specs=(
            P(None, "space", "energy", None),
            P(None, "space", "energy", None),
            P("energy", "space"),
            P("energy", "space"),
        ),
        check_vma=False,
    )
```

time: 52.5 us -> 47.9 us (0.912)
  Pallas kernels: 0 us -> 8.09 us
  waiting for transfers between devices: 13.7 us -> 21 us
  between operations: 6.1 us -> 0.69 us
  other arithmetic: 6.18 us -> 1.17 us
  starting transfers between devices: 17.2 us -> 12.7 us
  matrix products: 3.19 us -> 0 us
  local copies, waits for them, and re-layouts: 5.54 us -> 3.81 us
    all_to_all x1, waiting for transfers between devices: 6.98 us -> 15.3 us  [local(): lax.all_to_all(outgoing, 'energy', split_axis=0, concat_axis=0, tiled=True)]
    pallas_call x0 -> x4, Pallas kernels: none -> 8.09 us  [the longest x1 3.81 us: local(): pl.pallas_call(functools.partial(green_kernel, swap, split), out_shape=(j...]
    ppermute x2 -> x1, starting transfers between devices: 4.92 us -> 0.52 us  [local(): halos = (lax.ppermute(edge, 'space', [(0, 1), (1, 0)]),)]
    dot_general x4 -> x0, matrix products: 3.19 us -> none  [the longest x2 2.16 us: sandwich(): jnp.einsum('kenil,enml->kenim', half_product, retarded, preferred_element...]
    reduce_sum x2, other arithmetic: 3.19 us -> 0.66 us  [the longest x1 0.54 us: local(): current = jnp.sum(parts, axis=0)]
    all_to_all x1, waiting for transfers between devices: 6.76 us -> 4.78 us  [local(): lax.all_to_all(parts, 'energy', split_axis=0, concat_axis=0, tiled=True)]
    and x2 -> x0, other arithmetic: 1.31 us -> none  [displaced(): inside_grid = (target >= 0) & (target < energies)]
    slice x4 -> x0, local copies, waits for them, and re-layouts: 1.11 us -> none  [the longest x1 0.58 us: local(): offset = phonon_shift[branch]]
  transfers between devices with their start and end apart: 4 -> 3, of which waited for: 2 -> 3; matrix products, arithmetic and copies ran while one was open for 9% -> 1% of each run, Pallas kernels for 0% -> 4%
where the time goes in v2:
time: 47.9 us; the launch traced here: 47.5 us
  waiting for transfers between devices  21 us (44%)
  starting transfers between devices  12.7 us (27%)
  Pallas kernels  8.09 us (17%)
  local copies, waits for them, and re-layouts  3.81 us (8%)
  other arithmetic  1.17 us (2%)
  between operations  0.69 us (1%)
    all_to_all x1, waiting for transfers between devices, local(): lax.all_to_all(outgoing, 'energy', split_axis=0, concat_axis=0, tiled=True)  15.3 us
    all_to_all x1, starting transfers between devices, local(): lax.all_to_all(outgoing, 'energy', split_axis=0, concat_axis=0, tiled=True)  8.22 us
    all_to_all x1, waiting for transfers between devices, local(): lax.all_to_all(parts, 'energy', split_axis=0, concat_axis=0, tiled=True)  4.78 us
    all_to_all x1, starting transfers between devices, local(): lax.all_to_all(parts, 'energy', split_axis=0, concat_axis=0, tiled=True)  3.94 us
    pallas_call x1, Pallas kernels, local(): pl.pallas_call(functools.partial(green_kernel, swap, split), out_shape=(j...  3.81 us
    unnamed x14, local copies, waits for them, and re-layouts  3.81 us
    pallas_call x1, Pallas kernels, local(): pl.pallas_call(current_kernel, out_shape=jax.ShapeDtypeStruct((devices, 1...  2.12 us
    pallas_call x1, Pallas kernels, local(): pl.pallas_call(sigma_kernel, out_shape=(out, out), in_specs=[SMEM, VMEM,...  1.97 us
  transfers between devices with their start and end apart: 3, of which 3 were waited for; matrix products, arithmetic and copies ran while one was open for 1% of the time, Pallas kernels for 4%

profile of v2, /device:TPU:0, one launch (start us, length us, event | category | flops | bytes accessed | tf_op | source)
XLA Modules:
  0.0 47.5 jit_solution(4357235359316841756)
XLA Ops:
  0.6 0.0 copy-start
  0.6 0.9 %copy-done = bf16[1,8,128,128]{3,2,1,0:T(8,128)(2,1)S(1)} copy-done((bf16[1,8,128,128]{3,2,1,0:T(8,128)(2,1)S(1)}, bf16[1,8,128,128]{3,2,1,0:T(8,128)(2,1)}, u32[]{:S(2)}) %copy-start) | copy-done | bytes 262168
  1.6 0.0 copy-start.1
  1.6 0.9 %copy-done.1 = bf16[1,8,128,128]{3,2,1,0:T(8,128)(2,1)S(1)} copy-done((bf16[1,8,128,128]{3,2,1,0:T(8,128)(2,1)S(1)}, bf16[1,8,128,128]{3,2,1,0:T(8,128)(2,1)}, u32[]{:S(2)}) %copy-start.1) | copy-done | bytes 262168
  2.5 0.0 copy-start.2
  2.5 0.9 %copy-done.2 = bf16[1,8,128,128]{3,2,1,0:T(8,128)(2,1)S(1)} copy-done((bf16[1,8,128,128]{3,2,1,0:T(8,128)(2,1)S(1)}, bf16[1,8,128,128]{3,2,1,0:T(8,128)(2,1)}, u32[]{:S(2)}) %copy-start.2) | copy-done | bytes 262168
  3.5 0.0 copy-start.3
  3.5 0.9 %copy-done.3 = bf16[8,128,128]{2,1,0:T(8,128)(2,1)S(1)} copy-done((bf16[8,128,128]{2,1,0:T(8,128)(2,1)S(1)}, bf16[8,128,128]{2,1,0:T(8,128)(2,1)}, u32[]{:S(2)}) %copy-start.3) | copy-done | bytes 262168
  4.4 0.0 copy-start.6
  4.4 0.2 shard_map.102
  4.6 0.5 %collective-permute-start = (bf16[4,128,128]{2,1,0:T(8,128)(2,1)S(1)}, bf16[4,128,128]{2,1,0:T(8,128)(2,1)S(1)}, u32[]{:S(2)}, u32[]{:S(2)}) collective-permute-start(bf16[4,128,128]{2,1,0:T(8,128)(2,1)S(1)} %shard_map.102), channel_id=1, source_target_pairs={{0,1},{1,0},{2,3},{3,2},{4,5},{5,4},{6,7},{7,6},{8,9},{9,8},{10,11... | collective-permute-start | bytes 393224 | tf_op jit(solution)/shard_map/ppermute | solution.py:212
  5.1 1.0 %collective-permute-done.rest_0_ = bf16[4,128,128]{2,1,0:T(8,128)(2,1)S(1)} collective-permute-done((bf16[4,128,128]{2,1,0:T(8,128)(2,1)S(1)}, bf16[4,128,128]{2,1,0:T(8,128)(2,1)S(1)}, u32[]{:S(2)}, u32[]{:S(2)}) %collective-permute-start) | collective-permute-done | bytes 131104 | tf_op jit(solution)/shard_map/ppermute | solution.py:212
  6.1 0.0 copy-done.6
  6.1 3.8 %shard_map.103 = (bf16[16,2,8,8,128]{4,3,2,1,0:T(8,128)(2,1)}, f32[8,128]{1,0:T(8,128)S(1)}) custom-call(s32[16]{0:T(128)S(1)} %copy-done.6, bf16[1,8,128,128]{3,2,1,0:T(8,128)(2,1)S(1)} %copy-done, bf16[1,8,128,128]{3,2,1,0:T(8,128)(2,1)S(1)} %copy-done.1, bf16[1,8,128,128]{3,2,1,0:T(8,128)(2,1)S(1)} %copy-done.2, bf16[8,128,128]{2,1,0:T(8,128)(2,1)S(1)} %copy-done.3, ...), custom_call_target="tpu_custom_call" | custom-call | tf_op jit(solution)/shard_map/pallas_call | solution.py:225
  10.0 8.2 %all-to-all-start = ((bf16[16,2,8,8,128]{4,3,2,1,0:T(8,128)(2,1)}), bf16[16,2,8,8,128]{4,3,2,1,0:T(8,128)(2,1)S(1)}, u32[]{:S(2)}, u32[]{:S(2)}) async-start(bf16[16,2,8,8,128]{4,3,2,1,0:T(8,128)(2,1)} %get-tuple-element.8), calls=%async_computation | async-start | bytes 1048576 | tf_op jit(solution)/shard_map/all_to_all | solution.py:240
  18.2 0.0 copy-start.4
  18.2 0.0 copy-start.5
  18.2 0.1 reduce_sum.22
  18.3 15.3 %all-to-all-done.rows = bf16[16,2,8,8,128]{4,3,2,1,0:T(8,128)(2,1)S(1)} async-done(((bf16[16,2,8,8,128]{4,3,2,1,0:T(8,128)(2,1)}), bf16[16,2,8,8,128]{4,3,2,1,0:T(8,128)(2,1)S(1)}, u32[]{:S(2)}, u32[]{:S(2)}) %all-to-all-start) | async-done | bytes 524320 | tf_op jit(solution)/shard_map/all_to_all | solution.py:240
  33.6 0.0 copy-done.4
  33.6 0.0 copy-done.5
  33.6 2.1 %shard_map.105 = f32[16,1,8]{2,1,0:T(1,128)} custom-call(s32[2]{0:T(128)S(1)} %copy-done.5, bf16[16,2,8,8,128]{4,3,2,1,0:T(8,128)(2,1)S(1)} %all-to-all-done.rows, f32[8,128]{1,0:T(8,128)S(1)} %copy-done.4), custom_call_target="tpu_custom_call" | custom-call | tf_op jit(solution)/shard_map/pallas_call | solution.py:241
  35.7 3.9 %all-to-all-start.1 = ((f32[16,1,8]{2,1,0:T(1,128)}), f32[16,1,8]{2,1,0:T(1,128)S(1)}, u32[]{:S(2)}, u32[]{:S(2)}) async-start(f32[16,1,8]{2,1,0:T(1,128)} %shard_map.105), calls=%async_computation.1 | async-start | bytes 16384 | tf_op jit(solution)/shard_map/all_to_all | solution.py:249
  39.7 0.5 %multiply_bitcast_fusion = f32[1,8]{1,0:T(1,128)} fusion(f32[8]{0:T(128)S(1)} %reduce_sum.22), kind=kLoop, calls=%fused_computation | loop fusion | flops 8 | bytes 64 | tf_op jit(solution)/shard_map/div | solution.py:239
  40.2 2.0 %shard_map.104 = (bf16[16,8,8,128]{3,2,1,0:T(8,128)(2,1)}, bf16[16,8,8,128]{3,2,1,0:T(8,128)(2,1)}) custom-call(s32[2]{0:T(128)S(1)} %copy-done.5, bf16[16,2,8,8,128]{4,3,2,1,0:T(8,128)(2,1)S(1)} %all-to-all-done.rows, f32[8,128]{1,0:T(8,128)S(1)} %copy-done.4), custom_call_target="tpu_custom_call" | custom-call | flops 5242880 | bytes 1048576 | tf_op jit(solution)/shard_map/pallas_call | solution.py:251
  42.1 4.8 %all-to-all-done.1 = f32[16,1,8]{2,1,0:T(1,128)S(1)} async-done(((f32[16,1,8]{2,1,0:T(1,128)}), f32[16,1,8]{2,1,0:T(1,128)S(1)}, u32[]{:S(2)}, u32[]{:S(2)}) %all-to-all-start.1) | async-done | bytes 544 | tf_op jit(solution)/shard_map/all_to_all | solution.py:249
  46.9 0.5 %reduce_sum.20 = f32[8]{0:T(128)} reduce(f32[16,1,8]{2,1,0:T(1,128)S(1)} %all-to-all-done.1, f32[]{:T(128)} %constant.1.clone.1), dimensions={0,1}, to_apply=%region_0.0 | reduce | flops 120 | bytes 548 | tf_op jit(solution)/shard_map/reduce_sum | solution.py:261
Async XLA Ops:
  0.6 1.0 %copy-start = (bf16[1,8,128,128]{3,2,1,0:T(8,128)(2,1)S(1)}, bf16[1,8,128,128]{3,2,1,0:T(8,128)(2,1)}, u32[]{:S(2)}) copy-start(bf16[1,8,128,128]{3,2,1,0:T(8,128)(2,1)} %green.3) | copy-start | bytes 786436
  1.6 0.9 %copy-start.1 = (bf16[1,8,128,128]{3,2,1,0:T(8,128)(2,1)S(1)}, bf16[1,8,128,128]{3,2,1,0:T(8,128)(2,1)}, u32[]{:S(2)}) copy-start(bf16[1,8,128,128]{3,2,1,0:T(8,128)(2,1)} %less.3) | copy-start | bytes 786436
  2.5 0.9 %copy-start.2 = (bf16[1,8,128,128]{3,2,1,0:T(8,128)(2,1)S(1)}, bf16[1,8,128,128]{3,2,1,0:T(8,128)(2,1)}, u32[]{:S(2)}) copy-start(bf16[1,8,128,128]{3,2,1,0:T(8,128)(2,1)} %great.3) | copy-start | bytes 786436
  3.5 0.9 %copy-start.3 = (bf16[8,128,128]{2,1,0:T(8,128)(2,1)S(1)}, bf16[8,128,128]{2,1,0:T(8,128)(2,1)}, u32[]{:S(2)}) copy-start(bf16[8,128,128]{2,1,0:T(8,128)(2,1)} %coupling.3) | copy-start | bytes 786436
  4.4 1.7 %copy-start.6 = (s32[16]{0:T(128)S(1)}, s32[16]{0:T(128)}, u32[]{:S(2)}) copy-start(s32[16]{0:T(128)} %active.1) | copy-start | bytes 196
  4.6 1.5 %collective-permute-start = (bf16[4,128,128]{2,1,0:T(8,128)(2,1)S(1)}, bf16[4,128,128]{2,1,0:T(8,128)(2,1)S(1)}, u32[]{:S(2)}, u32[]{:S(2)}) collective-permute-start(bf16[4,128,128]{2,1,0:T(8,128)(2,1)S(1)} %shard_map.102), channel_id=1, source_target_pairs={{0,1},{1,0},{2,3},{3,2},{4,5},{5,4},{6,7},{7,6},{8,9},{9,8},{10,11... | collective-permute-start | bytes 393224 | tf_op jit(solution)/shard_map/ppermute | solution.py:212
  10.0 23.6 %all-to-all-start = ((bf16[16,2,8,8,128]{4,3,2,1,0:T(8,128)(2,1)}), bf16[16,2,8,8,128]{4,3,2,1,0:T(8,128)(2,1)S(1)}, u32[]{:S(2)}, u32[]{:S(2)}) async-start(bf16[16,2,8,8,128]{4,3,2,1,0:T(8,128)(2,1)} %get-tuple-element.8), calls=%async_computation | async-start | bytes 1048576 | tf_op jit(solution)/shard_map/all_to_all | solution.py:240
  18.2 15.4 %copy-start.4 = (f32[8,128]{1,0:T(8,128)S(1)}, f32[8,128]{1,0:T(8,128)}, u32[]{:S(2)}) copy-start(f32[8,128]{1,0:T(8,128)} %strength.3) | copy-start | bytes 12292
  18.2 15.4 %copy-start.5 = (s32[2]{0:T(128)S(1)}, s32[2]{0:T(128)}, u32[]{:S(2)}) copy-start(s32[2]{0:T(128)} %shift.3) | copy-start | bytes 28
  35.7 11.2 %all-to-all-start.1 = ((f32[16,1,8]{2,1,0:T(1,128)}), f32[16,1,8]{2,1,0:T(1,128)S(1)}, u32[]{:S(2)}, u32[]{:S(2)}) async-start(f32[16,1,8]{2,1,0:T(1,128)} %shard_map.105), calls=%async_computation.1 | async-start | bytes 16384 | tf_op jit(solution)/shard_map/all_to_all | solution.py:249

commit v3 on v2

--- a/solution.py
+++ b/solution.py
@@ -34,6 +34,14 @@
     )
 
 
+def held(shape, dtype):
+    return pltpu.VMEM(shape, dtype)
+
+
+def in_hbm(*arrays):
+    return [pltpu.with_memory_space_constraint(array, pltpu.HBM) for array in arrays]
+
+
 def pack_kernel(block_of, green, less, great, coupling, packed, sems):
     block = block_of()
     copies = [
@@ -52,12 +60,12 @@
     orbitals = green.shape[-1]
     return pl.pallas_call(
         functools.partial(pack_kernel, block_of),
-        out_shape=jax.ShapeDtypeStruct((4, orbitals, orbitals), green.dtype),
+        out_shape=held((4, orbitals, orbitals), green.dtype),
         in_specs=[ANY] * 4,
-        out_specs=ANY,
+        out_specs=VMEM,
         scratch_shapes=[pltpu.SemaphoreType.DMA((4,))],
         compiler_params=params(),
-    )(green, less, great, coupling)
+    )(*in_hbm(green, less, great, coupling))
 
 
 def through(operator, less, great):
@@ -67,16 +75,31 @@
     return product_t(stacked, operator)
 
 
-def green_kernel(swap, split, active, green, less, great, coupling, *rest):
-    halos, (outgoing, diagonal, source) = rest[:-3], rest[-3:]
-    block_count, orbitals = green.shape[1], green.shape[2]
-    energy, place = lax.axis_index("energy"), lax.axis_index("space")
-    places = lax.axis_size("space")
-    open_count = active[energy] - place * block_count
+def hop_kernel(
+    green_in, less_in, great_in, coupling_in, green, coupling, source, less, great, sems
+):
+    block_count, orbitals = green.shape[0], green.shape[1]
+    copies = []
     for block in range(block_count):
-        source[block] = jnp.concatenate([less[0, block], great[0, block]], 0).astype(jnp.float32)
+        pairs = (
+            (coupling_in.at[block], coupling.at[block]),
+            (green_in.at[0, block], green.at[block]),
+            (less_in.at[0, block], less.at[block]),
+            (great_in.at[0, block], great.at[block]),
+        )
+        copies.append(
+            [
+                pltpu.make_async_copy(origin, target, sems.at[block, slot])
+                for slot, (origin, target) in enumerate(pairs)
+            ]
+        )
+    for group in copies:
+        for copy in group:
+            copy.start()
     for block in range(block_count):
-        retarded, low, high = green[0, block], less[0, block], great[0, block]
+        for copy in copies[block]:
+            copy.wait()
+        retarded, low, high = green[block], less[block], great[block]
         rise = block + 1 < block_count
         fall = block > 0
         hops = []
@@ -86,32 +109,44 @@
             hops.append(coupling[block - 1])
         hops = product(jnp.concatenate(hops, 0), retarded).astype(jnp.bfloat16)
         both = product(hops, jnp.concatenate([low, high], 1)).astype(jnp.bfloat16)
+        prior = jnp.concatenate([low, high], 0).astype(jnp.float32)
+        source[block] = source[block] + prior if fall else prior
         first = 0
         for wanted, target in ((rise, block + 1), (fall, block - 1)):
             if wanted:
                 piece = slice(first, first + orbitals)
                 stacked = jnp.concatenate([both[piece, :orbitals], both[piece, orbitals:]], 0)
-                source[target] = source[target] + product_t(stacked, hops[piece])
+                moved = product_t(stacked, hops[piece])
+                source[target] = moved if target > block else source[target] + moved
                 first += orbitals
+
+
+def green_kernel(swap, split, active, green, coupling, source, *rest):
+    halos, (outgoing, diagonal) = rest[:-2], rest[-2:]
+    block_count, orbitals = green.shape[0], green.shape[1]
+    energy, place = lax.axis_index("energy"), lax.axis_index("space")
+    open_count = active[energy] - place * block_count
     last = block_count - 1
+    added = {}
     if swap:
         (halo,) = halos
         hop = jnp.where(place == 0, coupling[last], halo[3].T)
         edge = through(product(hop, halo[0]).astype(jnp.bfloat16), halo[1], halo[2])
-        source[0] = source[0] + jnp.where(place > 0, edge, 0.0)
-        source[last] = source[last] + jnp.where(place == 0, edge, 0.0)
+        added = {0: jnp.where(place > 0, edge, 0.0), last: jnp.where(place == 0, edge, 0.0)}
     elif halos:
         before, after = halos
         hop = product(before[3].T, before[0]).astype(jnp.bfloat16)
-        source[0] = source[0] + through(hop, before[1], before[2])
+        added[0] = through(hop, before[1], before[2])
         hop = product(coupling[last], after[0]).astype(jnp.bfloat16)
-        source[last] = source[last] + through(hop, after[1], after[2])
+        added[last] = through(hop, after[1], after[2])
     row_ids = lax.broadcasted_iota(jnp.int32, (orbitals, orbitals), 0)
     column_ids = lax.broadcasted_iota(jnp.int32, (orbitals, orbitals), 1)
     on_diagonal = row_ids == column_ids
-    for block in range(block_count):
-        retarded = green[0, block]
-        middle = source[block].astype(jnp.bfloat16)
+    for block in [*range(1, last), 0, last]:
+        retarded, middle = green[block], source[block]
+        if block in added:
+            middle = middle + added[block]
+        middle = middle.astype(jnp.bfloat16)
         half = product(retarded, jnp.concatenate([middle[:orbitals], middle[orbitals:]], 1))
         half = half.astype(jnp.bfloat16)
         stacked = jnp.concatenate([half[:, :orbitals], half[:, orbitals:]], 0)
@@ -222,17 +257,38 @@
         out_shape = (devices, 2, block_count, row_count, orbitals)
     else:
         out_shape = (2, block_count, orbitals, orbitals)
+    blocks = (block_count, orbitals, orbitals)
+    green, hops, source = pl.pallas_call(
+        hop_kernel,
+        out_shape=(
+            held(blocks, jnp.bfloat16),
+            held(blocks, jnp.bfloat16),
+            held((block_count, 2 * orbitals, orbitals), jnp.float32),
+        ),
+        in_specs=[ANY] * 4,
+        out_specs=(VMEM, VMEM, VMEM),
+        scratch_shapes=[
+            pltpu.VMEM(blocks, jnp.bfloat16),
+            pltpu.VMEM(blocks, jnp.bfloat16),
+            pltpu.SemaphoreType.DMA((block_count, 4)),
+        ],
+        compiler_params=params(),
+        cost_estimate=pl.CostEstimate(
+            flops=20 * block_count * orbitals**3,
+            bytes_accessed=8 * block_count * orbitals**2,
+            transcendentals=0,
+        ),
+    )(*in_hbm(*arrays))
     outgoing, diagonal = pl.pallas_call(
         functools.partial(green_kernel, swap, split),
         out_shape=(
-            jax.ShapeDtypeStruct(out_shape, jnp.bfloat16),
+            held(out_shape, jnp.bfloat16),
             jax.ShapeDtypeStruct((block_count, orbitals), jnp.float32),
         ),
-        in_specs=[SMEM] + [VMEM] * (4 + len(halos)),
+        in_specs=[SMEM] + [VMEM] * (3 + len(halos)),
         out_specs=(VMEM, VMEM),
-        scratch_shapes=[pltpu.VMEM((block_count, 2 * orbitals, orbitals), jnp.float32)],
-        compiler_params=params(),
-    )(active_blocks, *arrays, *halos)
+        compiler_params=params(),
+    )(active_blocks, green, hops, source, *halos)
     if not split:
         outgoing = outgoing.reshape(2, block_count, devices, row_count, orbitals)
         outgoing = jnp.transpose(outgoing, (2, 0, 1, 3, 4))
@@ -240,7 +296,7 @@
     rows = lax.all_to_all(outgoing, "energy", split_axis=0, concat_axis=0, tiled=True)
     parts = pl.pallas_call(
         current_kernel,
-        out_shape=jax.ShapeDtypeStruct((devices, 1, block_count), jnp.float32),
+        out_shape=held((devices, 1, block_count), jnp.float32),
         in_specs=[SMEM, VMEM, VMEM],
         out_specs=VMEM,
         scratch_shapes=[pltpu.VMEM((devices, block_count, row_count, orbitals), jnp.float32)],

time: 47.9 us -> 47.5 us (level)
  Pallas kernels: 8.09 us -> 11.9 us
  local copies, waits for them, and re-layouts: 3.81 us -> 0.66 us
  waiting for transfers between devices: 21 us -> 20.1 us
    pallas_call x3 -> x4, Pallas kernels: 6.12 us -> 9.88 us  [the longest x1 4.81 us: local(): pl.pallas_call(hop_kernel, out_shape=(held(blocks, jnp.bfloat16), held(bl...]
    unnamed x14 -> x6, local copies, waits for them, and re-layouts: 3.81 us -> 0.66 us
    ppermute x1, waiting for transfers between devices: 0.99 us -> 0.01 us  [local(): halos = (lax.ppermute(edge, 'space', [(0, 1), (1, 0)]),)]
  transfers between devices with their start and end apart: 3 -> 3, of which waited for: 3 -> 2; matrix products, arithmetic and copies ran while one was open for 1% -> 1% of each run, Pallas kernels for 4% -> 14%
where the time goes in v3:
time: 47.5 us; the launch traced here: 47.1 us
  waiting for transfers between devices  20.1 us (42%)
  starting transfers between devices  12.6 us (27%)
  Pallas kernels  11.9 us (25%)
  other arithmetic  1.17 us (2%)
  between operations  0.7 us (1%)
  local copies, waits for them, and re-layouts  0.66 us (1%)
    all_to_all x1, waiting for transfers between devices, local(): lax.all_to_all(outgoing, 'energy', split_axis=0, concat_axis=0, tiled=True)  15.3 us
    all_to_all x1, starting transfers between devices, local(): lax.all_to_all(outgoing, 'energy', split_axis=0, concat_axis=0, tiled=True)  7.88 us
    pallas_call x1, Pallas kernels, local(): pl.pallas_call(hop_kernel, out_shape=(held(blocks, jnp.bfloat16), held(bl...  4.81 us
    all_to_all x1, waiting for transfers between devices, local(): lax.all_to_all(parts, 'energy', split_axis=0, concat_axis=0, tiled=True)  4.79 us
    all_to_all x1, starting transfers between devices, local(): lax.all_to_all(parts, 'energy', split_axis=0, concat_axis=0, tiled=True)  4.23 us
    pallas_call x1, Pallas kernels, local(): pl.pallas_call(current_kernel, out_shape=held((devices, 1, block_count),...  2.12 us
    pallas_call x1, Pallas kernels, local(): pl.pallas_call(functools.partial(green_kernel, swap, split), out_shape=(h...  2.11 us
    pallas_call x1, Pallas kernels, local(): pl.pallas_call(sigma_kernel, out_shape=(out, out), in_specs=[SMEM, VMEM,...  1.97 us
  transfers between devices with their start and end apart: 3, of which 2 were waited for; matrix products, arithmetic and copies ran while one was open for 1% of the time, Pallas kernels for 14%

profile of v3, /device:TPU:0, one launch (start us, length us, event | category | flops | bytes accessed | tf_op | source)
XLA Modules:
  0.0 47.1 jit_solution(16302976908421421223)
XLA Ops:
  0.6 0.9 %shard_map.103 = bf16[4,128,128]{2,1,0:T(8,128)(2,1)S(1)} custom-call(bf16[1,8,128,128]{3,2,1,0:T(8,128)(2,1)} %green.1, bf16[1,8,128,128]{3,2,1,0:T(8,128)(2,1)} %less.1, bf16[1,8,128,128]{3,2,1,0:T(8,128)(2,1)} %great.1, bf16[8,128,128]{2,1,0:T(8,128)(2,1)} %coupling.1), custom_call_target="tpu_custom_call" | custom-call | tf_op jit(solution)/shard_map/pallas_call | solution.py:61
  1.5 0.5 %collective-permute-start = (bf16[4,128,128]{2,1,0:T(8,128)(2,1)S(1)}, bf16[4,128,128]{2,1,0:T(8,128)(2,1)S(1)}, u32[]{:S(2)}, u32[]{:S(2)}) collective-permute-start(bf16[4,128,128]{2,1,0:T(8,128)(2,1)S(1)} %shard_map.103), channel_id=1, source_target_pairs={{0,1},{1,0},{2,3},{3,2},{4,5},{5,4},{6,7},{7,6},{8,9},{9,8},{10,11... | collective-permute-start | bytes 393224 | tf_op jit(solution)/shard_map/ppermute | solution.py:247
  2.0 4.8 %shard_map.102 = (bf16[8,128,128]{2,1,0:T(8,128)(2,1)S(1)}, bf16[8,128,128]{2,1,0:T(8,128)(2,1)S(1)}, f32[8,256,128]{2,1,0:T(8,128)S(1)}) custom-call(bf16[1,8,128,128]{3,2,1,0:T(8,128)(2,1)} %green.1, bf16[1,8,128,128]{3,2,1,0:T(8,128)(2,1)} %less.1, bf16[1,8,128,128]{3,2,1,0:T(8,128)(2,1)} %great.1, bf16[8,128,128]{2,1,0:T(8,128)(2,1)} %coupling.1), custom_call_target="tpu_custom_call" | custom-call | flops 335544320 | bytes 1048576 | tf_op jit(solution)/shard_map/pallas_call | solution.py:261
  6.8 0.0 collective-permute-done.rest_0_
  6.8 0.0 copy-start.2
  6.8 0.6 %copy-done.2 = s32[16]{0:T(128)S(1)} copy-done((s32[16]{0:T(128)S(1)}, s32[16]{0:T(128)}, u32[]{:S(2)}) %copy-start.2) | copy-done | bytes 88
  7.5 2.1 %shard_map.104 = (bf16[16,2,8,8,128]{4,3,2,1,0:T(8,128)(2,1)}, f32[8,128]{1,0:T(8,128)S(1)}) custom-call(s32[16]{0:T(128)S(1)} %copy-done.2, bf16[8,128,128]{2,1,0:T(8,128)(2,1)S(1)} %get-tuple-element.11.green, bf16[8,128,128]{2,1,0:T(8,128)(2,1)S(1)} %get-tuple-element.12.coupling, f32[8,256,128]{2,1,0:T(8,128)S(1)} %get-tuple-element.13.source, ...), custom_call_target="tpu_custom_call" | custom-call | tf_op jit(solution)/shard_map/pallas_call | solution.py:282
  9.6 7.9 %all-to-all-start = ((bf16[16,2,8,8,128]{4,3,2,1,0:T(8,128)(2,1)}), bf16[16,2,8,8,128]{4,3,2,1,0:T(8,128)(2,1)S(1)}, u32[]{:S(2)}, u32[]{:S(2)}) async-start(bf16[16,2,8,8,128]{4,3,2,1,0:T(8,128)(2,1)} %get-tuple-element.14), calls=%async_computation | async-start | bytes 1048576 | tf_op jit(solution)/shard_map/all_to_all | solution.py:296
  17.5 0.0 copy-start
  17.5 0.0 copy-start.1
  17.5 0.1 reduce_sum.22
  17.6 15.3 %all-to-all-done.rows = bf16[16,2,8,8,128]{4,3,2,1,0:T(8,128)(2,1)S(1)} async-done(((bf16[16,2,8,8,128]{4,3,2,1,0:T(8,128)(2,1)}), bf16[16,2,8,8,128]{4,3,2,1,0:T(8,128)(2,1)S(1)}, u32[]{:S(2)}, u32[]{:S(2)}) %all-to-all-start) | async-done | bytes 524320 | tf_op jit(solution)/shard_map/all_to_all | solution.py:296
  32.9 0.0 copy-done
  32.9 0.0 copy-done.1
  33.0 2.1 %shard_map.106 = f32[16,1,8]{2,1,0:T(1,128)} custom-call(s32[2]{0:T(128)S(1)} %copy-done.1, bf16[16,2,8,8,128]{4,3,2,1,0:T(8,128)(2,1)S(1)} %all-to-all-done.rows, f32[8,128]{1,0:T(8,128)S(1)} %copy-done), custom_call_target="tpu_custom_call" | custom-call | tf_op jit(solution)/shard_map/pallas_call | solution.py:297
  35.1 4.2 %all-to-all-start.1 = ((f32[16,1,8]{2,1,0:T(1,128)}), f32[16,1,8]{2,1,0:T(1,128)S(1)}, u32[]{:S(2)}, u32[]{:S(2)}) async-start(f32[16,1,8]{2,1,0:T(1,128)} %shard_map.106), calls=%async_computation.1 | async-start | bytes 16384 | tf_op jit(solution)/shard_map/all_to_all | solution.py:305
  39.3 0.5 %multiply_bitcast_fusion = f32[1,8]{1,0:T(1,128)} fusion(f32[8]{0:T(128)S(1)} %reduce_sum.22), kind=kLoop, calls=%fused_computation | loop fusion | flops 8 | bytes 64 | tf_op jit(solution)/shard_map/div | solution.py:295
  39.8 2.0 %shard_map.105 = (bf16[16,8,8,128]{3,2,1,0:T(8,128)(2,1)}, bf16[16,8,8,128]{3,2,1,0:T(8,128)(2,1)}) custom-call(s32[2]{0:T(128)S(1)} %copy-done.1, bf16[16,2,8,8,128]{4,3,2,1,0:T(8,128)(2,1)S(1)} %all-to-all-done.rows, f32[8,128]{1,0:T(8,128)S(1)} %copy-done), custom_call_target="tpu_custom_call" | custom-call | flops 5242880 | bytes 1048576 | tf_op jit(solution)/shard_map/pallas_call | solution.py:307
  41.8 4.8 %all-to-all-done.1 = f32[16,1,8]{2,1,0:T(1,128)S(1)} async-done(((f32[16,1,8]{2,1,0:T(1,128)}), f32[16,1,8]{2,1,0:T(1,128)S(1)}, u32[]{:S(2)}, u32[]{:S(2)}) %all-to-all-start.1) | async-done | bytes 544 | tf_op jit(solution)/shard_map/all_to_all | solution.py:305
  46.6 0.5 %reduce_sum.20 = f32[8]{0:T(128)} reduce(f32[16,1,8]{2,1,0:T(1,128)S(1)} %all-to-all-done.1, f32[]{:T(128)} %constant.1.clone.1), dimensions={0,1}, to_apply=%region_0.0 | reduce | flops 120 | bytes 548 | tf_op jit(solution)/shard_map/reduce_sum | solution.py:317
Async XLA Ops:
  1.5 5.3 %collective-permute-start = (bf16[4,128,128]{2,1,0:T(8,128)(2,1)S(1)}, bf16[4,128,128]{2,1,0:T(8,128)(2,1)S(1)}, u32[]{:S(2)}, u32[]{:S(2)}) collective-permute-start(bf16[4,128,128]{2,1,0:T(8,128)(2,1)S(1)} %shard_map.103), channel_id=1, source_target_pairs={{0,1},{1,0},{2,3},{3,2},{4,5},{5,4},{6,7},{7,6},{8,9},{9,8},{10,11... | collective-permute-start | bytes 393224 | tf_op jit(solution)/shard_map/ppermute | solution.py:247
  6.8 0.7 %copy-start.2 = (s32[16]{0:T(128)S(1)}, s32[16]{0:T(128)}, u32[]{:S(2)}) copy-start(s32[16]{0:T(128)} %active.1) | copy-start | bytes 196
  9.6 23.3 %all-to-all-start = ((bf16[16,2,8,8,128]{4,3,2,1,0:T(8,128)(2,1)}), bf16[16,2,8,8,128]{4,3,2,1,0:T(8,128)(2,1)S(1)}, u32[]{:S(2)}, u32[]{:S(2)}) async-start(bf16[16,2,8,8,128]{4,3,2,1,0:T(8,128)(2,1)} %get-tuple-element.14), calls=%async_computation | async-start | bytes 1048576 | tf_op jit(solution)/shard_map/all_to_all | solution.py:296
  17.5 15.5 %copy-start = (f32[8,128]{1,0:T(8,128)S(1)}, f32[8,128]{1,0:T(8,128)}, u32[]{:S(2)}) copy-start(f32[8,128]{1,0:T(8,128)} %strength.3) | copy-start | bytes 12292
  17.5 15.4 %copy-start.1 = (s32[2]{0:T(128)S(1)}, s32[2]{0:T(128)}, u32[]{:S(2)}) copy-start(s32[2]{0:T(128)} %shift.3) | copy-start | bytes 28
  35.1 11.5 %all-to-all-start.1 = ((f32[16,1,8]{2,1,0:T(1,128)}), f32[16,1,8]{2,1,0:T(1,128)S(1)}, u32[]{:S(2)}, u32[]{:S(2)}) async-start(f32[16,1,8]{2,1,0:T(1,128)} %shard_map.106), calls=%async_computation.1 | async-start | bytes 16384 | tf_op jit(solution)/shard_map/all_to_all | solution.py:305

commit v4 on v2

v4 whole, which is shorter than its diff:
```python
import functools

import jax
import jax.numpy as jnp
from jax import lax
from jax.experimental import pallas as pl
from jax.experimental.pallas import tpu as pltpu
from jax.sharding import PartitionSpec as P

phonon_occupation = 0.5

VMEM = pl.BlockSpec(memory_space=pltpu.VMEM)
SMEM = pl.BlockSpec(memory_space=pltpu.SMEM)
ANY = pl.BlockSpec(memory_space=pl.ANY)


def shifted(value, axis, steps):
    count = lax.axis_size(axis)
    initial, last = (max(0, -steps), min(count, count - steps))
    return lax.ppermute(value, axis, [(source, source + steps) for source in range(initial, last)])


def params():
    return pltpu.CompilerParams(vmem_limit_bytes=24 * 1024 * 1024)


def product(left, right):
    return jnp.dot(left, right, preferred_element_type=jnp.float32)


def product_t(left, right):
    return lax.dot_general(
        left, right, (((1,), (1,)), ((), ())), preferred_element_type=jnp.float32
    )


def held(shape, dtype):
    return pltpu.VMEM(shape, dtype)


def in_hbm(*arrays):
    return [pltpu.with_memory_space_constraint(array, pltpu.HBM) for array in arrays]


def in_smem(array):
    return pltpu.with_memory_space_constraint(array, pltpu.SMEM)


def load_kernel(edges, *refs):
    inputs, active, shift = refs[:4], refs[4], refs[5]
    outputs, steps, open_mask = refs[6:10], refs[10], refs[11]
    packed, counts, sems = refs[12 : 12 + len(edges)], refs[-2], refs[-1]
    blocks = [ref if ref.ndim == 3 else ref.at[0] for ref in inputs]
    pairs = [(active, counts), (shift, steps)]
    for block_of, target in zip(edges, packed):
        block = block_of()
        pairs += [(ref.at[block], target.at[slot]) for slot, ref in enumerate(blocks)]
    pairs += list(zip(blocks, outputs))
    copies = [
        pltpu.make_async_copy(origin, target, sems.at[index])
        for index, (origin, target) in enumerate(pairs)
    ]
    for copy in copies:
        copy.start()
    for copy in copies:
        copy.wait()
    block_count = open_mask.shape[0]
    open_count = counts[lax.axis_index("energy")] - lax.axis_index("space") * block_count
    block_ids = lax.broadcasted_iota(jnp.int32, open_mask.shape, 0)
    open_mask[...] = (block_ids < open_count).astype(jnp.float32)


def load(edges, arrays, active, shift):
    _, block_count, orbitals, _ = arrays[0].shape
    blocks = held((block_count, orbitals, orbitals), jnp.bfloat16)
    edge = held((len(arrays), orbitals, orbitals), jnp.bfloat16)
    copies = len(arrays) * (1 + len(edges)) + 2
    results = pl.pallas_call(
        functools.partial(load_kernel, edges),
        out_shape=(
            *[blocks] * len(arrays),
            pltpu.SMEM(shift.shape, shift.dtype),
            held((block_count, orbitals), jnp.float32),
            *[edge] * len(edges),
        ),
        in_specs=[ANY] * (len(arrays) + 2),
        out_specs=(*[VMEM] * len(arrays), SMEM, VMEM, *[VMEM] * len(edges)),
        scratch_shapes=[
            pltpu.SMEM(active.shape, active.dtype),
            pltpu.SemaphoreType.DMA((copies,)),
        ],
        compiler_params=params(),
    )(*in_hbm(*arrays, active, shift))
    kept = len(arrays)
    return results[:kept], results[kept], results[kept + 1], results[kept + 2 :]


def through(operator, less, great):
    rows = operator.shape[0]
    half = product(operator, jnp.concatenate([less, great], 1)).astype(jnp.bfloat16)
    stacked = jnp.concatenate([half[:, :rows], half[:, rows:]], 0)
    return product_t(stacked, operator)


def hop_kernel(green, less, great, coupling, source):
    block_count, orbitals = green.shape[0], green.shape[1]
    blocks = range(block_count)
    hops, both = [], []
    for block in blocks:
        factors = []
        if block + 1 < block_count:
            factors.append(coupling[block].T)
        if block > 0:
            factors.append(coupling[block - 1])
        hops.append(product(jnp.concatenate(factors, 0), green[block]).astype(jnp.bfloat16))
    for block in blocks:
        prior = jnp.concatenate([less[block], great[block]], 1)
        both.append(product(hops[block], prior).astype(jnp.bfloat16))
    for block in blocks:
        prior = jnp.concatenate([less[block], great[block]], 0).astype(jnp.float32)
        source[block] = source[block] + prior if block > 0 else prior
        first = 0
        for target in (block + 1, block - 1):
            if 0 <= target < block_count:
                piece = slice(first, first + orbitals)
                half = both[block][piece]
                stacked = jnp.concatenate([half[:, :orbitals], half[:, orbitals:]], 0)
                moved = product_t(stacked, hops[block][piece])
                source[target] = moved if target > block else source[target] + moved
                first += orbitals


def green_kernel(swap, split, green, coupling, source, open_mask, *rest):
    halos, (outgoing, diagonal) = rest[:-2], rest[-2:]
    block_count, orbitals = green.shape[0], green.shape[1]
    place = lax.axis_index("space")
    last = block_count - 1
    added = {}
    if swap:
        (halo,) = halos
        hop = jnp.where(place == 0, coupling[last], halo[3].T)
        edge = through(product(hop, halo[0]).astype(jnp.bfloat16), halo[1], halo[2])
        added = {0: jnp.where(place > 0, edge, 0.0), last: jnp.where(place == 0, edge, 0.0)}
    elif halos:
        before, after = halos
        hop = product(before[3].T, before[0]).astype(jnp.bfloat16)
        added[0] = through(hop, before[1], before[2])
        hop = product(coupling[last], after[0]).astype(jnp.bfloat16)
        added[last] = through(hop, after[1], after[2])
    row_ids = lax.broadcasted_iota(jnp.int32, (orbitals, orbitals), 0)
    column_ids = lax.broadcasted_iota(jnp.int32, (orbitals, orbitals), 1)
    on_diagonal = row_ids == column_ids
    order = [*range(1, last), 0, last]
    halves, kinds = {}, {}
    for block in order:
        middle = source[block]
        if block in added:
            middle = middle + added[block]
        middle = middle.astype(jnp.bfloat16)
        middle = jnp.concatenate([middle[:orbitals], middle[orbitals:]], 1)
        halves[block] = product(green[block], middle).astype(jnp.bfloat16)
    for block in order:
        half = halves[block]
        stacked = jnp.concatenate([half[:, :orbitals], half[:, orbitals:]], 0)
        result = product_t(stacked, green[block]) * open_mask[block : block + 1]
        kinds[block] = [result[:orbitals], result[orbitals:]]
        total = sum(kind.astype(jnp.bfloat16).astype(jnp.float32) for kind in kinds[block])
        diagonal[block : block + 1] = jnp.sum(
            jnp.where(on_diagonal, total, 0.0), axis=0, keepdims=True
        )
        if not split:
            for kind in range(2):
                outgoing[kind, block] = kinds[block][kind].astype(jnp.bfloat16)
    if split:
        devices, _, rows, _ = outgoing.shape
        rows //= block_count
        for block in range(0, block_count, 2):
            for kind in range(2):
                pair = [
                    kinds[block + step][kind].reshape(devices, rows, orbitals) for step in range(2)
                ]
                outgoing[:, kind, block * rows : (block + 2) * rows] = jnp.concatenate(
                    pair, 1
                ).astype(jnp.bfloat16)


def spread(strength, rows):
    return jnp.concatenate([strength] * (rows // strength.shape[0]), 0)


def current_kernel(shift, rows, strength, parts, wide, total):
    energies, _, row_count, orbitals = rows.shape
    block_count = total.shape[1]
    pad = energies // 2
    edge = jnp.zeros((pad, 2, row_count, orbitals), jnp.float32)
    wide[0:pad] = edge
    wide[pad + energies :] = edge
    wide[pad : pad + energies] = rows[...].astype(jnp.float32)
    scale = spread(strength[...] * (1.0 / orbitals), row_count)
    first, second = shift[0], shift[1]

    def step(energy, carry):
        here = energy + pad
        above, below = (
            [wide[here + first, kind] + wide[here + second, kind] for kind in range(2)],
            [wide[here - first, kind] + wide[here - second, kind] for kind in range(2)],
        )
        gain = (1.0 + phonon_occupation) * above[0] + phonon_occupation * below[0]
        loss = (1.0 + phonon_occupation) * below[1] + phonon_occupation * above[1]
        flow = (gain * wide[here, 1] - loss * wide[here, 0]) * scale
        total[energy] = jnp.sum(flow.reshape(block_count, -1, orbitals), axis=1)
        return carry

    lax.fori_loop(0, energies, step, 0, unroll=4)
    summed = total[...].reshape(energies * block_count, orbitals)
    coarse = summed.astype(jnp.bfloat16)
    fine = (summed - coarse.astype(jnp.float32)).astype(jnp.bfloat16)
    ones = jnp.ones((8, 2 * orbitals), jnp.bfloat16)
    flat = product_t(ones, jnp.concatenate([coarse, fine], 1))
    for energy in range(energies):
        parts[energy] = flat[0:1, energy * block_count : (energy + 1) * block_count]


def sigma_kernel(shift, rows, strength, less_out, great_out):
    energies = rows.shape[0]
    factor = spread(strength[...], rows.shape[2])

    def step(energy, carry):
        less_sum, great_sum = 0.0, 0.0
        for branch in range(2):
            above, below = energy + shift[branch], energy - shift[branch]
            has_above = (above < energies).astype(jnp.float32)
            has_below = (below >= 0).astype(jnp.float32)
            above = jnp.minimum(above, energies - 1)
            below = jnp.maximum(below, 0)
            more, fewer = 1.0 + phonon_occupation, phonon_occupation
            less_sum = (
                less_sum
                + (more * has_above) * rows[above, 0].astype(jnp.float32)
                + (fewer * has_below) * rows[below, 0].astype(jnp.float32)
            )
            great_sum = (
                great_sum
                + (more * has_below) * rows[below, 1].astype(jnp.float32)
                + (fewer * has_above) * rows[above, 1].astype(jnp.float32)
            )
        less_out[energy] = (factor * less_sum).astype(less_out.dtype)
        great_out[energy] = (factor * great_sum).astype(great_out.dtype)
        return carry

    lax.fori_loop(0, energies, step, 0)


def local(
    green_ret, prior_less, prior_great, coupling, phonon_coupling, phonon_shift, active_blocks
):
    _, block_count, orbitals, _ = green_ret.shape
    devices, places = lax.axis_size("energy"), lax.axis_size("space")
    row_count = orbitals // devices
    last = block_count - 1
    swap = places == 2
    if swap:
        edges = [lambda: last * (1 - lax.axis_index("space"))]
    elif places > 1:
        edges = [lambda: last, lambda: 0]
    else:
        edges = []
    arrays, shift, open_mask, packed = load(
        edges, (green_ret, prior_less, prior_great, coupling), active_blocks, phonon_shift
    )
    green, less, great, coupling = arrays
    if swap:
        halos = (lax.ppermute(packed[0], "space", [(0, 1), (1, 0)]),)
    else:
        halos = tuple(
            shifted(edge, "space", step) for edge, step in zip(packed, (1, -1), strict=False)
        )
    source = pl.pallas_call(
        hop_kernel,
        out_shape=held((block_count, 2 * orbitals, orbitals), jnp.float32),
        in_specs=[VMEM] * 4,
        out_specs=VMEM,
        compiler_params=params(),
        cost_estimate=pl.CostEstimate(
            flops=20 * block_count * orbitals**3,
            bytes_accessed=8 * block_count * orbitals**2,
            transcendentals=0,
        ),
    )(green, less, great, coupling)
    split = row_count % 8 == 0 and block_count % 2 == 0
    if split:
        out_shape = (devices, 2, block_count * row_count, orbitals)
    else:
        out_shape = (2, block_count, orbitals, orbitals)
    outgoing, diagonal = pl.pallas_call(
        functools.partial(green_kernel, swap, split),
        out_shape=(
            held(out_shape, jnp.bfloat16),
            jax.ShapeDtypeStruct((block_count, orbitals), jnp.float32),
        ),
        in_specs=[VMEM] * (4 + len(halos)),
        out_specs=(VMEM, VMEM),
        compiler_params=params(),
    )(green, coupling, source, open_mask, *halos)
    if not split:
        outgoing = outgoing.reshape(2, block_count, devices, row_count, orbitals)
        outgoing = jnp.transpose(outgoing, (2, 0, 1, 3, 4))
        outgoing = outgoing.reshape(devices, 2, block_count * row_count, orbitals)
    ldos = jnp.sum(diagonal, axis=1)[None, :] / orbitals
    rows = lax.all_to_all(outgoing, "energy", split_axis=0, concat_axis=0, tiled=True)
    parts = pl.pallas_call(
        current_kernel,
        out_shape=held((devices, 1, block_count), jnp.float32),
        in_specs=[SMEM, VMEM, VMEM],
        out_specs=VMEM,
        scratch_shapes=[
            pltpu.VMEM((2 * devices, *rows.shape[1:]), jnp.float32),
            pltpu.VMEM((devices, block_count, orbitals), jnp.float32),
        ],
        compiler_params=params(),
    )(in_smem(shift), rows, phonon_coupling)
    parts = lax.all_to_all(parts, "energy", split_axis=0, concat_axis=0, tiled=True)
    out = jax.ShapeDtypeStruct((devices, block_count * row_count, orbitals), jnp.bfloat16)
    sigmas = pl.pallas_call(
        sigma_kernel,
        out_shape=(out, out),
        in_specs=[SMEM, VMEM, VMEM],
        out_specs=(VMEM, VMEM),
        compiler_params=params(),
        cost_estimate=pl.CostEstimate(
            flops=20 * rows.size, bytes_accessed=4 * rows.size, transcendentals=0
        ),
    )(in_smem(shift), rows, phonon_coupling)
    sigma_l, sigma_g = [
        sigma.reshape(devices, block_count, row_count, orbitals) for sigma in sigmas
    ]
    current = jnp.sum(parts, axis=0)
    return (sigma_l, sigma_g, current, ldos)


def solution(mesh):
    return jax.shard_map(
        local,
        mesh=mesh,
        in_specs=(
            P("energy", "space", None, None),
            P("energy", "space", None, None),
            P("energy", "space", None, None),
            P("space", None, None),
            P("energy", None),
            P(),
            P(),
        ),
        out_specs=(
            P(None, "space", "energy", None),
            P(None, "space", "energy", None),
            P("energy", "space"),
            P("energy", "space"),
        ),
        check_vma=False,
    )
```

time: 47.9 us -> 42.2 us (0.88)
  local copies, waits for them, and re-layouts: 3.81 us -> 0.01 us
  Pallas kernels: 8.09 us -> 6.62 us
    unnamed x14 -> x2, local copies, waits for them, and re-layouts: 3.81 us -> 0.01 us
    pallas_call x3 -> x4, Pallas kernels: 6.12 us -> 5.2 us  [the longest x1 1.62 us: local(): pl.pallas_call(functools.partial(green_kernel, swap, split), out_shape=(h...]
    ppermute x1, waiting for transfers between devices: 0.99 us -> 0.15 us  [local(): halos = (lax.ppermute(packed[0], 'space', [(0, 1), (1, 0)]),)]
    all_to_all x1, waiting for transfers between devices: 4.78 us -> 5.33 us  [local(): lax.all_to_all(parts, 'energy', split_axis=0, concat_axis=0, tiled=True)]
    pallas_call x1, Pallas kernels: 1.97 us -> 1.42 us  [local(): pl.pallas_call(sigma_kernel, out_shape=(out, out), in_specs=[SMEM, VMEM,...]
  transfers between devices with their start and end apart: 3 -> 3, of which waited for: 3 -> 3; matrix products, arithmetic and copies ran while one was open for 1% -> 2% of each run, Pallas kernels for 4% -> 5%
where the time goes in v4:
time: 42.2 us; the launch traced here: 41.9 us
  waiting for transfers between devices  20.8 us (49%)
  starting transfers between devices  12.7 us (30%)
  Pallas kernels  6.62 us (16%)
  other arithmetic  1.17 us (3%)
  between operations  0.68 us (2%)
    all_to_all x1, waiting for transfers between devices, local(): lax.all_to_all(outgoing, 'energy', split_axis=0, concat_axis=0, tiled=True)  15.3 us
    all_to_all x1, starting transfers between devices, local(): lax.all_to_all(outgoing, 'energy', split_axis=0, concat_axis=0, tiled=True)  8.22 us
    all_to_all x1, waiting for transfers between devices, local(): lax.all_to_all(parts, 'energy', split_axis=0, concat_axis=0, tiled=True)  5.33 us
    all_to_all x1, starting transfers between devices, local(): lax.all_to_all(parts, 'energy', split_axis=0, concat_axis=0, tiled=True)  3.94 us
    pallas_call x1, Pallas kernels, local(): pl.pallas_call(functools.partial(green_kernel, swap, split), out_shape=(h...  1.62 us
    pallas_call x1, Pallas kernels, local(): pl.pallas_call(sigma_kernel, out_shape=(out, out), in_specs=[SMEM, VMEM,...  1.42 us
    pallas_call x1, Pallas kernels, local(): pl.pallas_call(current_kernel, out_shape=held((devices, 1, block_count),...  1.38 us
    pallas_call x1, Pallas kernels, load(): pl.pallas_call(functools.partial(load_kernel, edges), out_shape=(*[blocks...  1.37 us
  transfers between devices with their start and end apart: 3, of which 3 were waited for; matrix products, arithmetic and copies ran while one was open for 2% of the time, Pallas kernels for 5%

profile of v4, /device:TPU:0, one launch (start us, length us, event | category | flops | bytes accessed | tf_op | source)
XLA Modules:
  0.0 41.9 jit_solution(7606354833133362209)
XLA Ops:
  0.6 1.4 %shard_map.102 = (bf16[8,128,128]{2,1,0:T(8,128)(2,1)S(1)}, bf16[8,128,128]{2,1,0:T(8,128)(2,1)S(1)}, bf16[8,128,128]{2,1,0:T(8,128)(2,1)S(1)}, bf16[8,128,128]{...) custom-call(bf16[1,8,128,128]{3,2,1,0:T(8,128)(2,1)} %refs_0_.1, ...), custom_call_target="tpu_custom_call" | custom-call | tf_op jit(solution)/shard_map/pallas_call | solution.py:78
  2.0 0.5 %collective-permute-start = (bf16[4,128,128]{2,1,0:T(8,128)(2,1)S(1)}, bf16[4,128,128]{2,1,0:T(8,128)(2,1)S(1)}, u32[]{:S(2)}, u32[]{:S(2)}) collective-permute-start(bf16[4,128,128]{2,1,0:T(8,128)(2,1)S(1)} %get-tuple-element.21), channel_id=1, source_target_pairs={{0,1},{1,0},{2,3},{3,2},{4,5},{5,4},{6,7},{7,6},{8,9},{9,8},{10,11... | collective-permute-start | bytes 393224 | tf_op jit(solution)/shard_map/ppermute | solution.py:273
  2.5 0.8 %shard_map.103.source = f32[8,256,128]{2,1,0:T(8,128)S(1)} custom-call(bf16[8,128,128]{2,1,0:T(8,128)(2,1)S(1)} %get-tuple-element.16.green, bf16[8,128,128]{2,1,0:T(8,128)(2,1)S(1)} %get-tuple-element.18.less, bf16[8,128,128]{2,1,0:T(8,128)(2,1)S(1)} %get-tuple-element.19.great, bf16[8,128,128]{2,1,0:T(8,128)(2,1)S(1)} %get-tuple-element.17.coupling), custom_call_target="tpu_custom_call" | custom-call | flops 335544320 | bytes 1048576 | tf_op jit(solution)/shard_map/pallas_call | solution.py:278
  3.4 0.1 collective-permute-done.rest_0_
  3.5 1.6 %shard_map.104 = (bf16[16,2,64,128]{3,2,1,0:T(8,128)(2,1)}, f32[8,128]{1,0:T(8,128)S(1)}) custom-call(bf16[8,128,128]{2,1,0:T(8,128)(2,1)S(1)} %get-tuple-element.16.green, bf16[8,128,128]{2,1,0:T(8,128)(2,1)S(1)} %get-tuple-element.17.coupling, f32[8,256,128]{2,1,0:T(8,128)S(1)} %shard_map.103.source, f32[8,128]{1,0:T(8,128)S(1)} %get-tuple-element.20.open_mask, ...), custom_call_target="tpu_custom_call" | custom-call | tf_op jit(solution)/shard_map/pallas_call | solution.py:295
  5.1 8.2 %all-to-all-start = ((bf16[16,2,64,128]{3,2,1,0:T(8,128)(2,1)}), bf16[16,2,64,128]{3,2,1,0:T(8,128)(2,1)S(1)}, u32[]{:S(2)}, u32[]{:S(2)}) async-start(bf16[16,2,64,128]{3,2,1,0:T(8,128)(2,1)} %get-tuple-element.22), calls=%async_computation | async-start | bytes 1048576 | tf_op jit(solution)/shard_map/all_to_all | solution.py:310
  13.4 0.0 copy-start
  13.4 0.1 reduce_sum.22
  13.5 15.3 %all-to-all-done.rows = bf16[16,2,64,128]{3,2,1,0:T(8,128)(2,1)S(1)} async-done(((bf16[16,2,64,128]{3,2,1,0:T(8,128)(2,1)}), bf16[16,2,64,128]{3,2,1,0:T(8,128)(2,1)S(1)}, u32[]{:S(2)}, u32[]{:S(2)}) %all-to-all-start) | async-done | bytes 524320 | tf_op jit(solution)/shard_map/all_to_all | solution.py:310
  28.8 0.0 copy-done
  28.8 1.4 %shard_map.106 = f32[16,1,8]{2,1,0:T(1,128)} custom-call(s32[2]{0:T(128)S(4)} %get-tuple-element.15.shift, bf16[16,2,64,128]{3,2,1,0:T(8,128)(2,1)S(1)} %all-to-all-done.rows, f32[8,128]{1,0:T(8,128)S(1)} %copy-done), custom_call_target="tpu_custom_call" | custom-call | tf_op jit(solution)/shard_map/pallas_call | solution.py:311
  30.1 3.9 %all-to-all-start.1 = ((f32[16,1,8]{2,1,0:T(1,128)}), f32[16,1,8]{2,1,0:T(1,128)S(1)}, u32[]{:S(2)}, u32[]{:S(2)}) async-start(f32[16,1,8]{2,1,0:T(1,128)} %shard_map.106), calls=%async_computation.1 | async-start | bytes 16384 | tf_op jit(solution)/shard_map/all_to_all | solution.py:322
  34.1 0.5 %multiply_bitcast_fusion = f32[1,8]{1,0:T(1,128)} fusion(f32[8]{0:T(128)S(1)} %reduce_sum.22), kind=kLoop, calls=%fused_computation | loop fusion | flops 8 | bytes 64 | tf_op jit(solution)/shard_map/div | solution.py:309
  34.6 1.4 %shard_map.105 = (bf16[16,64,128]{2,1,0:T(8,128)(2,1)}, bf16[16,64,128]{2,1,0:T(8,128)(2,1)}) custom-call(s32[2]{0:T(128)S(4)} %get-tuple-element.15.shift, bf16[16,2,64,128]{3,2,1,0:T(8,128)(2,1)S(1)} %all-to-all-done.rows, f32[8,128]{1,0:T(8,128)S(1)} %copy-done), custom_call_target="tpu_custom_call" | custom-call | flops 5242880 | bytes 1048576 | tf_op jit(solution)/shard_map/pallas_call | solution.py:324
  36.0 5.3 %all-to-all-done.1 = f32[16,1,8]{2,1,0:T(1,128)S(1)} async-done(((f32[16,1,8]{2,1,0:T(1,128)}), f32[16,1,8]{2,1,0:T(1,128)S(1)}, u32[]{:S(2)}, u32[]{:S(2)}) %all-to-all-start.1) | async-done | bytes 544 | tf_op jit(solution)/shard_map/all_to_all | solution.py:322
  41.4 0.5 %reduce_sum.20 = f32[8]{0:T(128)} reduce(f32[16,1,8]{2,1,0:T(1,128)S(1)} %all-to-all-done.1, f32[]{:T(128)} %constant.1.clone.1), dimensions={0,1}, to_apply=%region_0.0 | reduce | flops 120 | bytes 548 | tf_op jit(solution)/shard_map/reduce_sum | solution.py:337
Async XLA Ops:
  2.0 1.5 %collective-permute-start = (bf16[4,128,128]{2,1,0:T(8,128)(2,1)S(1)}, bf16[4,128,128]{2,1,0:T(8,128)(2,1)S(1)}, u32[]{:S(2)}, u32[]{:S(2)}) collective-permute-start(bf16[4,128,128]{2,1,0:T(8,128)(2,1)S(1)} %get-tuple-element.21), channel_id=1, source_target_pairs={{0,1},{1,0},{2,3},{3,2},{4,5},{5,4},{6,7},{7,6},{8,9},{9,8},{10,11... | collective-permute-start | bytes 393224 | tf_op jit(solution)/shard_map/ppermute | solution.py:273
  5.1 23.6 %all-to-all-start = ((bf16[16,2,64,128]{3,2,1,0:T(8,128)(2,1)}), bf16[16,2,64,128]{3,2,1,0:T(8,128)(2,1)S(1)}, u32[]{:S(2)}, u32[]{:S(2)}) async-start(bf16[16,2,64,128]{3,2,1,0:T(8,128)(2,1)} %get-tuple-element.22), calls=%async_computation | async-start | bytes 1048576 | tf_op jit(solution)/shard_map/all_to_all | solution.py:310
  13.4 15.4 %copy-start = (f32[8,128]{1,0:T(8,128)S(1)}, f32[8,128]{1,0:T(8,128)}, u32[]{:S(2)}) copy-start(f32[8,128]{1,0:T(8,128)} %strength.3) | copy-start | bytes 12292
  30.1 11.2 %all-to-all-start.1 = ((f32[16,1,8]{2,1,0:T(1,128)}), f32[16,1,8]{2,1,0:T(1,128)S(1)}, u32[]{:S(2)}, u32[]{:S(2)}) async-start(f32[16,1,8]{2,1,0:T(1,128)} %shard_map.106), calls=%async_computation.1 | async-start | bytes 16384 | tf_op jit(solution)/shard_map/all_to_all | solution.py:322

commit v5 on v4

--- a/solution.py
+++ b/solution.py
@@ -18,6 +18,27 @@
     count = lax.axis_size(axis)
     initial, last = (max(0, -steps), min(count, count - steps))
     return lax.ppermute(value, axis, [(source, source + steps) for source in range(initial, last)])
+
+
+def place_of(index):
+    return index // 4, index // 2 % 2, index % 2
+
+
+def near(count, root):
+    def key(index):
+        return sum(abs(a - b) for a, b in zip(place_of(root), place_of(index))), index
+
+    return sorted(range(count), key=key)
+
+
+def orders(count):
+    return near(count, 9 * count // 16), near(count, count - 1)
+
+
+def exchange(chunks, order):
+    return lax.all_to_all(
+        chunks, "energy", split_axis=0, concat_axis=0, tiled=True, axis_index_groups=[order]
+    )
 
 
 def params():
@@ -130,7 +151,7 @@
                 first += orbitals
 
 
-def green_kernel(swap, split, green, coupling, source, open_mask, *rest):
+def green_kernel(swap, split, order, green, coupling, source, open_mask, *rest):
     halos, (outgoing, diagonal) = rest[:-2], rest[-2:]
     block_count, orbitals = green.shape[0], green.shape[1]
     place = lax.axis_index("space")
@@ -150,16 +171,16 @@
     row_ids = lax.broadcasted_iota(jnp.int32, (orbitals, orbitals), 0)
     column_ids = lax.broadcasted_iota(jnp.int32, (orbitals, orbitals), 1)
     on_diagonal = row_ids == column_ids
-    order = [*range(1, last), 0, last]
+    sequence = [*range(1, last), 0, last]
     halves, kinds = {}, {}
-    for block in order:
+    for block in sequence:
         middle = source[block]
         if block in added:
             middle = middle + added[block]
         middle = middle.astype(jnp.bfloat16)
         middle = jnp.concatenate([middle[:orbitals], middle[orbitals:]], 1)
         halves[block] = product(green[block], middle).astype(jnp.bfloat16)
-    for block in order:
+    for block in sequence:
         half = halves[block]
         stacked = jnp.concatenate([half[:, :orbitals], half[:, orbitals:]], 0)
         result = product_t(stacked, green[block]) * open_mask[block : block + 1]
@@ -176,26 +197,27 @@
         rows //= block_count
         for block in range(0, block_count, 2):
             for kind in range(2):
-                pair = [
-                    kinds[block + step][kind].reshape(devices, rows, orbitals) for step in range(2)
-                ]
-                outgoing[:, kind, block * rows : (block + 2) * rows] = jnp.concatenate(
-                    pair, 1
-                ).astype(jnp.bfloat16)
+                for spot, device in enumerate(order):
+                    piece = slice(device * rows, (device + 1) * rows)
+                    pair = [kinds[block + step][kind][piece] for step in range(2)]
+                    outgoing[spot, kind, block * rows : (block + 2) * rows] = jnp.concatenate(
+                        pair, 0
+                    ).astype(jnp.bfloat16)
 
 
 def spread(strength, rows):
     return jnp.concatenate([strength] * (rows // strength.shape[0]), 0)
 
 
-def current_kernel(shift, rows, strength, parts, wide, total):
+def current_kernel(order, back_order, shift, rows, strength, parts, wide, total):
     energies, _, row_count, orbitals = rows.shape
     block_count = total.shape[1]
     pad = energies // 2
     edge = jnp.zeros((pad, 2, row_count, orbitals), jnp.float32)
     wide[0:pad] = edge
     wide[pad + energies :] = edge
-    wide[pad : pad + energies] = rows[...].astype(jnp.float32)
+    for spot, energy in enumerate(order):
+        wide[pad + energy] = rows[spot].astype(jnp.float32)
     scale = spread(strength[...] * (1.0 / orbitals), row_count)
     first, second = shift[0], shift[1]
 
@@ -217,12 +239,14 @@
     fine = (summed - coarse.astype(jnp.float32)).astype(jnp.bfloat16)
     ones = jnp.ones((8, 2 * orbitals), jnp.bfloat16)
     flat = product_t(ones, jnp.concatenate([coarse, fine], 1))
-    for energy in range(energies):
-        parts[energy] = flat[0:1, energy * block_count : (energy + 1) * block_count]
-
-
-def sigma_kernel(shift, rows, strength, less_out, great_out):
+    for spot, energy in enumerate(back_order):
+        parts[spot] = flat[0:1, energy * block_count : (energy + 1) * block_count]
+
+
+def sigma_kernel(order, shift, arrived, strength, less_out, great_out, rows):
     energies = rows.shape[0]
+    for spot, energy in enumerate(order):
+        rows[energy] = arrived[spot]
     factor = spread(strength[...], rows.shape[2])
 
     def step(energy, carry):
@@ -258,6 +282,7 @@
     devices, places = lax.axis_size("energy"), lax.axis_size("space")
     row_count = orbitals // devices
     last = block_count - 1
+    order, back_order = orders(devices)
     swap = places == 2
     if swap:
         edges = [lambda: last * (1 - lax.axis_index("space"))]
@@ -293,7 +318,7 @@
     else:
         out_shape = (2, block_count, orbitals, orbitals)
     outgoing, diagonal = pl.pallas_call(
-        functools.partial(green_kernel, swap, split),
+        functools.partial(green_kernel, swap, split, order),
         out_shape=(
             held(out_shape, jnp.bfloat16),
             jax.ShapeDtypeStruct((block_count, orbitals), jnp.float32),
@@ -304,12 +329,12 @@
     )(green, coupling, source, open_mask, *halos)
     if not split:
         outgoing = outgoing.reshape(2, block_count, devices, row_count, orbitals)
-        outgoing = jnp.transpose(outgoing, (2, 0, 1, 3, 4))
+        outgoing = jnp.stack([outgoing[:, :, device] for device in order])
         outgoing = outgoing.reshape(devices, 2, block_count * row_count, orbitals)
     ldos = jnp.sum(diagonal, axis=1)[None, :] / orbitals
-    rows = lax.all_to_all(outgoing, "energy", split_axis=0, concat_axis=0, tiled=True)
+    rows = exchange(outgoing, order)
     parts = pl.pallas_call(
-        current_kernel,
+        functools.partial(current_kernel, order, back_order),
         out_shape=held((devices, 1, block_count), jnp.float32),
         in_specs=[SMEM, VMEM, VMEM],
         out_specs=VMEM,
@@ -319,13 +344,14 @@
         ],
         compiler_params=params(),
     )(in_smem(shift), rows, phonon_coupling)
-    parts = lax.all_to_all(parts, "energy", split_axis=0, concat_axis=0, tiled=True)
+    parts = exchange(parts, back_order)
     out = jax.ShapeDtypeStruct((devices, block_count * row_count, orbitals), jnp.bfloat16)
     sigmas = pl.pallas_call(
-        sigma_kernel,
+        functools.partial(sigma_kernel, order),
         out_shape=(out, out),
         in_specs=[SMEM, VMEM, VMEM],
         out_specs=(VMEM, VMEM),
+        scratch_shapes=[pltpu.VMEM(rows.shape, rows.dtype)],
         compiler_params=params(),
         cost_estimate=pl.CostEstimate(
             flops=20 * rows.size, bytes_accessed=4 * rows.size, transcendentals=0

time: 42.2 us -> 38.3 us (0.908)
  waiting for transfers between devices: 20.8 us -> 11.8 us
  starting transfers between devices: 12.7 us -> 17.7 us
    all_to_all x2, waiting for transfers between devices: 20.6 us -> 11.7 us  [exchange(): lax.all_to_all(chunks, 'energy', split_axis=0, concat_axis=0, tiled=True,...]
    all_to_all x2, starting transfers between devices: 12.2 us -> 17.2 us  [exchange(): lax.all_to_all(chunks, 'energy', split_axis=0, concat_axis=0, tiled=True,...]
  transfers between devices with their start and end apart: 3 -> 3, of which waited for: 3 -> 3; matrix products, arithmetic and copies ran while one was open for 2% -> 2% of each run, Pallas kernels for 5% -> 6%
where the time goes in v5:
time: 38.3 us; the launch traced here: 38 us
  starting transfers between devices  17.7 us (46%)
  waiting for transfers between devices  11.8 us (31%)
  Pallas kernels  6.66 us (17%)
  other arithmetic  1.17 us (3%)
  between operations  0.66 us (2%)
    all_to_all x2, starting transfers between devices, exchange(): lax.all_to_all(chunks, 'energy', split_axis=0, concat_axis=0, tiled=True,...  17.2 us
    all_to_all x2, waiting for transfers between devices, exchange(): lax.all_to_all(chunks, 'energy', split_axis=0, concat_axis=0, tiled=True,...  11.7 us
    pallas_call x1, Pallas kernels, local(): pl.pallas_call(functools.partial(green_kernel, swap, split, order), out_s...  1.62 us
    pallas_call x1, Pallas kernels, local(): pl.pallas_call(functools.partial(sigma_kernel, order), out_shape=(out, ou...  1.46 us
    pallas_call x1, Pallas kernels, local(): pl.pallas_call(functools.partial(current_kernel, order, back_order), out_...  1.38 us
    pallas_call x1, Pallas kernels, load(): pl.pallas_call(functools.partial(load_kernel, edges), out_shape=(*[blocks...  1.37 us
    pallas_call x1, Pallas kernels, local(): pl.pallas_call(hop_kernel, out_shape=held((block_count, 2 * orbitals, orb...  0.83 us
  transfers between devices with their start and end apart: 3, of which 3 were waited for; matrix products, arithmetic and copies ran while one was open for 2% of the time, Pallas kernels for 6%

profile of v5, /device:TPU:0, one launch (start us, length us, event | category | flops | bytes accessed | tf_op | source)
XLA Modules:
  0.0 38.0 jit_solution(926353041289629411)
XLA Ops:
  0.6 1.4 %shard_map.102 = (bf16[8,128,128]{2,1,0:T(8,128)(2,1)S(1)}, bf16[8,128,128]{2,1,0:T(8,128)(2,1)S(1)}, bf16[8,128,128]{2,1,0:T(8,128)(2,1)S(1)}, bf16[8,128,128]{...) custom-call(bf16[1,8,128,128]{3,2,1,0:T(8,128)(2,1)} %refs_0_.1, ...), custom_call_target="tpu_custom_call" | custom-call | tf_op jit(solution)/shard_map/pallas_call | solution.py:99
  2.0 0.5 %collective-permute-start = (bf16[4,128,128]{2,1,0:T(8,128)(2,1)S(1)}, bf16[4,128,128]{2,1,0:T(8,128)(2,1)S(1)}, u32[]{:S(2)}, u32[]{:S(2)}) collective-permute-start(bf16[4,128,128]{2,1,0:T(8,128)(2,1)S(1)} %get-tuple-element.21), channel_id=1, source_target_pairs={{0,1},{1,0},{2,3},{3,2},{4,5},{5,4},{6,7},{7,6},{8,9},{9,8},{10,11... | collective-permute-start | bytes 393224 | tf_op jit(solution)/shard_map/ppermute | solution.py:298
  2.5 0.8 %shard_map.103.source = f32[8,256,128]{2,1,0:T(8,128)S(1)} custom-call(bf16[8,128,128]{2,1,0:T(8,128)(2,1)S(1)} %get-tuple-element.16.green, bf16[8,128,128]{2,1,0:T(8,128)(2,1)S(1)} %get-tuple-element.18.less, bf16[8,128,128]{2,1,0:T(8,128)(2,1)S(1)} %get-tuple-element.19.great, bf16[8,128,128]{2,1,0:T(8,128)(2,1)S(1)} %get-tuple-element.17.coupling), custom_call_target="tpu_custom_call" | custom-call | flops 335544320 | bytes 1048576 | tf_op jit(solution)/shard_map/pallas_call | solution.py:303
  3.4 0.1 collective-permute-done.rest_0_
  3.5 1.6 %shard_map.104 = (bf16[16,2,64,128]{3,2,1,0:T(8,128)(2,1)}, f32[8,128]{1,0:T(8,128)S(1)}) custom-call(bf16[8,128,128]{2,1,0:T(8,128)(2,1)S(1)} %get-tuple-element.16.green, bf16[8,128,128]{2,1,0:T(8,128)(2,1)S(1)} %get-tuple-element.17.coupling, f32[8,256,128]{2,1,0:T(8,128)S(1)} %shard_map.103.source, f32[8,128]{1,0:T(8,128)S(1)} %get-tuple-element.20.open_mask, ...), custom_call_target="tpu_custom_call" | custom-call | tf_op jit(solution)/shard_map/pallas_call | solution.py:320
  5.1 8.7 %all-to-all-start = ((bf16[16,2,64,128]{3,2,1,0:T(8,128)(2,1)}), bf16[16,2,64,128]{3,2,1,0:T(8,128)(2,1)S(1)}, u32[]{:S(2)}, u32[]{:S(2)}) async-start(bf16[16,2,64,128]{3,2,1,0:T(8,128)(2,1)} %get-tuple-element.22), calls=%async_computation | async-start | bytes 1048576 | tf_op jit(solution)/shard_map/all_to_all | solution.py:39
  13.8 0.0 copy-start
  13.8 0.1 reduce_sum.22
  13.9 11.3 %all-to-all-done.arrived.rows = bf16[16,2,64,128]{3,2,1,0:T(8,128)(2,1)S(1)} async-done(((bf16[16,2,64,128]{3,2,1,0:T(8,128)(2,1)}), bf16[16,2,64,128]{3,2,1,0:T(8,128)(2,1)S(1)}, u32[]{:S(2)}, u32[]{:S(2)}) %all-to-all-start) | async-done | bytes 524320 | tf_op jit(solution)/shard_map/all_to_all | solution.py:39
  25.3 0.0 copy-done
  25.3 1.4 %shard_map.106 = f32[16,1,8]{2,1,0:T(1,128)} custom-call(s32[2]{0:T(128)S(4)} %get-tuple-element.15.shift, bf16[16,2,64,128]{3,2,1,0:T(8,128)(2,1)S(1)} %all-to-all-done.arrived.rows, f32[8,128]{1,0:T(8,128)S(1)} %copy-done), custom_call_target="tpu_custom_call" | custom-call | tf_op jit(solution)/shard_map/pallas_call | solution.py:336
  26.7 8.5 %all-to-all-start.1 = ((f32[16,1,8]{2,1,0:T(1,128)}), f32[16,1,8]{2,1,0:T(1,128)S(1)}, u32[]{:S(2)}, u32[]{:S(2)}) async-start(f32[16,1,8]{2,1,0:T(1,128)} %shard_map.106), calls=%async_computation.1 | async-start | bytes 16384 | tf_op jit(solution)/shard_map/all_to_all | solution.py:39
  35.1 0.5 %multiply_bitcast_fusion = f32[1,8]{1,0:T(1,128)} fusion(f32[8]{0:T(128)S(1)} %reduce_sum.22), kind=kLoop, calls=%fused_computation | loop fusion | flops 8 | bytes 64 | tf_op jit(solution)/shard_map/div | solution.py:334
  35.7 1.5 %shard_map.105 = (bf16[16,64,128]{2,1,0:T(8,128)(2,1)}, bf16[16,64,128]{2,1,0:T(8,128)(2,1)}) custom-call(s32[2]{0:T(128)S(4)} %get-tuple-element.15.shift, bf16[16,2,64,128]{3,2,1,0:T(8,128)(2,1)S(1)} %all-to-all-done.arrived.rows, f32[8,128]{1,0:T(8,128)S(1)} %copy-done), custom_call_target="tpu_custom_call" | custom-call | flops 5242880 | bytes 1048576 | tf_op jit(solution)/shard_map/pallas_call | solution.py:349
  37.1 0.3 all-to-all-done.1
  37.5 0.5 %reduce_sum.20 = f32[8]{0:T(128)} reduce(f32[16,1,8]{2,1,0:T(1,128)S(1)} %all-to-all-done.1, f32[]{:T(128)} %constant.1.clone.1), dimensions={0,1}, to_apply=%region_0.0 | reduce | flops 120 | bytes 548 | tf_op jit(solution)/shard_map/reduce_sum | solution.py:363
Async XLA Ops:
  2.0 1.5 %collective-permute-start = (bf16[4,128,128]{2,1,0:T(8,128)(2,1)S(1)}, bf16[4,128,128]{2,1,0:T(8,128)(2,1)S(1)}, u32[]{:S(2)}, u32[]{:S(2)}) collective-permute-start(bf16[4,128,128]{2,1,0:T(8,128)(2,1)S(1)} %get-tuple-element.21), channel_id=1, source_target_pairs={{0,1},{1,0},{2,3},{3,2},{4,5},{5,4},{6,7},{7,6},{8,9},{9,8},{10,11... | collective-permute-start | bytes 393224 | tf_op jit(solution)/shard_map/ppermute | solution.py:298
  5.1 20.2 %all-to-all-start = ((bf16[16,2,64,128]{3,2,1,0:T(8,128)(2,1)}), bf16[16,2,64,128]{3,2,1,0:T(8,128)(2,1)S(1)}, u32[]{:S(2)}, u32[]{:S(2)}) async-start(bf16[16,2,64,128]{3,2,1,0:T(8,128)(2,1)} %get-tuple-element.22), calls=%async_computation | async-start | bytes 1048576 | tf_op jit(solution)/shard_map/all_to_all | solution.py:39
  13.8 11.5 %copy-start = (f32[8,128]{1,0:T(8,128)S(1)}, f32[8,128]{1,0:T(8,128)}, u32[]{:S(2)}) copy-start(f32[8,128]{1,0:T(8,128)} %strength.3) | copy-start | bytes 12292
  26.7 10.8 %all-to-all-start.1 = ((f32[16,1,8]{2,1,0:T(1,128)}), f32[16,1,8]{2,1,0:T(1,128)S(1)}, u32[]{:S(2)}, u32[]{:S(2)}) async-start(f32[16,1,8]{2,1,0:T(1,128)} %shard_map.106), calls=%async_computation.1 | async-start | bytes 16384 | tf_op jit(solution)/shard_map/all_to_all | solution.py:39

commit v6 on v5

v6 whole, which is shorter than its diff:
```python
import functools

import jax
import jax.numpy as jnp
from jax import lax
from jax.experimental import pallas as pl
from jax.experimental.pallas import tpu as pltpu
from jax.sharding import PartitionSpec as P

phonon_occupation = 0.5

VMEM = pl.BlockSpec(memory_space=pltpu.VMEM)
SMEM = pl.BlockSpec(memory_space=pltpu.SMEM)
ANY = pl.BlockSpec(memory_space=pl.ANY)


def shifted(value, axis, steps):
    count = lax.axis_size(axis)
    initial, last = (max(0, -steps), min(count, count - steps))
    return lax.ppermute(value, axis, [(source, source + steps) for source in range(initial, last)])


def orders(count):
    def starting(root):
        return [root] + [index for index in range(count) if index != root]

    return starting(9 * count // 16), starting(count - 1)


def exchange(chunks, order):
    return lax.all_to_all(
        chunks, "energy", split_axis=0, concat_axis=0, tiled=True, axis_index_groups=[order]
    )


def params():
    return pltpu.CompilerParams(vmem_limit_bytes=24 * 1024 * 1024)


def product(left, right):
    return jnp.dot(left, right, preferred_element_type=jnp.float32)


def product_t(left, right):
    return lax.dot_general(
        left, right, (((1,), (1,)), ((), ())), preferred_element_type=jnp.float32
    )


def held(shape, dtype):
    return pltpu.VMEM(shape, dtype)


def in_hbm(*arrays):
    return [pltpu.with_memory_space_constraint(array, pltpu.HBM) for array in arrays]


def in_smem(array):
    return pltpu.with_memory_space_constraint(array, pltpu.SMEM)


def load_kernel(edges, *refs):
    inputs, active, shift = refs[:4], refs[4], refs[5]
    outputs, steps, open_mask = refs[6:10], refs[10], refs[11]
    packed, counts, sems = refs[12 : 12 + len(edges)], refs[-2], refs[-1]
    blocks = [ref if ref.ndim == 3 else ref.at[0] for ref in inputs]
    pairs = [(active, counts), (shift, steps)]
    for block_of, target in zip(edges, packed):
        block = block_of()
        pairs += [(ref.at[block], target.at[slot]) for slot, ref in enumerate(blocks)]
    pairs += list(zip(blocks, outputs))
    copies = [
        pltpu.make_async_copy(origin, target, sems.at[index])
        for index, (origin, target) in enumerate(pairs)
    ]
    for copy in copies:
        copy.start()
    for copy in copies:
        copy.wait()
    block_count = open_mask.shape[0]
    open_count = counts[lax.axis_index("energy")] - lax.axis_index("space") * block_count
    block_ids = lax.broadcasted_iota(jnp.int32, open_mask.shape, 0)
    open_mask[...] = (block_ids < open_count).astype(jnp.float32)


def load(edges, arrays, active, shift):
    _, block_count, orbitals, _ = arrays[0].shape
    blocks = held((block_count, orbitals, orbitals), jnp.bfloat16)
    edge = held((len(arrays), orbitals, orbitals), jnp.bfloat16)
    copies = len(arrays) * (1 + len(edges)) + 2
    results = pl.pallas_call(
        functools.partial(load_kernel, edges),
        out_shape=(
            *[blocks] * len(arrays),
            pltpu.SMEM(shift.shape, shift.dtype),
            held((block_count, orbitals), jnp.float32),
            *[edge] * len(edges),
        ),
        in_specs=[ANY] * (len(arrays) + 2),
        out_specs=(*[VMEM] * len(arrays), SMEM, VMEM, *[VMEM] * len(edges)),
        scratch_shapes=[
            pltpu.SMEM(active.shape, active.dtype),
            pltpu.SemaphoreType.DMA((copies,)),
        ],
        compiler_params=params(),
    )(*in_hbm(*arrays, active, shift))
    kept = len(arrays)
    return results[:kept], results[kept], results[kept + 1], results[kept + 2 :]


def through(operator, less, great):
    rows = operator.shape[0]
    half = product(operator, jnp.concatenate([less, great], 1)).astype(jnp.bfloat16)
    stacked = jnp.concatenate([half[:, :rows], half[:, rows:]], 0)
    return product_t(stacked, operator)


def finish(blocks, middles, green, open_mask, outgoing, order):
    orbitals = green.shape[1]
    halves, kinds = {}, {}
    for block in blocks:
        middle = middles[block].astype(jnp.bfloat16)
        middle = jnp.concatenate([middle[:orbitals], middle[orbitals:]], 1)
        halves[block] = product(green[block], middle).astype(jnp.bfloat16)
    for block in blocks:
        half = halves[block]
        stacked = jnp.concatenate([half[:, :orbitals], half[:, orbitals:]], 0)
        result = product_t(stacked, green[block]) * open_mask[block : block + 1]
        kinds[block] = [result[:orbitals], result[orbitals:]]
    for block in blocks:
        for kind in range(2):
            if order is None:
                outgoing[kind, block] = kinds[block][kind].astype(jnp.bfloat16)
            elif block % 2 == 0:
                rows = orbitals // len(order)
                for spot, device in enumerate(order):
                    piece = slice(device * rows, (device + 1) * rows)
                    pair = [kinds[block + step][kind][piece] for step in range(2)]
                    outgoing[spot, kind, block * rows : (block + 2) * rows] = jnp.concatenate(
                        pair, 0
                    ).astype(jnp.bfloat16)


def hop_kernel(outer, order, green, less, great, coupling, open_mask, source, outgoing):
    block_count, orbitals = green.shape[0], green.shape[1]
    blocks = range(block_count)
    hops, both, middles = [], [], []
    for block in blocks:
        factors = []
        if block + 1 < block_count:
            factors.append(coupling[block].T)
        if block > 0:
            factors.append(coupling[block - 1])
        hops.append(product(jnp.concatenate(factors, 0), green[block]).astype(jnp.bfloat16))
    for block in blocks:
        prior = jnp.concatenate([less[block], great[block]], 1)
        both.append(product(hops[block], prior).astype(jnp.bfloat16))
        middles.append(jnp.concatenate([less[block], great[block]], 0).astype(jnp.float32))
    for block in blocks:
        first = 0
        for target in (block + 1, block - 1):
            if 0 <= target < block_count:
                piece = slice(first, first + orbitals)
                half = both[block][piece]
                stacked = jnp.concatenate([half[:, :orbitals], half[:, orbitals:]], 0)
                middles[target] = middles[target] + product_t(stacked, hops[block][piece])
                first += orbitals
    for slot, block in enumerate(outer):
        source[slot] = middles[block]
    inner = [block for block in blocks if block not in outer]
    finish(inner, middles, green, open_mask, outgoing, order)


def green_kernel(swap, outer, order, green, coupling, open_mask, source, _, *rest):
    halos, outgoing = rest[:-1], rest[-1]
    last = green.shape[0] - 1
    place = lax.axis_index("space")
    middles = {block: source[slot] for slot, block in enumerate(outer)}
    if swap:
        (halo,) = halos
        hop = jnp.where(place == 0, coupling[last], halo[3].T)
        edge = through(product(hop, halo[0]).astype(jnp.bfloat16), halo[1], halo[2])
        middles[0] = middles[0] + jnp.where(place > 0, edge, 0.0)
        middles[last] = middles[last] + jnp.where(place == 0, edge, 0.0)
    elif halos:
        before, after = halos
        hop = product(before[3].T, before[0]).astype(jnp.bfloat16)
        middles[0] = middles[0] + through(hop, before[1], before[2])
        hop = product(coupling[last], after[0]).astype(jnp.bfloat16)
        middles[last] = middles[last] + through(hop, after[1], after[2])
    finish(outer, middles, green, open_mask, outgoing, order)


def lane_sums(values):
    coarse = values.astype(jnp.bfloat16)
    fine = (values - coarse.astype(jnp.float32)).astype(jnp.bfloat16)
    ones = jnp.ones((8, 2 * values.shape[1]), jnp.bfloat16)
    return product_t(ones, jnp.concatenate([coarse, fine], 1))[0:1]


def density_kernel(order, rows, density):
    _, _, row_count, orbitals = rows.shape
    block_count = density.shape[1]
    local_rows = row_count // block_count
    row_ids = lax.broadcasted_iota(jnp.int32, (row_count, orbitals), 0) % local_rows
    column_ids = lax.broadcasted_iota(jnp.int32, (row_count, orbitals), 1)
    total = jnp.zeros((row_count, orbitals), jnp.float32)
    for spot, device in enumerate(order):
        both = rows[spot, 0].astype(jnp.float32) + rows[spot, 1].astype(jnp.float32)
        total = jnp.where(column_ids == row_ids + device * local_rows, both, total)
    total = jnp.sum(total.reshape(block_count, local_rows, orbitals), axis=1)
    density[...] = lane_sums(total) / orbitals


def spread(strength, rows):
    return jnp.concatenate([strength] * (rows // strength.shape[0]), 0)


def current_kernel(order, back_order, shift, rows, strength, parts, wide, total):
    energies, _, row_count, orbitals = rows.shape
    block_count = total.shape[1]
    pad = energies // 2
    edge = jnp.zeros((pad, 2, row_count, orbitals), jnp.float32)
    wide[0:pad] = edge
    wide[pad + energies :] = edge
    for spot, energy in enumerate(order):
        wide[pad + energy] = rows[spot].astype(jnp.float32)
    scale = spread(strength[...] * (1.0 / orbitals), row_count)
    first, second = shift[0], shift[1]

    def step(energy, carry):
        here = energy + pad
        above, below = (
            [wide[here + first, kind] + wide[here + second, kind] for kind in range(2)],
            [wide[here - first, kind] + wide[here - second, kind] for kind in range(2)],
        )
        gain = (1.0 + phonon_occupation) * above[0] + phonon_occupation * below[0]
        loss = (1.0 + phonon_occupation) * below[1] + phonon_occupation * above[1]
        flow = (gain * wide[here, 1] - loss * wide[here, 0]) * scale
        total[energy] = jnp.sum(flow.reshape(block_count, -1, orbitals), axis=1)
        return carry

    lax.fori_loop(0, energies, step, 0, unroll=4)
    flat = lane_sums(total[...].reshape(energies * block_count, orbitals))
    for spot, energy in enumerate(back_order):
        parts[spot] = flat[:, energy * block_count : (energy + 1) * block_count]


def sigma_kernel(pieces, shift, wide, strength, less_out, great_out, less, great, sems):
    energies, row_count, _ = less.shape
    pad = energies // 2
    factor = spread(strength[...], row_count)
    first, second = shift[0], shift[1]

    def step(energy, carry):
        here = energy + pad
        above, below = (
            [wide[here + first, kind] + wide[here + second, kind] for kind in range(2)],
            [wide[here - first, kind] + wide[here - second, kind] for kind in range(2)],
        )
        gain = (1.0 + phonon_occupation) * above[0] + phonon_occupation * below[0]
        loss = (1.0 + phonon_occupation) * below[1] + phonon_occupation * above[1]
        less[energy] = (factor * gain).astype(less.dtype)
        great[energy] = (factor * loss).astype(great.dtype)
        return carry

    copies = []
    length = energies // pieces
    for piece in range(pieces):
        lax.fori_loop(piece * length, (piece + 1) * length, step, 0, unroll=2)
        part = pl.ds(piece * length, length)
        for slot, (origin, target) in enumerate(((less, less_out), (great, great_out))):
            copy = pltpu.make_async_copy(origin.at[part], target.at[part], sems.at[slot, piece])
            copy.start()
            copies.append(copy)
    for copy in copies:
        copy.wait()


def local(
    green_ret, prior_less, prior_great, coupling, phonon_coupling, phonon_shift, active_blocks
):
    _, block_count, orbitals, _ = green_ret.shape
    devices, places = lax.axis_size("energy"), lax.axis_size("space")
    row_count = orbitals // devices
    last = block_count - 1
    order, back_order = orders(devices)
    swap = places == 2
    if swap:
        edges = [lambda: last * (1 - lax.axis_index("space"))]
    elif places > 1:
        edges = [lambda: last, lambda: 0]
    else:
        edges = []
    arrays, shift, open_mask, packed = load(
        edges, (green_ret, prior_less, prior_great, coupling), active_blocks, phonon_shift
    )
    green, less, great, coupling = arrays
    if swap:
        halos = (lax.ppermute(packed[0], "space", [(0, 1), (1, 0)]),)
    else:
        halos = tuple(
            shifted(edge, "space", step) for edge, step in zip(packed, (1, -1), strict=False)
        )
    split = row_count % 8 == 0 and block_count % 2 == 0
    if split:
        out_shape = (devices, 2, block_count * row_count, orbitals)
    else:
        out_shape = (2, block_count, orbitals, orbitals)
    outer = sorted({0, 1, last - 1, last})
    store_order = order if split else None
    source, outgoing = pl.pallas_call(
        functools.partial(hop_kernel, outer, store_order),
        out_shape=(
            held((len(outer), 2 * orbitals, orbitals), jnp.float32),
            held(out_shape, jnp.bfloat16),
        ),
        in_specs=[VMEM] * 5,
        out_specs=(VMEM, VMEM),
        compiler_params=params(),
        cost_estimate=pl.CostEstimate(
            flops=20 * block_count * orbitals**3,
            bytes_accessed=8 * block_count * orbitals**2,
            transcendentals=0,
        ),
    )(green, less, great, coupling, open_mask)
    outgoing = pl.pallas_call(
        functools.partial(green_kernel, swap, outer, store_order),
        out_shape=held(out_shape, jnp.bfloat16),
        in_specs=[VMEM] * (5 + len(halos)),
        out_specs=VMEM,
        input_output_aliases={4: 0},
        compiler_params=params(),
    )(green, coupling, open_mask, source, outgoing, *halos)
    if not split:
        outgoing = outgoing.reshape(2, block_count, devices, row_count, orbitals)
        outgoing = jnp.stack([outgoing[:, :, device] for device in order])
        outgoing = outgoing.reshape(devices, 2, block_count * row_count, orbitals)
    rows = exchange(outgoing, order)
    ldos = pl.pallas_call(
        functools.partial(density_kernel, order),
        out_shape=jax.ShapeDtypeStruct((1, block_count), jnp.float32),
        in_specs=[VMEM],
        out_specs=VMEM,
        compiler_params=params(),
        cost_estimate=pl.CostEstimate(
            flops=4 * rows.size, bytes_accessed=2 * rows.size, transcendentals=0
        ),
    )(outgoing)
    parts, wide = pl.pallas_call(
        functools.partial(current_kernel, order, back_order),
        out_shape=(
            held((devices, 1, block_count), jnp.float32),
            held((2 * devices, *rows.shape[1:]), jnp.float32),
        ),
        in_specs=[SMEM, VMEM, VMEM],
        out_specs=(VMEM, VMEM),
        scratch_shapes=[pltpu.VMEM((devices, block_count, orbitals), jnp.float32)],
        compiler_params=params(),
    )(in_smem(shift), rows, phonon_coupling)
    parts = exchange(parts, back_order)
    out_shape = (devices, block_count * row_count, orbitals)
    pieces = 4 if devices % 4 == 0 else 1
    sigmas = pl.pallas_call(
        functools.partial(sigma_kernel, pieces),
        out_shape=[pltpu.HBM(out_shape, jnp.bfloat16)] * 2,
        in_specs=[SMEM, VMEM, VMEM],
        out_specs=[ANY] * 2,
        scratch_shapes=[
            *[pltpu.VMEM(out_shape, jnp.bfloat16)] * 2,
            pltpu.SemaphoreType.DMA((2, pieces)),
        ],
        compiler_params=params(),
        cost_estimate=pl.CostEstimate(
            flops=20 * rows.size, bytes_accessed=4 * rows.size, transcendentals=0
        ),
    )(in_smem(shift), wide, phonon_coupling)
    sigma_l, sigma_g = [
        sigma.reshape(devices, block_count, row_count, orbitals) for sigma in sigmas
    ]
    current = jnp.sum(parts, axis=0)
    return (sigma_l, sigma_g, current, ldos)


def solution(mesh):
    return jax.shard_map(
        local,
        mesh=mesh,
        in_specs=(
            P("energy", "space", None, None),
            P("energy", "space", None, None),
            P("energy", "space", None, None),
            P("space", None, None),
            P("energy", None),
            P(),
            P(),
        ),
        out_specs=(
            P(None, "space", "energy", None),
            P(None, "space", "energy", None),
            P("energy", "space"),
            P("energy", "space"),
        ),
        check_vma=False,
    )
```

time: 38.3 us -> 36.8 us (0.961)
  blocking collectives: 0 us -> 20.7 us
  waiting for transfers between devices: 11.8 us -> 0.62 us
  starting transfers between devices: 17.7 us -> 7.67 us
  other arithmetic: 1.17 us -> 0.54 us
    all_to_all x0 -> x1, blocking collectives: none -> 20.7 us  [exchange(): lax.all_to_all(chunks, 'energy', split_axis=0, concat_axis=0, tiled=True,...]
    all_to_all x2 -> x1, waiting for transfers between devices: 11.7 us -> 0.61 us  [exchange(): lax.all_to_all(chunks, 'energy', split_axis=0, concat_axis=0, tiled=True,...]
    all_to_all x2 -> x1, starting transfers between devices: 17.2 us -> 7.15 us  [exchange(): lax.all_to_all(chunks, 'energy', split_axis=0, concat_axis=0, tiled=True,...]
    div x1 -> x0, other arithmetic: 0.51 us -> none  [local(): ldos = jnp.sum(diagonal, axis=1)[None, :] / orbitals]
    pallas_call x3 -> x4, Pallas kernels: 3.91 us -> 3.62 us  [the longest x1 1.08 us: local(): pl.pallas_call(functools.partial(hop_kernel, outer, store_order), out_sha...]
  transfers between devices with their start and end apart: 3 -> 2, of which waited for: 3 -> 1; matrix products, arithmetic and copies ran while one was open for 2% -> 0% of each run, Pallas kernels for 6% -> 8%
where the time goes in v6:
time: 36.8 us; the launch traced here: 36.6 us
  blocking collectives  20.7 us (56%)
  starting transfers between devices  7.67 us (21%)
  Pallas kernels  6.36 us (17%)
  between operations  0.68 us (2%)
  waiting for transfers between devices  0.62 us (2%)
  other arithmetic  0.54 us (1%)
    all_to_all x1, blocking collectives, exchange(): lax.all_to_all(chunks, 'energy', split_axis=0, concat_axis=0, tiled=True,...  20.7 us
    all_to_all x1, starting transfers between devices, exchange(): lax.all_to_all(chunks, 'energy', split_axis=0, concat_axis=0, tiled=True,...  7.15 us
    pallas_call x1, Pallas kernels, load(): pl.pallas_call(functools.partial(load_kernel, edges), out_shape=(*[blocks...  1.37 us
    pallas_call x1, Pallas kernels, local(): pl.pallas_call(functools.partial(current_kernel, order, back_order), out_...  1.37 us
    pallas_call x1, Pallas kernels, local(): pl.pallas_call(functools.partial(hop_kernel, outer, store_order), out_sha...  1.08 us
    pallas_call x1, Pallas kernels, local(): pl.pallas_call(functools.partial(sigma_kernel, pieces), out_shape=[pltpu....  0.99 us
    pallas_call x1, Pallas kernels, local(): pl.pallas_call(functools.partial(green_kernel, swap, outer, store_order),...  0.8 us
    pallas_call x1, Pallas kernels, local(): pl.pallas_call(functools.partial(density_kernel, order), out_shape=jax.Sh...  0.75 us
  transfers between devices with their start and end apart: 2, of which 1 were waited for; matrix products, arithmetic and copies ran while one was open for 0% of the time, Pallas kernels for 8%

profile of v6, /device:TPU:0, one launch (start us, length us, event | category | flops | bytes accessed | tf_op | source)
XLA Modules:
  0.0 36.6 jit_solution(13091154574808798728)
XLA Ops:
  0.6 1.4 %shard_map.102 = (bf16[8,128,128]{2,1,0:T(8,128)(2,1)S(1)}, bf16[8,128,128]{2,1,0:T(8,128)(2,1)S(1)}, bf16[8,128,128]{2,1,0:T(8,128)(2,1)S(1)}, bf16[8,128,128]{...) custom-call(bf16[1,8,128,128]{3,2,1,0:T(8,128)(2,1)} %refs_0_.1, ...), custom_call_target="tpu_custom_call" | custom-call | tf_op jit(solution)/shard_map/pallas_call | solution.py:91
  2.0 0.5 %collective-permute-start = (bf16[4,128,128]{2,1,0:T(8,128)(2,1)S(1)}, bf16[4,128,128]{2,1,0:T(8,128)(2,1)S(1)}, u32[]{:S(2)}, u32[]{:S(2)}) collective-permute-start(bf16[4,128,128]{2,1,0:T(8,128)(2,1)S(1)} %get-tuple-element.25), channel_id=1, source_target_pairs={{0,1},{1,0},{2,3},{3,2},{4,5},{5,4},{6,7},{7,6},{8,9},{9,8},{10,11... | collective-permute-start | bytes 393224 | tf_op jit(solution)/shard_map/ppermute | solution.py:300
  2.5 0.0 copy-start
  2.5 1.1 %shard_map.103 = (f32[4,256,128]{2,1,0:T(8,128)S(1)}, bf16[16,2,64,128]{3,2,1,0:T(8,128)(2,1)S(1)}) custom-call(bf16[8,128,128]{2,1,0:T(8,128)(2,1)S(1)} %get-tuple-element.18.green, bf16[8,128,128]{2,1,0:T(8,128)(2,1)S(1)} %get-tuple-element.21.less, bf16[8,128,128]{2,1,0:T(8,128)(2,1)S(1)} %get-tuple-element.22.great, ...), custom_call_target="tpu_custom_call" | custom-call | flops 335544320 | bytes 1048576 | tf_op jit(solution)/shard_map/pallas_call | solution.py:312
  3.6 0.0 collective-permute-done.rest_0_
  3.6 0.8 %shard_map.104.rows = bf16[16,2,64,128]{3,2,1,0:T(8,128)(2,1)S(1)} custom-call(bf16[8,128,128]{2,1,0:T(8,128)(2,1)S(1)} %get-tuple-element.18.green, bf16[8,128,128]{2,1,0:T(8,128)(2,1)S(1)} %get-tuple-element.19.coupling, f32[8,128]{1,0:T(8,128)S(1)} %get-tuple-element.20.open_mask, ...), custom_call_target="tpu_custom_call", output_to_operand_aliasing={{}: (4, {})} | custom-call | tf_op jit(solution)/shard_map/pallas_call | solution.py:327
  4.4 20.7 %all_to_all.10.rows = bf16[16,2,64,128]{3,2,1,0:T(8,128)(2,1)S(1)} all-to-all(bf16[16,2,64,128]{3,2,1,0:T(8,128)(2,1)S(1)} %shard_map.104.rows), channel_id=1, replica_groups={{18,0,2,4,6,8,10,12,14,16,20,22,24,26,28,30},{19,1,3,5,7,9,11,13,15,17,..., dimensions={0} | all-to-all | bytes 1048576 | tf_op jit(solution)/shard_map/all_to_all | solution.py:31
  25.1 0.0 copy-done
  25.1 1.4 %shard_map.105 = (f32[16,1,8]{2,1,0:T(1,128)}, f32[32,2,64,128]{3,2,1,0:T(8,128)S(1)}) custom-call(s32[2]{0:T(128)S(4)} %get-tuple-element.17.shift, bf16[16,2,64,128]{3,2,1,0:T(8,128)(2,1)S(1)} %all_to_all.10.rows, f32[8,128]{1,0:T(8,128)S(1)} %copy-done), custom_call_target="tpu_custom_call" | custom-call | tf_op jit(solution)/shard_map/pallas_call | solution.py:350
  26.5 7.1 %all-to-all-start.1 = ((f32[16,1,8]{2,1,0:T(1,128)}), f32[16,1,8]{2,1,0:T(1,128)S(1)}, u32[]{:S(2)}, u32[]{:S(2)}) async-start(f32[16,1,8]{2,1,0:T(1,128)} %get-tuple-element.29), calls=%async_computation.1 | async-start | bytes 16384 | tf_op jit(solution)/shard_map/all_to_all | solution.py:31
  33.6 0.8 %shard_map.107 = f32[1,8]{1,0:T(1,128)} custom-call(bf16[16,2,64,128]{3,2,1,0:T(8,128)(2,1)S(1)} %shard_map.104.rows), custom_call_target="tpu_custom_call" | custom-call | flops 1048576 | bytes 524288 | tf_op jit(solution)/shard_map/pallas_call | solution.py:340
  34.4 1.0 %shard_map.106 = (bf16[16,64,128]{2,1,0:T(8,128)(2,1)}, bf16[16,64,128]{2,1,0:T(8,128)(2,1)}) custom-call(s32[2]{0:T(128)S(4)} %get-tuple-element.17.shift, f32[32,2,64,128]{3,2,1,0:T(8,128)S(1)} %get-tuple-element.26.wide, f32[8,128]{1,0:T(8,128)S(1)} %copy-done), custom_call_target="tpu_custom_call" | custom-call | flops 5242880 | bytes 1048576 | tf_op jit(solution)/shard_map/pallas_call | solution.py:364
  35.4 0.6 %all-to-all-done.1 = f32[16,1,8]{2,1,0:T(1,128)S(1)} async-done(((f32[16,1,8]{2,1,0:T(1,128)}), f32[16,1,8]{2,1,0:T(1,128)S(1)}, u32[]{:S(2)}, u32[]{:S(2)}) %all-to-all-start.1) | async-done | bytes 544 | tf_op jit(solution)/shard_map/all_to_all | solution.py:31
  36.0 0.5 %reduce_sum.11 = f32[8]{0:T(128)} reduce(f32[16,1,8]{2,1,0:T(1,128)S(1)} %all-to-all-done.1, f32[]{:T(128)} %constant.0.clone.1), dimensions={0,1}, to_apply=%region_0.0 | reduce | flops 120 | bytes 548 | tf_op jit(solution)/shard_map/reduce_sum | solution.py:381
Async XLA Ops:
  2.0 1.6 %collective-permute-start = (bf16[4,128,128]{2,1,0:T(8,128)(2,1)S(1)}, bf16[4,128,128]{2,1,0:T(8,128)(2,1)S(1)}, u32[]{:S(2)}, u32[]{:S(2)}) collective-permute-start(bf16[4,128,128]{2,1,0:T(8,128)(2,1)S(1)} %get-tuple-element.25), channel_id=1, source_target_pairs={{0,1},{1,0},{2,3},{3,2},{4,5},{5,4},{6,7},{7,6},{8,9},{9,8},{10,11... | collective-permute-start | bytes 393224 | tf_op jit(solution)/shard_map/ppermute | solution.py:300
  2.5 22.6 %copy-start = (f32[8,128]{1,0:T(8,128)S(1)}, f32[8,128]{1,0:T(8,128)}, u32[]{:S(2)}) copy-start(f32[8,128]{1,0:T(8,128)} %strength.3) | copy-start | bytes 12292
  26.5 9.5 %all-to-all-start.1 = ((f32[16,1,8]{2,1,0:T(1,128)}), f32[16,1,8]{2,1,0:T(1,128)S(1)}, u32[]{:S(2)}, u32[]{:S(2)}) async-start(f32[16,1,8]{2,1,0:T(1,128)} %get-tuple-element.29), calls=%async_computation.1 | async-start | bytes 16384 | tf_op jit(solution)/shard_map/all_to_all | solution.py:31

commit v7 on v6

--- a/solution.py
+++ b/solution.py
@@ -24,7 +24,7 @@
     def starting(root):
         return [root] + [index for index in range(count) if index != root]
 
-    return starting(9 * count // 16), starting(count - 1)
+    return starting(11 * count // 16), starting(count - 1)
 
 
 def exchange(chunks, order):
@@ -115,8 +115,10 @@
     return product_t(stacked, operator)
 
 
-def finish(blocks, middles, green, open_mask, outgoing, order):
+def finish(blocks, middles, green, open_mask, outgoing, diagonal, order):
     orbitals = green.shape[1]
+    row_ids = lax.broadcasted_iota(jnp.int32, (orbitals, orbitals), 0)
+    on_diagonal = row_ids == lax.broadcasted_iota(jnp.int32, (orbitals, orbitals), 1)
     halves, kinds = {}, {}
     for block in blocks:
         middle = middles[block].astype(jnp.bfloat16)
@@ -127,6 +129,9 @@
         stacked = jnp.concatenate([half[:, :orbitals], half[:, orbitals:]], 0)
         result = product_t(stacked, green[block]) * open_mask[block : block + 1]
         kinds[block] = [result[:orbitals], result[orbitals:]]
+        diagonal[block : block + 1] = jnp.sum(
+            jnp.where(on_diagonal, kinds[block][0] + kinds[block][1], 0.0), axis=0, keepdims=True
+        )
     for block in blocks:
         for kind in range(2):
             if order is None:
@@ -141,7 +146,7 @@
                     ).astype(jnp.bfloat16)
 
 
-def hop_kernel(outer, order, green, less, great, coupling, open_mask, source, outgoing):
+def hop_kernel(outer, order, green, less, great, coupling, open_mask, source, outgoing, diagonal):
     block_count, orbitals = green.shape[0], green.shape[1]
     blocks = range(block_count)
     hops, both, middles = [], [], []
@@ -168,11 +173,11 @@
     for slot, block in enumerate(outer):
         source[slot] = middles[block]
     inner = [block for block in blocks if block not in outer]
-    finish(inner, middles, green, open_mask, outgoing, order)
-
-
-def green_kernel(swap, outer, order, green, coupling, open_mask, source, _, *rest):
-    halos, outgoing = rest[:-1], rest[-1]
+    finish(inner, middles, green, open_mask, outgoing, diagonal, order)
+
+
+def green_kernel(swap, outer, order, green, coupling, open_mask, source, *rest):
+    (_, inner_diagonal), halos, (outgoing, diagonal) = rest[:2], rest[2:-2], rest[-2:]
     last = green.shape[0] - 1
     place = lax.axis_index("space")
     middles = {block: source[slot] for slot, block in enumerate(outer)}
@@ -188,7 +193,8 @@
         middles[0] = middles[0] + through(hop, before[1], before[2])
         hop = product(coupling[last], after[0]).astype(jnp.bfloat16)
         middles[last] = middles[last] + through(hop, after[1], after[2])
-    finish(outer, middles, green, open_mask, outgoing, order)
+    diagonal[...] = inner_diagonal[...]
+    finish(outer, middles, green, open_mask, outgoing, diagonal, order)
 
 
 def lane_sums(values):
@@ -198,25 +204,27 @@
     return product_t(ones, jnp.concatenate([coarse, fine], 1))[0:1]
 
 
-def density_kernel(order, rows, density):
-    _, _, row_count, orbitals = rows.shape
-    block_count = density.shape[1]
-    local_rows = row_count // block_count
-    row_ids = lax.broadcasted_iota(jnp.int32, (row_count, orbitals), 0) % local_rows
-    column_ids = lax.broadcasted_iota(jnp.int32, (row_count, orbitals), 1)
-    total = jnp.zeros((row_count, orbitals), jnp.float32)
-    for spot, device in enumerate(order):
-        both = rows[spot, 0].astype(jnp.float32) + rows[spot, 1].astype(jnp.float32)
-        total = jnp.where(column_ids == row_ids + device * local_rows, both, total)
-    total = jnp.sum(total.reshape(block_count, local_rows, orbitals), axis=1)
-    density[...] = lane_sums(total) / orbitals
+def totals_kernel(parts, diagonal, less, great, current, density, less_out, great_out, sems):
+    copies = [
+        pltpu.make_async_copy(less, less_out, sems.at[0]),
+        pltpu.make_async_copy(great, great_out, sems.at[1]),
+    ]
+    for copy in copies:
+        copy.start()
+    total = parts[0]
+    for spot in range(1, parts.shape[0]):
+        total = total + parts[spot]
+    current[...] = total
+    density[...] = lane_sums(diagonal[...]) / diagonal.shape[1]
+    for copy in copies:
+        copy.wait()
 
 
 def spread(strength, rows):
     return jnp.concatenate([strength] * (rows // strength.shape[0]), 0)
 
 
-def current_kernel(order, back_order, shift, rows, strength, parts, wide, total):
+def current_kernel(order, back_order, shift, rows, strength, parts, less, great, wide, total):
     energies, _, row_count, orbitals = rows.shape
     block_count = total.shape[1]
     pad = energies // 2
@@ -225,31 +233,8 @@
     wide[pad + energies :] = edge
     for spot, energy in enumerate(order):
         wide[pad + energy] = rows[spot].astype(jnp.float32)
+    factor = spread(strength[...], row_count)
     scale = spread(strength[...] * (1.0 / orbitals), row_count)
-    first, second = shift[0], shift[1]
-
-    def step(energy, carry):
-        here = energy + pad
-        above, below = (
-            [wide[here + first, kind] + wide[here + second, kind] for kind in range(2)],
-            [wide[here - first, kind] + wide[here - second, kind] for kind in range(2)],
-        )
-        gain = (1.0 + phonon_occupation) * above[0] + phonon_occupation * below[0]
-        loss = (1.0 + phonon_occupation) * below[1] + phonon_occupation * above[1]
-        flow = (gain * wide[here, 1] - loss * wide[here, 0]) * scale
-        total[energy] = jnp.sum(flow.reshape(block_count, -1, orbitals), axis=1)
-        return carry
-
-    lax.fori_loop(0, energies, step, 0, unroll=4)
-    flat = lane_sums(total[...].reshape(energies * block_count, orbitals))
-    for spot, energy in enumerate(back_order):
-        parts[spot] = flat[:, energy * block_count : (energy + 1) * block_count]
-
-
-def sigma_kernel(pieces, shift, wide, strength, less_out, great_out, less, great, sems):
-    energies, row_count, _ = less.shape
-    pad = energies // 2
-    factor = spread(strength[...], row_count)
     first, second = shift[0], shift[1]
 
     def step(energy, carry):
@@ -262,19 +247,14 @@
         loss = (1.0 + phonon_occupation) * below[1] + phonon_occupation * above[1]
         less[energy] = (factor * gain).astype(less.dtype)
         great[energy] = (factor * loss).astype(great.dtype)
+        flow = (gain * wide[here, 1] - loss * wide[here, 0]) * scale
+        total[energy] = jnp.sum(flow.reshape(block_count, -1, orbitals), axis=1)
         return carry
 
-    copies = []
-    length = energies // pieces
-    for piece in range(pieces):
-        lax.fori_loop(piece * length, (piece + 1) * length, step, 0, unroll=2)
-        part = pl.ds(piece * length, length)
-        for slot, (origin, target) in enumerate(((less, less_out), (great, great_out))):
-            copy = pltpu.make_async_copy(origin.at[part], target.at[part], sems.at[slot, piece])
-            copy.start()
-            copies.append(copy)
-    for copy in copies:
-        copy.wait()
+    lax.fori_loop(0, energies, step, 0, unroll=4)
+    flat = lane_sums(total[...].reshape(energies * block_count, orbitals))
+    for spot, energy in enumerate(back_order):
+        parts[spot] = flat[:, energy * block_count : (energy + 1) * block_count]
 
 
 def local(
@@ -309,14 +289,16 @@
         out_shape = (2, block_count, orbitals, orbitals)
     outer = sorted({0, 1, last - 1, last})
     store_order = order if split else None
-    source, outgoing = pl.pallas_call(
+    diagonals = held((block_count, orbitals), jnp.float32)
+    source, outgoing, diagonal = pl.pallas_call(
         functools.partial(hop_kernel, outer, store_order),
         out_shape=(
             held((len(outer), 2 * orbitals, orbitals), jnp.float32),
             held(out_shape, jnp.bfloat16),
+            diagonals,
         ),
         in_specs=[VMEM] * 5,
-        out_specs=(VMEM, VMEM),
+        out_specs=(VMEM, VMEM, VMEM),
         compiler_params=params(),
         cost_estimate=pl.CostEstimate(
             flops=20 * block_count * orbitals**3,
@@ -324,61 +306,45 @@
             transcendentals=0,
         ),
     )(green, less, great, coupling, open_mask)
-    outgoing = pl.pallas_call(
+    outgoing, diagonal = pl.pallas_call(
         functools.partial(green_kernel, swap, outer, store_order),
-        out_shape=held(out_shape, jnp.bfloat16),
-        in_specs=[VMEM] * (5 + len(halos)),
-        out_specs=VMEM,
+        out_shape=(held(out_shape, jnp.bfloat16), diagonals),
+        in_specs=[VMEM] * (6 + len(halos)),
+        out_specs=(VMEM, VMEM),
         input_output_aliases={4: 0},
         compiler_params=params(),
-    )(green, coupling, open_mask, source, outgoing, *halos)
+    )(green, coupling, open_mask, source, outgoing, diagonal, *halos)
     if not split:
         outgoing = outgoing.reshape(2, block_count, devices, row_count, orbitals)
         outgoing = jnp.stack([outgoing[:, :, device] for device in order])
         outgoing = outgoing.reshape(devices, 2, block_count * row_count, orbitals)
     rows = exchange(outgoing, order)
-    ldos = pl.pallas_call(
-        functools.partial(density_kernel, order),
-        out_shape=jax.ShapeDtypeStruct((1, block_count), jnp.float32),
-        in_specs=[VMEM],
-        out_specs=VMEM,
-        compiler_params=params(),
-        cost_estimate=pl.CostEstimate(
-            flops=4 * rows.size, bytes_accessed=2 * rows.size, transcendentals=0
-        ),
-    )(outgoing)
-    parts, wide = pl.pallas_call(
+    sigma_shape = held((devices, block_count * row_count, orbitals), jnp.bfloat16)
+    parts, *sigmas = pl.pallas_call(
         functools.partial(current_kernel, order, back_order),
-        out_shape=(
-            held((devices, 1, block_count), jnp.float32),
-            held((2 * devices, *rows.shape[1:]), jnp.float32),
-        ),
+        out_shape=(held((devices, 1, block_count), jnp.float32), sigma_shape, sigma_shape),
         in_specs=[SMEM, VMEM, VMEM],
-        out_specs=(VMEM, VMEM),
-        scratch_shapes=[pltpu.VMEM((devices, block_count, orbitals), jnp.float32)],
+        out_specs=(VMEM, VMEM, VMEM),
+        scratch_shapes=[
+            pltpu.VMEM((2 * devices, *rows.shape[1:]), jnp.float32),
+            pltpu.VMEM((devices, block_count, orbitals), jnp.float32),
+        ],
         compiler_params=params(),
     )(in_smem(shift), rows, phonon_coupling)
     parts = exchange(parts, back_order)
-    out_shape = (devices, block_count * row_count, orbitals)
-    pieces = 4 if devices % 4 == 0 else 1
-    sigmas = pl.pallas_call(
-        functools.partial(sigma_kernel, pieces),
-        out_shape=[pltpu.HBM(out_shape, jnp.bfloat16)] * 2,
-        in_specs=[SMEM, VMEM, VMEM],
-        out_specs=[ANY] * 2,
-        scratch_shapes=[
-            *[pltpu.VMEM(out_shape, jnp.bfloat16)] * 2,
-            pltpu.SemaphoreType.DMA((2, pieces)),
-        ],
-        compiler_params=params(),
-        cost_estimate=pl.CostEstimate(
-            flops=20 * rows.size, bytes_accessed=4 * rows.size, transcendentals=0
-        ),
-    )(in_smem(shift), wide, phonon_coupling)
+    sums = jax.ShapeDtypeStruct((1, block_count), jnp.float32)
+    sigma_out = pltpu.HBM(sigmas[0].shape, sigmas[0].dtype)
+    current, ldos, *sigmas = pl.pallas_call(
+        totals_kernel,
+        out_shape=(sums, sums, sigma_out, sigma_out),
+        in_specs=[VMEM] * 4,
+        out_specs=(VMEM, VMEM, ANY, ANY),
+        scratch_shapes=[pltpu.SemaphoreType.DMA((2,))],
+        compiler_params=params(),
+    )(parts, diagonal, *sigmas)
     sigma_l, sigma_g = [
         sigma.reshape(devices, block_count, row_count, orbitals) for sigma in sigmas
     ]
-    current = jnp.sum(parts, axis=0)
     return (sigma_l, sigma_g, current, ldos)
 
 

time: 36.8 us -> 36.2 us (0.984)
  blocking collectives: 20.7 us -> 29.4 us
  starting transfers between devices: 7.67 us -> 0.52 us
  Pallas kernels: 6.36 us -> 5.38 us
  waiting for transfers between devices: 0.62 us -> 0.01 us
  other arithmetic: 0.54 us -> 0 us
    all_to_all x1 -> x2, blocking collectives: 20.7 us -> 29.4 us  [exchange(): lax.all_to_all(chunks, 'energy', split_axis=0, concat_axis=0, tiled=True,...]
    all_to_all x1 -> x0, starting transfers between devices: 7.15 us -> none  [exchange(): lax.all_to_all(chunks, 'energy', split_axis=0, concat_axis=0, tiled=True,...]
    all_to_all x1 -> x0, waiting for transfers between devices: 0.61 us -> none  [exchange(): lax.all_to_all(chunks, 'energy', split_axis=0, concat_axis=0, tiled=True,...]
    pallas_call x1, Pallas kernels: 1.37 us -> 0.78 us  [local(): pl.pallas_call(functools.partial(current_kernel, order, back_order), out_...]
    reduce_sum x1 -> x0, other arithmetic: 0.54 us -> none  [local(): current = jnp.sum(parts, axis=0)]
    pallas_call x2 -> x1, Pallas kernels: 1.74 us -> 1.32 us  [local(): pl.pallas_call(totals_kernel, out_shape=(sums, sums, sigma_out, sigma_out...]
  transfers between devices with their start and end apart: 2 -> 1, of which waited for: 1 -> 0; matrix products, arithmetic and copies ran while one was open for 0% -> 0% of each run, Pallas kernels for 8% -> 3%
where the time goes in v7:
time: 36.2 us; the launch traced here: 36 us
  blocking collectives  29.4 us (81%)
  Pallas kernels  5.38 us (15%)
  between operations  0.67 us (2%)
  starting transfers between devices  0.52 us (1%)
    all_to_all x2, blocking collectives, exchange(): lax.all_to_all(chunks, 'energy', split_axis=0, concat_axis=0, tiled=True,...  29.4 us
    pallas_call x1, Pallas kernels, load(): pl.pallas_call(functools.partial(load_kernel, edges), out_shape=(*[blocks...  1.37 us
    pallas_call x1, Pallas kernels, local(): pl.pallas_call(totals_kernel, out_shape=(sums, sums, sigma_out, sigma_out...  1.32 us
    pallas_call x1, Pallas kernels, local(): pl.pallas_call(functools.partial(hop_kernel, outer, store_order), out_sha...  1.1 us
    pallas_call x1, Pallas kernels, local(): pl.pallas_call(functools.partial(green_kernel, swap, outer, store_order),...  0.81 us
    pallas_call x1, Pallas kernels, local(): pl.pallas_call(functools.partial(current_kernel, order, back_order), out_...  0.78 us
  transfers between devices with their start and end apart: 1, of which 0 were waited for; matrix products, arithmetic and copies ran while one was open for 0% of the time, Pallas kernels for 3%

profile of v7, /device:TPU:0, one launch (start us, length us, event | category | flops | bytes accessed | tf_op | source)
XLA Modules:
  0.0 36.0 jit_solution(10610448386884459205)
XLA Ops:
  0.6 1.4 %shard_map.102 = (bf16[8,128,128]{2,1,0:T(8,128)(2,1)S(1)}, bf16[8,128,128]{2,1,0:T(8,128)(2,1)S(1)}, bf16[8,128,128]{2,1,0:T(8,128)(2,1)S(1)}, bf16[8,128,128]{...) custom-call(bf16[1,8,128,128]{3,2,1,0:T(8,128)(2,1)} %refs_0_.1, ...), custom_call_target="tpu_custom_call" | custom-call | tf_op jit(solution)/shard_map/pallas_call | solution.py:91
  2.0 0.5 %collective-permute-start = (bf16[4,128,128]{2,1,0:T(8,128)(2,1)S(1)}, bf16[4,128,128]{2,1,0:T(8,128)(2,1)S(1)}, u32[]{:S(2)}, u32[]{:S(2)}) collective-permute-start(bf16[4,128,128]{2,1,0:T(8,128)(2,1)S(1)} %get-tuple-element.32), channel_id=1, source_target_pairs={{0,1},{1,0},{2,3},{3,2},{4,5},{5,4},{6,7},{7,6},{8,9},{9,8},{10,11... | collective-permute-start | bytes 393224 | tf_op jit(solution)/shard_map/ppermute | solution.py:280
  2.5 1.1 %shard_map.103 = (f32[4,256,128]{2,1,0:T(8,128)S(1)}, bf16[16,2,64,128]{3,2,1,0:T(8,128)(2,1)S(1)}, f32[8,128]{1,0:T(8,128)S(1)}) custom-call(bf16[8,128,128]{2,1,0:T(8,128)(2,1)S(1)} %get-tuple-element.24.green, bf16[8,128,128]{2,1,0:T(8,128)(2,1)S(1)} %get-tuple-element.27.less, bf16[8,128,128]{2,1,0:T(8,128)(2,1)S(1)} %get-tuple-element.28.great, ...), custom_call_target="tpu_custom_call" | custom-call | flops 335544320 | bytes 1048576 | tf_op jit(solution)/shard_map/pallas_call | solution.py:293
  3.6 0.0 collective-permute-done.rest_2_
  3.6 0.8 %shard_map.104 = (bf16[16,2,64,128]{3,2,1,0:T(8,128)(2,1)S(1)}, f32[8,128]{1,0:T(8,128)S(1)}) custom-call(bf16[8,128,128]{2,1,0:T(8,128)(2,1)S(1)} %get-tuple-element.24.green, bf16[8,128,128]{2,1,0:T(8,128)(2,1)S(1)} %get-tuple-element.25.coupling, f32[8,128]{1,0:T(8,128)S(1)} %get-tuple-element.26.open_mask, ...), custom_call_target="tpu_custom_call", output_to_operand_aliasing={{0}: (4, {})} | custom-call | tf_op jit(solution)/shard_map/pallas_call | solution.py:309
  4.5 0.0 copy-start
  4.5 19.8 %all_to_all.10.rows = bf16[16,2,64,128]{3,2,1,0:T(8,128)(2,1)S(1)} all-to-all(bf16[16,2,64,128]{3,2,1,0:T(8,128)(2,1)S(1)} %get-tuple-element.33), channel_id=1, replica_groups={{22,0,2,4,6,8,10,12,14,16,18,20,24,26,28,30},{23,1,3,5,7,9,11,13,15,17,..., dimensions={0} | all-to-all | bytes 1048576 | tf_op jit(solution)/shard_map/all_to_all | solution.py:31
  24.2 0.0 copy-done
  24.2 0.8 %shard_map.105 = (f32[16,1,8]{2,1,0:T(1,128)S(1)}, bf16[16,64,128]{2,1,0:T(8,128)(2,1)S(1)}, bf16[16,64,128]{2,1,0:T(8,128)(2,1)S(1)}) custom-call(s32[2]{0:T(128)S(4)} %get-tuple-element.23.shift, bf16[16,2,64,128]{3,2,1,0:T(8,128)(2,1)S(1)} %all_to_all.10.rows, f32[8,128]{1,0:T(8,128)S(1)} %copy-done), custom_call_target="tpu_custom_call" | custom-call | tf_op jit(solution)/shard_map/pallas_call | solution.py:323
  25.0 9.7 %all_to_all.11.parts = f32[16,1,8]{2,1,0:T(1,128)S(1)} all-to-all(f32[16,1,8]{2,1,0:T(1,128)S(1)} %get-tuple-element.34), channel_id=1, replica_groups={{30,0,2,4,6,8,10,12,14,16,18,20,22,24,26,28},{31,1,3,5,7,9,11,13,15,17,..., dimensions={0} | all-to-all | bytes 1024 | tf_op jit(solution)/shard_map/all_to_all | solution.py:31
  34.7 1.3 %shard_map.106 = (f32[1,8]{1,0:T(1,128)}, f32[1,8]{1,0:T(1,128)}, bf16[16,64,128]{2,1,0:T(8,128)(2,1)}, bf16[16,64,128]{2,1,0:T(8,128)(2,1)}) custom-call(f32[16,1,8]{2,1,0:T(1,128)S(1)} %all_to_all.11.parts, f32[8,128]{1,0:T(8,128)S(1)} %get-tuple-element.35.diagonal, bf16[16,64,128]{2,1,0:T(8,128)(2,1)S(1)} %get-tuple-element.36.less, ...), custom_call_target="tpu_custom_call" | custom-call | tf_op jit(solution)/shard_map/pallas_call | solution.py:337
Async XLA Ops:
  2.0 1.6 %collective-permute-start = (bf16[4,128,128]{2,1,0:T(8,128)(2,1)S(1)}, bf16[4,128,128]{2,1,0:T(8,128)(2,1)S(1)}, u32[]{:S(2)}, u32[]{:S(2)}) collective-permute-start(bf16[4,128,128]{2,1,0:T(8,128)(2,1)S(1)} %get-tuple-element.32), channel_id=1, source_target_pairs={{0,1},{1,0},{2,3},{3,2},{4,5},{5,4},{6,7},{7,6},{8,9},{9,8},{10,11... | collective-permute-start | bytes 393224 | tf_op jit(solution)/shard_map/ppermute | solution.py:280
  4.5 19.8 %copy-start = (f32[8,128]{1,0:T(8,128)S(1)}, f32[8,128]{1,0:T(8,128)}, u32[]{:S(2)}) copy-start(f32[8,128]{1,0:T(8,128)} %strength.1) | copy-start | bytes 12292

commit v8 on v7

--- a/solution.py
+++ b/solution.py
@@ -162,14 +162,18 @@
         both.append(product(hops[block], prior).astype(jnp.bfloat16))
         middles.append(jnp.concatenate([less[block], great[block]], 0).astype(jnp.float32))
     for block in blocks:
-        first = 0
-        for target in (block + 1, block - 1):
-            if 0 <= target < block_count:
-                piece = slice(first, first + orbitals)
-                half = both[block][piece]
-                stacked = jnp.concatenate([half[:, :orbitals], half[:, orbitals:]], 0)
-                middles[target] = middles[target] + product_t(stacked, hops[block][piece])
-                first += orbitals
+        sent = []
+        if block > 0:
+            sent.append((block - 1, slice(0, orbitals)))
+        if block + 1 < block_count:
+            first = orbitals if block + 2 < block_count else 0
+            sent.append((block + 1, slice(first, first + orbitals)))
+        stacked = [
+            jnp.concatenate([both[origin][piece, kind] for origin, piece in sent], 1)
+            for kind in (slice(0, orbitals), slice(orbitals, 2 * orbitals))
+        ]
+        operators = jnp.concatenate([hops[origin][piece] for origin, piece in sent], 1)
+        middles[block] = middles[block] + product_t(jnp.concatenate(stacked, 0), operators)
     for slot, block in enumerate(outer):
         source[slot] = middles[block]
     inner = [block for block in blocks if block not in outer]
@@ -204,27 +208,37 @@
     return product_t(ones, jnp.concatenate([coarse, fine], 1))[0:1]
 
 
-def totals_kernel(parts, diagonal, less, great, current, density, less_out, great_out, sems):
+def copy_out(less, great, less_out, great_out, sems):
     copies = [
         pltpu.make_async_copy(less, less_out, sems.at[0]),
         pltpu.make_async_copy(great, great_out, sems.at[1]),
     ]
     for copy in copies:
         copy.start()
+    for copy in copies:
+        copy.wait()
+
+
+def has_time():
+    return lax.axis_index("energy") == 0
+
+
+def totals_kernel(parts, diagonal, less, great, _, __, current, density, *outputs):
     total = parts[0]
     for spot in range(1, parts.shape[0]):
         total = total + parts[spot]
     current[...] = total
     density[...] = lane_sums(diagonal[...]) / diagonal.shape[1]
-    for copy in copies:
-        copy.wait()
+    pl.when(jnp.logical_not(has_time()))(functools.partial(copy_out, less, great, *outputs))
 
 
 def spread(strength, rows):
     return jnp.concatenate([strength] * (rows // strength.shape[0]), 0)
 
 
-def current_kernel(order, back_order, shift, rows, strength, parts, less, great, wide, total):
+def current_kernel(
+    order, back_order, shift, rows, strength, parts, less, great, less_out, great_out, wide, total, sems
+):
     energies, _, row_count, orbitals = rows.shape
     block_count = total.shape[1]
     pad = energies // 2
@@ -255,6 +269,7 @@
     flat = lane_sums(total[...].reshape(energies * block_count, orbitals))
     for spot, energy in enumerate(back_order):
         parts[spot] = flat[:, energy * block_count : (energy + 1) * block_count]
+    pl.when(has_time())(functools.partial(copy_out, less, great, less_out, great_out, sems))
 
 
 def local(
@@ -319,29 +334,31 @@
         outgoing = jnp.stack([outgoing[:, :, device] for device in order])
         outgoing = outgoing.reshape(devices, 2, block_count * row_count, orbitals)
     rows = exchange(outgoing, order)
-    sigma_shape = held((devices, block_count * row_count, orbitals), jnp.bfloat16)
-    parts, *sigmas = pl.pallas_call(
+    sigma_shape = (devices, block_count * row_count, orbitals)
+    kept, written = held(sigma_shape, jnp.bfloat16), pltpu.HBM(sigma_shape, jnp.bfloat16)
+    parts, less, great, *sigmas = pl.pallas_call(
         functools.partial(current_kernel, order, back_order),
-        out_shape=(held((devices, 1, block_count), jnp.float32), sigma_shape, sigma_shape),
+        out_shape=(held((devices, 1, block_count), jnp.float32), kept, kept, written, written),
         in_specs=[SMEM, VMEM, VMEM],
-        out_specs=(VMEM, VMEM, VMEM),
+        out_specs=(VMEM, VMEM, VMEM, ANY, ANY),
         scratch_shapes=[
             pltpu.VMEM((2 * devices, *rows.shape[1:]), jnp.float32),
             pltpu.VMEM((devices, block_count, orbitals), jnp.float32),
+            pltpu.SemaphoreType.DMA((2,)),
         ],
         compiler_params=params(),
     )(in_smem(shift), rows, phonon_coupling)
     parts = exchange(parts, back_order)
     sums = jax.ShapeDtypeStruct((1, block_count), jnp.float32)
-    sigma_out = pltpu.HBM(sigmas[0].shape, sigmas[0].dtype)
     current, ldos, *sigmas = pl.pallas_call(
         totals_kernel,
-        out_shape=(sums, sums, sigma_out, sigma_out),
-        in_specs=[VMEM] * 4,
+        out_shape=(sums, sums, written, written),
+        in_specs=[VMEM] * 4 + [ANY] * 2,
         out_specs=(VMEM, VMEM, ANY, ANY),
         scratch_shapes=[pltpu.SemaphoreType.DMA((2,))],
-        compiler_params=params(),
-    )(parts, diagonal, *sigmas)
+        input_output_aliases={4: 2, 5: 3},
+        compiler_params=params(),
+    )(parts, diagonal, less, great, *sigmas)
     sigma_l, sigma_g = [
         sigma.reshape(devices, block_count, row_count, orbitals) for sigma in sigmas
     ]

time: 36.2 us -> 35.8 us (0.989)
  blocking collectives: 29.4 us -> 28.9 us
    pallas_call x1, Pallas kernels: 0.78 us -> 1.54 us  [local(): pl.pallas_call(functools.partial(current_kernel, order, back_order), out_...]
    pallas_call x1, Pallas kernels: 1.32 us -> 0.66 us  [local(): pl.pallas_call(totals_kernel, out_shape=(sums, sums, written, written), i...]
    all_to_all x2, blocking collectives: 29.4 us -> 28.9 us  [exchange(): lax.all_to_all(chunks, 'energy', split_axis=0, concat_axis=0, tiled=True,...]
where the time goes in v8:
time: 35.8 us; the launch traced here: 35.5 us
  blocking collectives  28.9 us (81%)
  Pallas kernels  5.43 us (15%)
  between operations  0.67 us (2%)
  starting transfers between devices  0.52 us (1%)
    all_to_all x2, blocking collectives, exchange(): lax.all_to_all(chunks, 'energy', split_axis=0, concat_axis=0, tiled=True,...  28.9 us
    pallas_call x1, Pallas kernels, local(): pl.pallas_call(functools.partial(current_kernel, order, back_order), out_...  1.54 us
    pallas_call x1, Pallas kernels, load(): pl.pallas_call(functools.partial(load_kernel, edges), out_shape=(*[blocks...  1.37 us
    pallas_call x1, Pallas kernels, local(): pl.pallas_call(functools.partial(hop_kernel, outer, store_order), out_sha...  1.06 us
    pallas_call x1, Pallas kernels, local(): pl.pallas_call(functools.partial(green_kernel, swap, outer, store_order),...  0.81 us
  transfers between devices with their start and end apart: 1, of which 0 were waited for; matrix products, arithmetic and copies ran while one was open for 0% of the time, Pallas kernels for 3%

profile of v8, /device:TPU:0, one launch (start us, length us, event | category | flops | bytes accessed | tf_op | source)
XLA Modules:
  0.0 35.5 jit_solution(17641427989418163566)
XLA Ops:
  0.6 1.4 %shard_map.102 = (bf16[8,128,128]{2,1,0:T(8,128)(2,1)S(1)}, bf16[8,128,128]{2,1,0:T(8,128)(2,1)S(1)}, bf16[8,128,128]{2,1,0:T(8,128)(2,1)S(1)}, bf16[8,128,128]{...) custom-call(bf16[1,8,128,128]{3,2,1,0:T(8,128)(2,1)} %refs_0_.1, ...), custom_call_target="tpu_custom_call" | custom-call | tf_op jit(solution)/shard_map/pallas_call | solution.py:91
  2.0 0.5 %collective-permute-start = (bf16[4,128,128]{2,1,0:T(8,128)(2,1)S(1)}, bf16[4,128,128]{2,1,0:T(8,128)(2,1)S(1)}, u32[]{:S(2)}, u32[]{:S(2)}) collective-permute-start(bf16[4,128,128]{2,1,0:T(8,128)(2,1)S(1)} %get-tuple-element.34), channel_id=1, source_target_pairs={{0,1},{1,0},{2,3},{3,2},{4,5},{5,4},{6,7},{7,6},{8,9},{9,8},{10,11... | collective-permute-start | bytes 393224 | tf_op jit(solution)/shard_map/ppermute | solution.py:295
  2.5 1.1 %shard_map.103 = (f32[4,256,128]{2,1,0:T(8,128)S(1)}, bf16[16,2,64,128]{3,2,1,0:T(8,128)(2,1)S(1)}, f32[8,128]{1,0:T(8,128)S(1)}) custom-call(bf16[8,128,128]{2,1,0:T(8,128)(2,1)S(1)} %get-tuple-element.26.green, bf16[8,128,128]{2,1,0:T(8,128)(2,1)S(1)} %get-tuple-element.29.less, bf16[8,128,128]{2,1,0:T(8,128)(2,1)S(1)} %get-tuple-element.30.great, ...), custom_call_target="tpu_custom_call" | custom-call | flops 335544320 | bytes 1048576 | tf_op jit(solution)/shard_map/pallas_call | solution.py:308
  3.6 0.0 collective-permute-done.rest_2_
  3.6 0.8 %shard_map.104 = (bf16[16,2,64,128]{3,2,1,0:T(8,128)(2,1)S(1)}, f32[8,128]{1,0:T(8,128)S(1)}) custom-call(bf16[8,128,128]{2,1,0:T(8,128)(2,1)S(1)} %get-tuple-element.26.green, bf16[8,128,128]{2,1,0:T(8,128)(2,1)S(1)} %get-tuple-element.27.coupling, f32[8,128]{1,0:T(8,128)S(1)} %get-tuple-element.28.open_mask, ...), custom_call_target="tpu_custom_call", output_to_operand_aliasing={{0}: (4, {})} | custom-call | tf_op jit(solution)/shard_map/pallas_call | solution.py:324
  4.4 0.0 copy-start
  4.4 19.8 %all_to_all.10.rows = bf16[16,2,64,128]{3,2,1,0:T(8,128)(2,1)S(1)} all-to-all(bf16[16,2,64,128]{3,2,1,0:T(8,128)(2,1)S(1)} %get-tuple-element.35), channel_id=1, replica_groups={{22,0,2,4,6,8,10,12,14,16,18,20,24,26,28,30},{23,1,3,5,7,9,11,13,15,17,..., dimensions={0} | all-to-all | bytes 1048576 | tf_op jit(solution)/shard_map/all_to_all | solution.py:31
  24.2 0.0 copy-done
  24.2 1.5 %shard_map.105 = (f32[16,1,8]{2,1,0:T(1,128)S(1)}, bf16[16,64,128]{2,1,0:T(8,128)(2,1)S(1)}, bf16[16,64,128]{2,1,0:T(8,128)(2,1)S(1)}, bf16[16,64,128]{2,1,0:T(8,128)(2,1)}, bf16[16,64,128]{2,1,0:T(8,128)(2,1)}) custom-call(s32[2]{0:T(128)S(4)} %get-tuple-element.25.shift, bf16[16,2,64,128]{3,2,1,0:T(8,128)(2,1)S(1)} %all_to_all.10.rows, f32[8,128]{1,0:T(8,128)S(1)} %copy-done), custom_call_target="tpu_custom_call" | custom-call | tf_op jit(solution)/shard_map/pallas_call | solution.py:339
  25.8 9.1 %all_to_all.11.parts = f32[16,1,8]{2,1,0:T(1,128)S(1)} all-to-all(f32[16,1,8]{2,1,0:T(1,128)S(1)} %get-tuple-element.36), channel_id=1, replica_groups={{30,0,2,4,6,8,10,12,14,16,18,20,22,24,26,28},{31,1,3,5,7,9,11,13,15,17,..., dimensions={0} | all-to-all | bytes 1024 | tf_op jit(solution)/shard_map/all_to_all | solution.py:31
  34.9 0.7 %shard_map.106 = (f32[1,8]{1,0:T(1,128)}, f32[1,8]{1,0:T(1,128)}, bf16[16,64,128]{2,1,0:T(8,128)(2,1)}, bf16[16,64,128]{2,1,0:T(8,128)(2,1)}) custom-call(f32[16,1,8]{2,1,0:T(1,128)S(1)} %all_to_all.11.parts, f32[8,128]{1,0:T(8,128)S(1)} %get-tuple-element.37.diagonal, ...), custom_call_target="tpu_custom_call", output_to_operand_aliasing={{2}: (4, {}), {3}: (5, {})} | custom-call | tf_op jit(solution)/shard_map/pallas_call | solution.py:353
Async XLA Ops:
  2.0 1.6 %collective-permute-start = (bf16[4,128,128]{2,1,0:T(8,128)(2,1)S(1)}, bf16[4,128,128]{2,1,0:T(8,128)(2,1)S(1)}, u32[]{:S(2)}, u32[]{:S(2)}) collective-permute-start(bf16[4,128,128]{2,1,0:T(8,128)(2,1)S(1)} %get-tuple-element.34), channel_id=1, source_target_pairs={{0,1},{1,0},{2,3},{3,2},{4,5},{5,4},{6,7},{7,6},{8,9},{9,8},{10,11... | collective-permute-start | bytes 393224 | tf_op jit(solution)/shard_map/ppermute | solution.py:295
  4.4 19.8 %copy-start = (f32[8,128]{1,0:T(8,128)S(1)}, f32[8,128]{1,0:T(8,128)}, u32[]{:S(2)}) copy-start(f32[8,128]{1,0:T(8,128)} %strength.1) | copy-start | bytes 12292

commit v9 on v8

--- a/solution.py
+++ b/solution.py
@@ -61,8 +61,8 @@
 
 def load_kernel(edges, *refs):
     inputs, active, shift = refs[:4], refs[4], refs[5]
-    outputs, steps, open_mask = refs[6:10], refs[10], refs[11]
-    packed, counts, sems = refs[12 : 12 + len(edges)], refs[-2], refs[-1]
+    outputs, steps, open_mask, wide = refs[6:10], refs[10], refs[11], refs[12]
+    packed, counts, sems = refs[13 : 13 + len(edges)], refs[-2], refs[-1]
     blocks = [ref if ref.ndim == 3 else ref.at[0] for ref in inputs]
     pairs = [(active, counts), (shift, steps)]
     for block_of, target in zip(edges, packed):
@@ -75,6 +75,10 @@
     ]
     for copy in copies:
         copy.start()
+    pad = wide.shape[0] // 4
+    zeros = jnp.zeros((pad, *wide.shape[1:]), wide.dtype)
+    wide[0:pad] = zeros
+    wide[3 * pad :] = zeros
     for copy in copies:
         copy.wait()
     block_count = open_mask.shape[0]
@@ -83,7 +87,7 @@
     open_mask[...] = (block_ids < open_count).astype(jnp.float32)
 
 
-def load(edges, arrays, active, shift):
+def load(edges, arrays, active, shift, devices):
     _, block_count, orbitals, _ = arrays[0].shape
     blocks = held((block_count, orbitals, orbitals), jnp.bfloat16)
     edge = held((len(arrays), orbitals, orbitals), jnp.bfloat16)
@@ -94,10 +98,11 @@
             *[blocks] * len(arrays),
             pltpu.SMEM(shift.shape, shift.dtype),
             held((block_count, orbitals), jnp.float32),
+            held((2 * devices, 2, block_count * orbitals // devices, orbitals), jnp.float32),
             *[edge] * len(edges),
         ),
         in_specs=[ANY] * (len(arrays) + 2),
-        out_specs=(*[VMEM] * len(arrays), SMEM, VMEM, *[VMEM] * len(edges)),
+        out_specs=(*[VMEM] * len(arrays), SMEM, VMEM, VMEM, *[VMEM] * len(edges)),
         scratch_shapes=[
             pltpu.SMEM(active.shape, active.dtype),
             pltpu.SemaphoreType.DMA((copies,)),
@@ -105,7 +110,7 @@
         compiler_params=params(),
     )(*in_hbm(*arrays, active, shift))
     kept = len(arrays)
-    return results[:kept], results[kept], results[kept + 1], results[kept + 2 :]
+    return results[:kept], results[kept : kept + 3], results[kept + 3 :]
 
 
 def through(operator, less, great):
@@ -115,19 +120,26 @@
     return product_t(stacked, operator)
 
 
-def finish(blocks, middles, green, open_mask, outgoing, diagonal, order):
+def sandwiches(middles, green):
     orbitals = green.shape[1]
+    halves, results = [], []
+    for block, middle in enumerate(middles):
+        middle = middle.astype(jnp.bfloat16)
+        middle = jnp.concatenate([middle[:orbitals], middle[orbitals:]], 1)
+        halves.append(product(green[block], middle).astype(jnp.bfloat16))
+    for block, half in enumerate(halves):
+        stacked = jnp.concatenate([half[:, :orbitals], half[:, orbitals:]], 0)
+        results.append(product_t(stacked, green[block]))
+    return results
+
+
+def store(blocks, results, open_mask, outgoing, diagonal, order):
+    orbitals = open_mask.shape[1]
     row_ids = lax.broadcasted_iota(jnp.int32, (orbitals, orbitals), 0)
     on_diagonal = row_ids == lax.broadcasted_iota(jnp.int32, (orbitals, orbitals), 1)
-    halves, kinds = {}, {}
+    kinds = {}
     for block in blocks:
-        middle = middles[block].astype(jnp.bfloat16)
-        middle = jnp.concatenate([middle[:orbitals], middle[orbitals:]], 1)
-        halves[block] = product(green[block], middle).astype(jnp.bfloat16)
-    for block in blocks:
-        half = halves[block]
-        stacked = jnp.concatenate([half[:, :orbitals], half[:, orbitals:]], 0)
-        result = product_t(stacked, green[block]) * open_mask[block : block + 1]
+        result = results[block] * open_mask[block : block + 1]
         kinds[block] = [result[:orbitals], result[orbitals:]]
         diagonal[block : block + 1] = jnp.sum(
             jnp.where(on_diagonal, kinds[block][0] + kinds[block][1], 0.0), axis=0, keepdims=True
@@ -146,7 +158,7 @@
                     ).astype(jnp.bfloat16)
 
 
-def hop_kernel(outer, order, green, less, great, coupling, open_mask, source, outgoing, diagonal):
+def hop_kernel(outer, order, green, less, great, coupling, open_mask, partial, outgoing, diagonal):
     block_count, orbitals = green.shape[0], green.shape[1]
     blocks = range(block_count)
     hops, both, middles = [], [], []
@@ -174,31 +186,36 @@
         ]
         operators = jnp.concatenate([hops[origin][piece] for origin, piece in sent], 1)
         middles[block] = middles[block] + product_t(jnp.concatenate(stacked, 0), operators)
+    results = sandwiches(middles, green)
     for slot, block in enumerate(outer):
-        source[slot] = middles[block]
+        partial[slot] = results[block]
     inner = [block for block in blocks if block not in outer]
-    finish(inner, middles, green, open_mask, outgoing, diagonal, order)
-
-
-def green_kernel(swap, outer, order, green, coupling, open_mask, source, *rest):
+    store(inner, results, open_mask, outgoing, diagonal, order)
+
+
+def edge_kernel(swap, outer, order, green, coupling, open_mask, partial, *rest):
     (_, inner_diagonal), halos, (outgoing, diagonal) = rest[:2], rest[2:-2], rest[-2:]
     last = green.shape[0] - 1
     place = lax.axis_index("space")
-    middles = {block: source[slot] for slot, block in enumerate(outer)}
+    results = {block: partial[slot] for slot, block in enumerate(outer)}
+
+    def sent(retarded, hop, halo):
+        operator = product(retarded, hop).astype(jnp.bfloat16)
+        operator = product(operator, halo[0]).astype(jnp.bfloat16)
+        return through(operator, halo[1], halo[2])
+
     if swap:
         (halo,) = halos
-        hop = jnp.where(place == 0, coupling[last], halo[3].T)
-        edge = through(product(hop, halo[0]).astype(jnp.bfloat16), halo[1], halo[2])
-        middles[0] = middles[0] + jnp.where(place > 0, edge, 0.0)
-        middles[last] = middles[last] + jnp.where(place == 0, edge, 0.0)
+        retarded = jnp.where(place == 0, green[last], green[0])
+        edge = sent(retarded, jnp.where(place == 0, coupling[last], halo[3].T), halo)
+        results[0] = results[0] + jnp.where(place > 0, edge, 0.0)
+        results[last] = results[last] + jnp.where(place == 0, edge, 0.0)
     elif halos:
         before, after = halos
-        hop = product(before[3].T, before[0]).astype(jnp.bfloat16)
-        middles[0] = middles[0] + through(hop, before[1], before[2])
-        hop = product(coupling[last], after[0]).astype(jnp.bfloat16)
-        middles[last] = middles[last] + through(hop, after[1], after[2])
+        results[0] = results[0] + sent(green[0], before[3].T, before)
+        results[last] = results[last] + sent(green[last], coupling[last], after)
     diagonal[...] = inner_diagonal[...]
-    finish(outer, middles, green, open_mask, outgoing, diagonal, order)
+    store(outer, results, open_mask, outgoing, diagonal, order)
 
 
 def lane_sums(values):
@@ -237,14 +254,12 @@
 
 
 def current_kernel(
-    order, back_order, shift, rows, strength, parts, less, great, less_out, great_out, wide, total, sems
+    order, back_order, shift, rows, strength, _, parts, less, great, wide, *rest
 ):
+    less_out, great_out, total, sems = rest
     energies, _, row_count, orbitals = rows.shape
     block_count = total.shape[1]
     pad = energies // 2
-    edge = jnp.zeros((pad, 2, row_count, orbitals), jnp.float32)
-    wide[0:pad] = edge
-    wide[pad + energies :] = edge
     for spot, energy in enumerate(order):
         wide[pad + energy] = rows[spot].astype(jnp.float32)
     factor = spread(strength[...], row_count)
@@ -287,8 +302,12 @@
         edges = [lambda: last, lambda: 0]
     else:
         edges = []
-    arrays, shift, open_mask, packed = load(
-        edges, (green_ret, prior_less, prior_great, coupling), active_blocks, phonon_shift
+    arrays, (shift, open_mask, wide), packed = load(
+        edges,
+        (green_ret, prior_less, prior_great, coupling),
+        active_blocks,
+        phonon_shift,
+        devices,
     )
     green, less, great, coupling = arrays
     if swap:
@@ -305,7 +324,7 @@
     outer = sorted({0, 1, last - 1, last})
     store_order = order if split else None
     diagonals = held((block_count, orbitals), jnp.float32)
-    source, outgoing, diagonal = pl.pallas_call(
+    partial, outgoing, diagonal = pl.pallas_call(
         functools.partial(hop_kernel, outer, store_order),
         out_shape=(
             held((len(outer), 2 * orbitals, orbitals), jnp.float32),
@@ -322,13 +341,13 @@
         ),
     )(green, less, great, coupling, open_mask)
     outgoing, diagonal = pl.pallas_call(
-        functools.partial(green_kernel, swap, outer, store_order),
+        functools.partial(edge_kernel, swap, outer, store_order),
         out_shape=(held(out_shape, jnp.bfloat16), diagonals),
         in_specs=[VMEM] * (6 + len(halos)),
         out_specs=(VMEM, VMEM),
         input_output_aliases={4: 0},
         compiler_params=params(),
-    )(green, coupling, open_mask, source, outgoing, diagonal, *halos)
+    )(green, coupling, open_mask, partial, outgoing, diagonal, *halos)
     if not split:
         outgoing = outgoing.reshape(2, block_count, devices, row_count, orbitals)
         outgoing = jnp.stack([outgoing[:, :, device] for device in order])
@@ -336,18 +355,25 @@
     rows = exchange(outgoing, order)
     sigma_shape = (devices, block_count * row_count, orbitals)
     kept, written = held(sigma_shape, jnp.bfloat16), pltpu.HBM(sigma_shape, jnp.bfloat16)
-    parts, less, great, *sigmas = pl.pallas_call(
+    parts, less, great, _, *sigmas = pl.pallas_call(
         functools.partial(current_kernel, order, back_order),
-        out_shape=(held((devices, 1, block_count), jnp.float32), kept, kept, written, written),
-        in_specs=[SMEM, VMEM, VMEM],
-        out_specs=(VMEM, VMEM, VMEM, ANY, ANY),
+        out_shape=(
+            held((devices, 1, block_count), jnp.float32),
+            kept,
+            kept,
+            held(wide.shape, wide.dtype),
+            written,
+            written,
+        ),
+        in_specs=[SMEM, VMEM, VMEM, VMEM],
+        out_specs=(VMEM, VMEM, VMEM, VMEM, ANY, ANY),
+        input_output_aliases={3: 3},
         scratch_shapes=[
-            pltpu.VMEM((2 * devices, *rows.shape[1:]), jnp.float32),
             pltpu.VMEM((devices, block_count, orbitals), jnp.float32),
             pltpu.SemaphoreType.DMA((2,)),
         ],
         compiler_params=params(),
-    )(in_smem(shift), rows, phonon_coupling)
+    )(in_smem(shift), rows, phonon_coupling, wide)
     parts = exchange(parts, back_order)
     sums = jax.ShapeDtypeStruct((1, block_count), jnp.float32)
     current, ldos, *sigmas = pl.pallas_call(

time: 35.8 us -> 35.5 us (level)
  no operation moved by 1% of the time
where the time goes in v9:
time: 35.5 us; the launch traced here: 35.3 us
  blocking collectives  28.8 us (81%)
  Pallas kernels  5.2 us (15%)
  between operations  0.68 us (2%)
  starting transfers between devices  0.52 us (1%)
    all_to_all x2, blocking collectives, exchange(): lax.all_to_all(chunks, 'energy', split_axis=0, concat_axis=0, tiled=True,...  28.8 us
    pallas_call x1, Pallas kernels, local(): pl.pallas_call(functools.partial(current_kernel, order, back_order), out_...  1.48 us
    pallas_call x1, Pallas kernels, load(): pl.pallas_call(functools.partial(load_kernel, edges), out_shape=(*[blocks...  1.37 us
    pallas_call x1, Pallas kernels, local(): pl.pallas_call(functools.partial(hop_kernel, outer, store_order), out_sha...  1.09 us
  transfers between devices with their start and end apart: 1, of which 0 were waited for; matrix products, arithmetic and copies ran while one was open for 0% of the time, Pallas kernels for 3%

profile of v9, /device:TPU:0, one launch (start us, length us, event | category | flops | bytes accessed | tf_op | source)
XLA Modules:
  0.0 35.3 jit_solution(13554879300960144543)
XLA Ops:
  0.6 1.4 %shard_map.102 = (bf16[8,128,128]{2,1,0:T(8,128)(2,1)S(1)}, bf16[8,128,128]{2,1,0:T(8,128)(2,1)S(1)}, bf16[8,128,128]{2,1,0:T(8,128)(2,1)S(1)}, bf16[8,128,128]{...) custom-call(bf16[1,8,128,128]{3,2,1,0:T(8,128)(2,1)} %refs_0_.1, ...), custom_call_target="tpu_custom_call" | custom-call | tf_op jit(solution)/shard_map/pallas_call | solution.py:95
  2.0 0.0 copy-start
  2.0 0.5 %collective-permute-start = (bf16[4,128,128]{2,1,0:T(8,128)(2,1)S(1)}, bf16[4,128,128]{2,1,0:T(8,128)(2,1)S(1)}, u32[]{:S(2)}, u32[]{:S(2)}) collective-permute-start(bf16[4,128,128]{2,1,0:T(8,128)(2,1)S(1)} %get-tuple-element.35), channel_id=1, source_target_pairs={{0,1},{1,0},{2,3},{3,2},{4,5},{5,4},{6,7},{7,6},{8,9},{9,8},{10,11... | collective-permute-start | bytes 393224 | tf_op jit(solution)/shard_map/ppermute | solution.py:314
  2.5 1.1 %shard_map.103 = (f32[4,256,128]{2,1,0:T(8,128)S(1)}, bf16[16,2,64,128]{3,2,1,0:T(8,128)(2,1)S(1)}, f32[8,128]{1,0:T(8,128)S(1)}) custom-call(bf16[8,128,128]{2,1,0:T(8,128)(2,1)S(1)} %get-tuple-element.27.green, bf16[8,128,128]{2,1,0:T(8,128)(2,1)S(1)} %get-tuple-element.30.less, bf16[8,128,128]{2,1,0:T(8,128)(2,1)S(1)} %get-tuple-element.31.great, ...), custom_call_target="tpu_custom_call" | custom-call | flops 335544320 | bytes 1048576 | tf_op jit(solution)/shard_map/pallas_call | solution.py:327
  3.6 0.0 collective-permute-done.rest_2_
  3.6 0.6 %shard_map.104 = (bf16[16,2,64,128]{3,2,1,0:T(8,128)(2,1)S(1)}, f32[8,128]{1,0:T(8,128)S(1)}) custom-call(bf16[8,128,128]{2,1,0:T(8,128)(2,1)S(1)} %get-tuple-element.27.green, bf16[8,128,128]{2,1,0:T(8,128)(2,1)S(1)} %get-tuple-element.28.coupling, f32[8,128]{1,0:T(8,128)S(1)} %get-tuple-element.29.open_mask, ...), custom_call_target="tpu_custom_call", output_to_operand_aliasing={{0}: (4, {})} | custom-call | tf_op jit(solution)/shard_map/pallas_call | solution.py:343
  4.3 19.8 %all_to_all.10.rows = bf16[16,2,64,128]{3,2,1,0:T(8,128)(2,1)S(1)} all-to-all(bf16[16,2,64,128]{3,2,1,0:T(8,128)(2,1)S(1)} %get-tuple-element.36), channel_id=1, replica_groups={{22,0,2,4,6,8,10,12,14,16,18,20,24,26,28,30},{23,1,3,5,7,9,11,13,15,17,..., dimensions={0} | all-to-all | bytes 1048576 | tf_op jit(solution)/shard_map/all_to_all | solution.py:31
  24.0 0.0 copy-done
  24.0 1.5 %shard_map.105 = (f32[16,1,8]{2,1,0:T(1,128)S(1)}, bf16[16,64,128]{2,1,0:T(8,128)(2,1)S(1)}, bf16[16,64,128]{2,1,0:T(8,128)(2,1)S(1)}, f32[32,2,64,128]{3,2,1,0:...) custom-call(s32[2]{0:T(128)S(4)} %get-tuple-element.26.shift, ...), custom_call_target="tpu_custom_call", output_to_operand_aliasing={{3}: (3, {})} | custom-call | tf_op jit(solution)/shard_map/pallas_call | solution.py:358
  25.5 9.1 %all_to_all.11.parts = f32[16,1,8]{2,1,0:T(1,128)S(1)} all-to-all(f32[16,1,8]{2,1,0:T(1,128)S(1)} %get-tuple-element.38), channel_id=1, replica_groups={{30,0,2,4,6,8,10,12,14,16,18,20,22,24,26,28},{31,1,3,5,7,9,11,13,15,17,..., dimensions={0} | all-to-all | bytes 1024 | tf_op jit(solution)/shard_map/all_to_all | solution.py:31
  34.6 0.7 %shard_map.106 = (f32[1,8]{1,0:T(1,128)}, f32[1,8]{1,0:T(1,128)}, bf16[16,64,128]{2,1,0:T(8,128)(2,1)}, bf16[16,64,128]{2,1,0:T(8,128)(2,1)}) custom-call(f32[16,1,8]{2,1,0:T(1,128)S(1)} %all_to_all.11.parts, f32[8,128]{1,0:T(8,128)S(1)} %get-tuple-element.39.diagonal, ...), custom_call_target="tpu_custom_call", output_to_operand_aliasing={{2}: (4, {}), {3}: (5, {})} | custom-call | tf_op jit(solution)/shard_map/pallas_call | solution.py:379
Async XLA Ops:
  2.0 22.0 %copy-start = (f32[8,128]{1,0:T(8,128)S(1)}, f32[8,128]{1,0:T(8,128)}, u32[]{:S(2)}) copy-start(f32[8,128]{1,0:T(8,128)} %strength.1) | copy-start | bytes 12292
  2.0 1.6 %collective-permute-start = (bf16[4,128,128]{2,1,0:T(8,128)(2,1)S(1)}, bf16[4,128,128]{2,1,0:T(8,128)(2,1)S(1)}, u32[]{:S(2)}, u32[]{:S(2)}) collective-permute-start(bf16[4,128,128]{2,1,0:T(8,128)(2,1)S(1)} %get-tuple-element.35), channel_id=1, source_target_pairs={{0,1},{1,0},{2,3},{3,2},{4,5},{5,4},{6,7},{7,6},{8,9},{9,8},{10,11... | collective-permute-start | bytes 393224 | tf_op jit(solution)/shard_map/ppermute | solution.py:314

commit v10 on v9

--- a/solution.py
+++ b/solution.py
@@ -225,28 +225,30 @@
     return product_t(ones, jnp.concatenate([coarse, fine], 1))[0:1]
 
 
-def copy_out(less, great, less_out, great_out, sems):
+def totals_kernel(
+    parts, diagonal, less, great, current_out, density_out, less_out, great_out, current, density, sems
+):
+    pairs = (
+        (less, less_out),
+        (great, great_out),
+        (density, density_out),
+        (current, current_out),
+    )
     copies = [
-        pltpu.make_async_copy(less, less_out, sems.at[0]),
-        pltpu.make_async_copy(great, great_out, sems.at[1]),
+        pltpu.make_async_copy(origin, target, sems.at[index])
+        for index, (origin, target) in enumerate(pairs)
     ]
-    for copy in copies:
-        copy.start()
-    for copy in copies:
-        copy.wait()
-
-
-def has_time():
-    return lax.axis_index("energy") == 0
-
-
-def totals_kernel(parts, diagonal, less, great, _, __, current, density, *outputs):
     total = parts[0]
     for spot in range(1, parts.shape[0]):
         total = total + parts[spot]
     current[...] = total
+    copies[3].start()
+    copies[0].start()
+    copies[1].start()
     density[...] = lane_sums(diagonal[...]) / diagonal.shape[1]
-    pl.when(jnp.logical_not(has_time()))(functools.partial(copy_out, less, great, *outputs))
+    copies[2].start()
+    for copy in copies:
+        copy.wait()
 
 
 def spread(strength, rows):
@@ -254,9 +256,8 @@
 
 
 def current_kernel(
-    order, back_order, shift, rows, strength, _, parts, less, great, wide, *rest
+    order, back_order, shift, rows, strength, _, parts, less, great, wide, total
 ):
-    less_out, great_out, total, sems = rest
     energies, _, row_count, orbitals = rows.shape
     block_count = total.shape[1]
     pad = energies // 2
@@ -284,7 +285,6 @@
     flat = lane_sums(total[...].reshape(energies * block_count, orbitals))
     for spot, energy in enumerate(back_order):
         parts[spot] = flat[:, energy * block_count : (energy + 1) * block_count]
-    pl.when(has_time())(functools.partial(copy_out, less, great, less_out, great_out, sems))
 
 
 def local(
@@ -355,36 +355,33 @@
     rows = exchange(outgoing, order)
     sigma_shape = (devices, block_count * row_count, orbitals)
     kept, written = held(sigma_shape, jnp.bfloat16), pltpu.HBM(sigma_shape, jnp.bfloat16)
-    parts, less, great, _, *sigmas = pl.pallas_call(
+    parts, less, great, _ = pl.pallas_call(
         functools.partial(current_kernel, order, back_order),
         out_shape=(
             held((devices, 1, block_count), jnp.float32),
             kept,
             kept,
             held(wide.shape, wide.dtype),
-            written,
-            written,
         ),
         in_specs=[SMEM, VMEM, VMEM, VMEM],
-        out_specs=(VMEM, VMEM, VMEM, VMEM, ANY, ANY),
+        out_specs=(VMEM, VMEM, VMEM, VMEM),
         input_output_aliases={3: 3},
-        scratch_shapes=[
-            pltpu.VMEM((devices, block_count, orbitals), jnp.float32),
-            pltpu.SemaphoreType.DMA((2,)),
-        ],
+        scratch_shapes=[pltpu.VMEM((devices, block_count, orbitals), jnp.float32)],
         compiler_params=params(),
     )(in_smem(shift), rows, phonon_coupling, wide)
     parts = exchange(parts, back_order)
-    sums = jax.ShapeDtypeStruct((1, block_count), jnp.float32)
+    sums = pltpu.HBM((1, block_count), jnp.float32)
     current, ldos, *sigmas = pl.pallas_call(
         totals_kernel,
         out_shape=(sums, sums, written, written),
-        in_specs=[VMEM] * 4 + [ANY] * 2,
-        out_specs=(VMEM, VMEM, ANY, ANY),
-        scratch_shapes=[pltpu.SemaphoreType.DMA((2,))],
-        input_output_aliases={4: 2, 5: 3},
+        in_specs=[VMEM] * 4,
+        out_specs=[ANY] * 4,
+        scratch_shapes=[
+            *[pltpu.VMEM((1, block_count), jnp.float32)] * 2,
+            pltpu.SemaphoreType.DMA((4,)),
+        ],
         compiler_params=params(),
-    )(parts, diagonal, less, great, *sigmas)
+    )(parts, diagonal, less, great)
     sigma_l, sigma_g = [
         sigma.reshape(devices, block_count, row_count, orbitals) for sigma in sigmas
     ]

time: 35.5 us -> 35.5 us (level)
  blocking collectives: 28.8 us -> 29.4 us
  Pallas kernels: 5.2 us -> 4.63 us
    pallas_call x1, Pallas kernels: 1.48 us -> 0.72 us  [local(): pl.pallas_call(functools.partial(current_kernel, order, back_order), out_...]
    all_to_all x2, blocking collectives: 28.8 us -> 29.4 us  [exchange(): lax.all_to_all(chunks, 'energy', split_axis=0, concat_axis=0, tiled=True,...]
where the time goes in v10:
time: 35.5 us; the launch traced here: 35.3 us
  blocking collectives  29.4 us (83%)
  Pallas kernels  4.63 us (13%)
  between operations  0.67 us (2%)
  starting transfers between devices  0.52 us (1%)
    all_to_all x2, blocking collectives, exchange(): lax.all_to_all(chunks, 'energy', split_axis=0, concat_axis=0, tiled=True,...  29.4 us
    pallas_call x1, Pallas kernels, load(): pl.pallas_call(functools.partial(load_kernel, edges), out_shape=(*[blocks...  1.37 us
    pallas_call x1, Pallas kernels, local(): pl.pallas_call(functools.partial(hop_kernel, outer, store_order), out_sha...  1.09 us
    pallas_call x1, Pallas kernels, local(): pl.pallas_call(totals_kernel, out_shape=(sums, sums, written, written), i...  0.85 us
    pallas_call x1, Pallas kernels, local(): pl.pallas_call(functools.partial(current_kernel, order, back_order), out_...  0.72 us
  transfers between devices with their start and end apart: 1, of which 0 were waited for; matrix products, arithmetic and copies ran while one was open for 0% of the time, Pallas kernels for 3%

profile of v10, /device:TPU:0, one launch (start us, length us, event | category | flops | bytes accessed | tf_op | source)
XLA Modules:
  0.0 35.3 jit_solution(10590886237545863626)
XLA Ops:
  0.6 1.4 %shard_map.102 = (bf16[8,128,128]{2,1,0:T(8,128)(2,1)S(1)}, bf16[8,128,128]{2,1,0:T(8,128)(2,1)S(1)}, bf16[8,128,128]{2,1,0:T(8,128)(2,1)S(1)}, bf16[8,128,128]{...) custom-call(bf16[1,8,128,128]{3,2,1,0:T(8,128)(2,1)} %refs_0_.1, ...), custom_call_target="tpu_custom_call" | custom-call | tf_op jit(solution)/shard_map/pallas_call | solution.py:95
  2.0 0.0 copy-start
  2.0 0.5 %collective-permute-start = (bf16[4,128,128]{2,1,0:T(8,128)(2,1)S(1)}, bf16[4,128,128]{2,1,0:T(8,128)(2,1)S(1)}, u32[]{:S(2)}, u32[]{:S(2)}) collective-permute-start(bf16[4,128,128]{2,1,0:T(8,128)(2,1)S(1)} %get-tuple-element.33), channel_id=1, source_target_pairs={{0,1},{1,0},{2,3},{3,2},{4,5},{5,4},{6,7},{7,6},{8,9},{9,8},{10,11... | collective-permute-start | bytes 393224 | tf_op jit(solution)/shard_map/ppermute | solution.py:314
  2.5 1.1 %shard_map.103 = (f32[4,256,128]{2,1,0:T(8,128)S(1)}, bf16[16,2,64,128]{3,2,1,0:T(8,128)(2,1)S(1)}, f32[8,128]{1,0:T(8,128)S(1)}) custom-call(bf16[8,128,128]{2,1,0:T(8,128)(2,1)S(1)} %get-tuple-element.25.green, bf16[8,128,128]{2,1,0:T(8,128)(2,1)S(1)} %get-tuple-element.28.less, bf16[8,128,128]{2,1,0:T(8,128)(2,1)S(1)} %get-tuple-element.29.great, ...), custom_call_target="tpu_custom_call" | custom-call | flops 335544320 | bytes 1048576 | tf_op jit(solution)/shard_map/pallas_call | solution.py:327
  3.6 0.0 collective-permute-done.rest_2_
  3.6 0.6 %shard_map.104 = (bf16[16,2,64,128]{3,2,1,0:T(8,128)(2,1)S(1)}, f32[8,128]{1,0:T(8,128)S(1)}) custom-call(bf16[8,128,128]{2,1,0:T(8,128)(2,1)S(1)} %get-tuple-element.25.green, bf16[8,128,128]{2,1,0:T(8,128)(2,1)S(1)} %get-tuple-element.26.coupling, f32[8,128]{1,0:T(8,128)S(1)} %get-tuple-element.27.open_mask, ...), custom_call_target="tpu_custom_call", output_to_operand_aliasing={{0}: (4, {})} | custom-call | tf_op jit(solution)/shard_map/pallas_call | solution.py:343
  4.3 19.8 %all_to_all.10.rows = bf16[16,2,64,128]{3,2,1,0:T(8,128)(2,1)S(1)} all-to-all(bf16[16,2,64,128]{3,2,1,0:T(8,128)(2,1)S(1)} %get-tuple-element.34), channel_id=1, replica_groups={{22,0,2,4,6,8,10,12,14,16,18,20,24,26,28,30},{23,1,3,5,7,9,11,13,15,17,..., dimensions={0} | all-to-all | bytes 1048576 | tf_op jit(solution)/shard_map/all_to_all | solution.py:31
  24.0 0.0 copy-done
  24.0 0.7 %shard_map.105 = (f32[16,1,8]{2,1,0:T(1,128)S(1)}, bf16[16,64,128]{2,1,0:T(8,128)(2,1)S(1)}, bf16[16,64,128]{2,1,0:T(8,128)(2,1)S(1)}, f32[32,2,64,128]{3,2,1,0:T(8,128)S(1)}) custom-call(s32[2]{0:T(128)S(4)} %get-tuple-element.24.shift, bf16[16,2,64,128]{3,2,1,0:T(8,128)(2,1)S(1)} %all_to_all.10.rows, ...), custom_call_target="tpu_custom_call", output_to_operand_aliasing={{3}: (3, {})} | custom-call | tf_op jit(solution)/shard_map/pallas_call | solution.py:358
  24.8 9.7 %all_to_all.11.parts = f32[16,1,8]{2,1,0:T(1,128)S(1)} all-to-all(f32[16,1,8]{2,1,0:T(1,128)S(1)} %get-tuple-element.36), channel_id=1, replica_groups={{30,0,2,4,6,8,10,12,14,16,18,20,22,24,26,28},{31,1,3,5,7,9,11,13,15,17,..., dimensions={0} | all-to-all | bytes 1024 | tf_op jit(solution)/shard_map/all_to_all | solution.py:31
  34.4 0.8 %shard_map.106 = (f32[1,8]{1,0:T(1,128)}, f32[1,8]{1,0:T(1,128)}, bf16[16,64,128]{2,1,0:T(8,128)(2,1)}, bf16[16,64,128]{2,1,0:T(8,128)(2,1)}) custom-call(f32[16,1,8]{2,1,0:T(1,128)S(1)} %all_to_all.11.parts, f32[8,128]{1,0:T(8,128)S(1)} %get-tuple-element.37.diagonal, bf16[16,64,128]{2,1,0:T(8,128)(2,1)S(1)} %get-tuple-element.38.less, ...), custom_call_target="tpu_custom_call" | custom-call | tf_op jit(solution)/shard_map/pallas_call | solution.py:374
Async XLA Ops:
  2.0 22.0 %copy-start = (f32[8,128]{1,0:T(8,128)S(1)}, f32[8,128]{1,0:T(8,128)}, u32[]{:S(2)}) copy-start(f32[8,128]{1,0:T(8,128)} %strength.1) | copy-start | bytes 12292
  2.0 1.6 %collective-permute-start = (bf16[4,128,128]{2,1,0:T(8,128)(2,1)S(1)}, bf16[4,128,128]{2,1,0:T(8,128)(2,1)S(1)}, u32[]{:S(2)}, u32[]{:S(2)}) collective-permute-start(bf16[4,128,128]{2,1,0:T(8,128)(2,1)S(1)} %get-tuple-element.33), channel_id=1, source_target_pairs={{0,1},{1,0},{2,3},{3,2},{4,5},{5,4},{6,7},{7,6},{8,9},{9,8},{10,11... | collective-permute-start | bytes 393224 | tf_op jit(solution)/shard_map/ppermute | solution.py:314

commit v11 on v9

--- a/solution.py
+++ b/solution.py
@@ -240,13 +240,24 @@
     return lax.axis_index("energy") == 0
 
 
-def totals_kernel(parts, diagonal, less, great, _, __, current, density, *outputs):
+def totals_kernel(
+    parts, diagonal, less, great, _, __, current_out, density_out, less_out, great_out, *scratch
+):
+    current, density, sums_sems, sems = scratch
     total = parts[0]
     for spot in range(1, parts.shape[0]):
         total = total + parts[spot]
     current[...] = total
+    first = pltpu.make_async_copy(current, current_out, sums_sems.at[0])
+    first.start()
     density[...] = lane_sums(diagonal[...]) / diagonal.shape[1]
-    pl.when(jnp.logical_not(has_time()))(functools.partial(copy_out, less, great, *outputs))
+    second = pltpu.make_async_copy(density, density_out, sums_sems.at[1])
+    second.start()
+    pl.when(jnp.logical_not(has_time()))(
+        functools.partial(copy_out, less, great, less_out, great_out, sems)
+    )
+    first.wait()
+    second.wait()
 
 
 def spread(strength, rows):
@@ -375,13 +386,16 @@
         compiler_params=params(),
     )(in_smem(shift), rows, phonon_coupling, wide)
     parts = exchange(parts, back_order)
-    sums = jax.ShapeDtypeStruct((1, block_count), jnp.float32)
+    sums = pltpu.HBM((1, block_count), jnp.float32)
     current, ldos, *sigmas = pl.pallas_call(
         totals_kernel,
         out_shape=(sums, sums, written, written),
         in_specs=[VMEM] * 4 + [ANY] * 2,
-        out_specs=(VMEM, VMEM, ANY, ANY),
-        scratch_shapes=[pltpu.SemaphoreType.DMA((2,))],
+        out_specs=[ANY] * 4,
+        scratch_shapes=[
+            *[pltpu.VMEM((1, block_count), jnp.float32)] * 2,
+            *[pltpu.SemaphoreType.DMA((2,))] * 2,
+        ],
         input_output_aliases={4: 2, 5: 3},
         compiler_params=params(),
     )(parts, diagonal, less, great, *sigmas)

time: 35.5 us -> 35.5 us (level)
  no operation moved by 1% of the time
where the time goes in v11:
time: 35.5 us; the launch traced here: 35.3 us
  blocking collectives  28.8 us (81%)
  Pallas kernels  5.21 us (15%)
  between operations  0.68 us (2%)
  starting transfers between devices  0.52 us (1%)
    all_to_all x2, blocking collectives, exchange(): lax.all_to_all(chunks, 'energy', split_axis=0, concat_axis=0, tiled=True,...  28.8 us
    pallas_call x1, Pallas kernels, local(): pl.pallas_call(functools.partial(current_kernel, order, back_order), out_...  1.48 us
    pallas_call x1, Pallas kernels, load(): pl.pallas_call(functools.partial(load_kernel, edges), out_shape=(*[blocks...  1.37 us
    pallas_call x1, Pallas kernels, local(): pl.pallas_call(functools.partial(hop_kernel, outer, store_order), out_sha...  1.09 us
  transfers between devices with their start and end apart: 1, of which 0 were waited for; matrix products, arithmetic and copies ran while one was open for 0% of the time, Pallas kernels for 3%

profile of v11, /device:TPU:0, one launch (start us, length us, event | category | flops | bytes accessed | tf_op | source)
XLA Modules:
  0.0 35.3 jit_solution(199835611823790524)
XLA Ops:
  0.6 1.4 %shard_map.102 = (bf16[8,128,128]{2,1,0:T(8,128)(2,1)S(1)}, bf16[8,128,128]{2,1,0:T(8,128)(2,1)S(1)}, bf16[8,128,128]{2,1,0:T(8,128)(2,1)S(1)}, bf16[8,128,128]{...) custom-call(bf16[1,8,128,128]{3,2,1,0:T(8,128)(2,1)} %refs_0_.1, ...), custom_call_target="tpu_custom_call" | custom-call | tf_op jit(solution)/shard_map/pallas_call | solution.py:95
  2.0 0.0 copy-start
  2.0 0.5 %collective-permute-start = (bf16[4,128,128]{2,1,0:T(8,128)(2,1)S(1)}, bf16[4,128,128]{2,1,0:T(8,128)(2,1)S(1)}, u32[]{:S(2)}, u32[]{:S(2)}) collective-permute-start(bf16[4,128,128]{2,1,0:T(8,128)(2,1)S(1)} %get-tuple-element.35), channel_id=1, source_target_pairs={{0,1},{1,0},{2,3},{3,2},{4,5},{5,4},{6,7},{7,6},{8,9},{9,8},{10,11... | collective-permute-start | bytes 393224 | tf_op jit(solution)/shard_map/ppermute | solution.py:325
  2.5 1.1 %shard_map.103 = (f32[4,256,128]{2,1,0:T(8,128)S(1)}, bf16[16,2,64,128]{3,2,1,0:T(8,128)(2,1)S(1)}, f32[8,128]{1,0:T(8,128)S(1)}) custom-call(bf16[8,128,128]{2,1,0:T(8,128)(2,1)S(1)} %get-tuple-element.27.green, bf16[8,128,128]{2,1,0:T(8,128)(2,1)S(1)} %get-tuple-element.30.less, bf16[8,128,128]{2,1,0:T(8,128)(2,1)S(1)} %get-tuple-element.31.great, ...), custom_call_target="tpu_custom_call" | custom-call | flops 335544320 | bytes 1048576 | tf_op jit(solution)/shard_map/pallas_call | solution.py:338
  3.6 0.0 collective-permute-done.rest_2_
  3.6 0.6 %shard_map.104 = (bf16[16,2,64,128]{3,2,1,0:T(8,128)(2,1)S(1)}, f32[8,128]{1,0:T(8,128)S(1)}) custom-call(bf16[8,128,128]{2,1,0:T(8,128)(2,1)S(1)} %get-tuple-element.27.green, bf16[8,128,128]{2,1,0:T(8,128)(2,1)S(1)} %get-tuple-element.28.coupling, f32[8,128]{1,0:T(8,128)S(1)} %get-tuple-element.29.open_mask, ...), custom_call_target="tpu_custom_call", output_to_operand_aliasing={{0}: (4, {})} | custom-call | tf_op jit(solution)/shard_map/pallas_call | solution.py:354
  4.3 19.8 %all_to_all.10.rows = bf16[16,2,64,128]{3,2,1,0:T(8,128)(2,1)S(1)} all-to-all(bf16[16,2,64,128]{3,2,1,0:T(8,128)(2,1)S(1)} %get-tuple-element.36), channel_id=1, replica_groups={{22,0,2,4,6,8,10,12,14,16,18,20,24,26,28,30},{23,1,3,5,7,9,11,13,15,17,..., dimensions={0} | all-to-all | bytes 1048576 | tf_op jit(solution)/shard_map/all_to_all | solution.py:31
  24.0 0.0 copy-done
  24.0 1.5 %shard_map.105 = (f32[16,1,8]{2,1,0:T(1,128)S(1)}, bf16[16,64,128]{2,1,0:T(8,128)(2,1)S(1)}, bf16[16,64,128]{2,1,0:T(8,128)(2,1)S(1)}, f32[32,2,64,128]{3,2,1,0:...) custom-call(s32[2]{0:T(128)S(4)} %get-tuple-element.26.shift, ...), custom_call_target="tpu_custom_call", output_to_operand_aliasing={{3}: (3, {})} | custom-call | tf_op jit(solution)/shard_map/pallas_call | solution.py:369
  25.5 9.1 %all_to_all.11.parts = f32[16,1,8]{2,1,0:T(1,128)S(1)} all-to-all(f32[16,1,8]{2,1,0:T(1,128)S(1)} %get-tuple-element.38), channel_id=1, replica_groups={{30,0,2,4,6,8,10,12,14,16,18,20,22,24,26,28},{31,1,3,5,7,9,11,13,15,17,..., dimensions={0} | all-to-all | bytes 1024 | tf_op jit(solution)/shard_map/all_to_all | solution.py:31
  34.6 0.7 %shard_map.106 = (f32[1,8]{1,0:T(1,128)}, f32[1,8]{1,0:T(1,128)}, bf16[16,64,128]{2,1,0:T(8,128)(2,1)}, bf16[16,64,128]{2,1,0:T(8,128)(2,1)}) custom-call(f32[16,1,8]{2,1,0:T(1,128)S(1)} %all_to_all.11.parts, f32[8,128]{1,0:T(8,128)S(1)} %get-tuple-element.39.diagonal, ...), custom_call_target="tpu_custom_call", output_to_operand_aliasing={{2}: (4, {}), {3}: (5, {})} | custom-call | tf_op jit(solution)/shard_map/pallas_call | solution.py:390
Async XLA Ops:
  2.0 22.0 %copy-start = (f32[8,128]{1,0:T(8,128)S(1)}, f32[8,128]{1,0:T(8,128)}, u32[]{:S(2)}) copy-start(f32[8,128]{1,0:T(8,128)} %strength.1) | copy-start | bytes 12292
  2.0 1.6 %collective-permute-start = (bf16[4,128,128]{2,1,0:T(8,128)(2,1)S(1)}, bf16[4,128,128]{2,1,0:T(8,128)(2,1)S(1)}, u32[]{:S(2)}, u32[]{:S(2)}) collective-permute-start(bf16[4,128,128]{2,1,0:T(8,128)(2,1)S(1)} %get-tuple-element.35), channel_id=1, source_target_pairs={{0,1},{1,0},{2,3},{3,2},{4,5},{5,4},{6,7},{7,6},{8,9},{9,8},{10,11... | collective-permute-start | bytes 393224 | tf_op jit(solution)/shard_map/ppermute | solution.py:325

commit v12 on v9

--- a/solution.py
+++ b/solution.py
@@ -61,14 +61,14 @@
 
 def load_kernel(edges, *refs):
     inputs, active, shift = refs[:4], refs[4], refs[5]
-    outputs, steps, open_mask, wide = refs[6:10], refs[10], refs[11], refs[12]
-    packed, counts, sems = refs[13 : 13 + len(edges)], refs[-2], refs[-1]
+    outputs, steps, open_mask, wide = refs[6:9], refs[9], refs[10], refs[11]
+    packed, counts, sems = refs[12 : 12 + len(edges)], refs[-2], refs[-1]
     blocks = [ref if ref.ndim == 3 else ref.at[0] for ref in inputs]
     pairs = [(active, counts), (shift, steps)]
     for block_of, target in zip(edges, packed):
         block = block_of()
         pairs += [(ref.at[block], target.at[slot]) for slot, ref in enumerate(blocks)]
-    pairs += list(zip(blocks, outputs))
+    pairs += list(zip((blocks[0], blocks[1], blocks[3]), outputs))
     copies = [
         pltpu.make_async_copy(origin, target, sems.at[index])
         for index, (origin, target) in enumerate(pairs)
@@ -95,21 +95,21 @@
     results = pl.pallas_call(
         functools.partial(load_kernel, edges),
         out_shape=(
-            *[blocks] * len(arrays),
+            *[blocks] * 3,
             pltpu.SMEM(shift.shape, shift.dtype),
             held((block_count, orbitals), jnp.float32),
             held((2 * devices, 2, block_count * orbitals // devices, orbitals), jnp.float32),
             *[edge] * len(edges),
         ),
         in_specs=[ANY] * (len(arrays) + 2),
-        out_specs=(*[VMEM] * len(arrays), SMEM, VMEM, VMEM, *[VMEM] * len(edges)),
+        out_specs=(*[VMEM] * 3, SMEM, VMEM, VMEM, *[VMEM] * len(edges)),
         scratch_shapes=[
             pltpu.SMEM(active.shape, active.dtype),
             pltpu.SemaphoreType.DMA((copies,)),
         ],
         compiler_params=params(),
     )(*in_hbm(*arrays, active, shift))
-    kept = len(arrays)
+    kept = 3
     return results[:kept], results[kept : kept + 3], results[kept + 3 :]
 
 
@@ -309,7 +309,8 @@
         phonon_shift,
         devices,
     )
-    green, less, great, coupling = arrays
+    green, less, coupling = arrays
+    great = prior_great[0]
     if swap:
         halos = (lax.ppermute(packed[0], "space", [(0, 1), (1, 0)]),)
     else:

time: 35.5 us -> 36.1 us (1.017)
  local copies, waits for them, and re-layouts: 0.01 us -> 0.96 us
    unnamed x2 -> x4, local copies, waits for them, and re-layouts: 0.01 us -> 0.96 us
where the time goes in v12:
time: 36.1 us; the launch traced here: 35.9 us
  blocking collectives  28.6 us (79%)
  Pallas kernels  5.14 us (14%)
  local copies, waits for them, and re-layouts  0.96 us (3%)
  between operations  0.68 us (2%)
  starting transfers between devices  0.52 us (1%)
    all_to_all x2, blocking collectives, exchange(): lax.all_to_all(chunks, 'energy', split_axis=0, concat_axis=0, tiled=True,...  28.6 us
    pallas_call x1, Pallas kernels, local(): pl.pallas_call(functools.partial(current_kernel, order, back_order), out_...  1.48 us
    pallas_call x1, Pallas kernels, load(): pl.pallas_call(functools.partial(load_kernel, edges), out_shape=(*[blocks...  1.32 us
    pallas_call x1, Pallas kernels, local(): pl.pallas_call(functools.partial(hop_kernel, outer, store_order), out_sha...  1.08 us
    unnamed x4, local copies, waits for them, and re-layouts  0.96 us
  transfers between devices with their start and end apart: 1, of which 0 were waited for; matrix products, arithmetic and copies ran while one was open for 0% of the time, Pallas kernels for 3%

profile of v12, /device:TPU:0, one launch (start us, length us, event | category | flops | bytes accessed | tf_op | source)
XLA Modules:
  0.0 35.9 jit_solution(12393599065731767909)
XLA Ops:
  0.6 1.3 %shard_map.102 = (bf16[8,128,128]{2,1,0:T(8,128)(2,1)S(1)}, bf16[8,128,128]{2,1,0:T(8,128)(2,1)S(1)}, bf16[8,128,128]{2,1,0:T(8,128)(2,1)S(1)}, s32[2]{0:T(128)S...) custom-call(bf16[1,8,128,128]{3,2,1,0:T(8,128)(2,1)} %refs_0_.1, ...), custom_call_target="tpu_custom_call" | custom-call | tf_op jit(solution)/shard_map/pallas_call | solution.py:95
  2.0 0.0 copy-start.1
  2.0 0.5 %collective-permute-start = (bf16[4,128,128]{2,1,0:T(8,128)(2,1)S(1)}, bf16[4,128,128]{2,1,0:T(8,128)(2,1)S(1)}, u32[]{:S(2)}, u32[]{:S(2)}) collective-permute-start(bf16[4,128,128]{2,1,0:T(8,128)(2,1)S(1)} %get-tuple-element.33), channel_id=1, source_target_pairs={{0,1},{1,0},{2,3},{3,2},{4,5},{5,4},{6,7},{7,6},{8,9},{9,8},{10,11... | collective-permute-start | bytes 393224 | tf_op jit(solution)/shard_map/ppermute | solution.py:315
  2.5 0.0 copy-start
  2.5 0.9 %copy-done = bf16[1,8,128,128]{3,2,1,0:T(8,128)(2,1)S(1)} copy-done((bf16[1,8,128,128]{3,2,1,0:T(8,128)(2,1)S(1)}, bf16[1,8,128,128]{3,2,1,0:T(8,128)(2,1)}, u32[]{:S(2)}) %copy-start) | copy-done | bytes 262168
  3.4 1.1 %shard_map.103 = (f32[4,256,128]{2,1,0:T(8,128)S(1)}, bf16[16,2,64,128]{3,2,1,0:T(8,128)(2,1)S(1)}, f32[8,128]{1,0:T(8,128)S(1)}) custom-call(bf16[8,128,128]{2,1,0:T(8,128)(2,1)S(1)} %get-tuple-element.26.green, bf16[8,128,128]{2,1,0:T(8,128)(2,1)S(1)} %get-tuple-element.29.less, bf16[8,128,128]{2,1,0:T(8,128)(2,1)S(1)} %bitcast.3, ...), custom_call_target="tpu_custom_call" | custom-call | flops 335544320 | bytes 1048576 | tf_op jit(solution)/shard_map/pallas_call | solution.py:328
  4.5 0.0 collective-permute-done.rest_2_
  4.5 0.6 %shard_map.104 = (bf16[16,2,64,128]{3,2,1,0:T(8,128)(2,1)S(1)}, f32[8,128]{1,0:T(8,128)S(1)}) custom-call(bf16[8,128,128]{2,1,0:T(8,128)(2,1)S(1)} %get-tuple-element.26.green, bf16[8,128,128]{2,1,0:T(8,128)(2,1)S(1)} %get-tuple-element.27.coupling, f32[8,128]{1,0:T(8,128)S(1)} %get-tuple-element.28.open_mask, ...), custom_call_target="tpu_custom_call", output_to_operand_aliasing={{0}: (4, {})} | custom-call | tf_op jit(solution)/shard_map/pallas_call | solution.py:344
  5.2 19.5 %all_to_all.10.rows = bf16[16,2,64,128]{3,2,1,0:T(8,128)(2,1)S(1)} all-to-all(bf16[16,2,64,128]{3,2,1,0:T(8,128)(2,1)S(1)} %get-tuple-element.34), channel_id=1, replica_groups={{22,0,2,4,6,8,10,12,14,16,18,20,24,26,28,30},{23,1,3,5,7,9,11,13,15,17,..., dimensions={0} | all-to-all | bytes 1048576 | tf_op jit(solution)/shard_map/all_to_all | solution.py:31
  24.7 0.0 copy-done.1
  24.7 1.5 %shard_map.105 = (f32[16,1,8]{2,1,0:T(1,128)S(1)}, bf16[16,64,128]{2,1,0:T(8,128)(2,1)S(1)}, bf16[16,64,128]{2,1,0:T(8,128)(2,1)S(1)}, f32[32,2,64,128]{3,2,1,0:...) custom-call(s32[2]{0:T(128)S(4)} %get-tuple-element.25.shift, ...), custom_call_target="tpu_custom_call", output_to_operand_aliasing={{3}: (3, {})} | custom-call | tf_op jit(solution)/shard_map/pallas_call | solution.py:359
  26.2 9.1 %all_to_all.11.parts = f32[16,1,8]{2,1,0:T(1,128)S(1)} all-to-all(f32[16,1,8]{2,1,0:T(1,128)S(1)} %get-tuple-element.36), channel_id=1, replica_groups={{30,0,2,4,6,8,10,12,14,16,18,20,22,24,26,28},{31,1,3,5,7,9,11,13,15,17,..., dimensions={0} | all-to-all | bytes 1024 | tf_op jit(solution)/shard_map/all_to_all | solution.py:31
  35.2 0.7 %shard_map.106 = (f32[1,8]{1,0:T(1,128)}, f32[1,8]{1,0:T(1,128)}, bf16[16,64,128]{2,1,0:T(8,128)(2,1)}, bf16[16,64,128]{2,1,0:T(8,128)(2,1)}) custom-call(f32[16,1,8]{2,1,0:T(1,128)S(1)} %all_to_all.11.parts, f32[8,128]{1,0:T(8,128)S(1)} %get-tuple-element.37.diagonal, ...), custom_call_target="tpu_custom_call", output_to_operand_aliasing={{2}: (4, {}), {3}: (5, {})} | custom-call | tf_op jit(solution)/shard_map/pallas_call | solution.py:380
Async XLA Ops:
  2.0 22.7 %copy-start.1 = (f32[8,128]{1,0:T(8,128)S(1)}, f32[8,128]{1,0:T(8,128)}, u32[]{:S(2)}) copy-start(f32[8,128]{1,0:T(8,128)} %strength.1) | copy-start | bytes 12292
  2.0 2.6 %collective-permute-start = (bf16[4,128,128]{2,1,0:T(8,128)(2,1)S(1)}, bf16[4,128,128]{2,1,0:T(8,128)(2,1)S(1)}, u32[]{:S(2)}, u32[]{:S(2)}) collective-permute-start(bf16[4,128,128]{2,1,0:T(8,128)(2,1)S(1)} %get-tuple-element.33), channel_id=1, source_target_pairs={{0,1},{1,0},{2,3},{3,2},{4,5},{5,4},{6,7},{7,6},{8,9},{9,8},{10,11... | collective-permute-start | bytes 393224 | tf_op jit(solution)/shard_map/ppermute | solution.py:315
  2.5 0.9 %copy-start = (bf16[1,8,128,128]{3,2,1,0:T(8,128)(2,1)S(1)}, bf16[1,8,128,128]{3,2,1,0:T(8,128)(2,1)}, u32[]{:S(2)}) copy-start(bf16[1,8,128,128]{3,2,1,0:T(8,128)(2,1)} %refs_2_.1) | copy-start | bytes 786436
